TPU v7x, 512 devices: a whole 4x8x8 slice. The times are simulated.
512 devices in a mesh: dp: 128 (over x, z, y_hi, core), head: 4 (over y_lo).
Axes of the slice: x: 4, y: 8 (y_hi: 2, y_lo: 4; y = y_hi * 4 + y_lo), z: 8, core: 2. Of those that a mesh axis runs over, the one named last changes fastest.
Arguments:
- attn_queries: bfloat16 [65536, 1536], P('dp', 'head'), may hold values from -64 to 64
- keys: bfloat16 [65536, 256], P('dp'), may hold values from -6 to 6
- values: bfloat16 [65536, 256], P('dp'), may hold values from -6 to 6
- out_weight: bfloat16 [1536, 1536], P('head'), may hold values from -0.15625 to 0.15625
- lengths: int32 [128, 8], P('dp'), may hold values from 1 to 256, 512 in all within a row
- queries: bfloat16 [512, 1536], P('dp', 'head'), may hold values from -48 to 48
- positives: int32 [512], replicated, may hold values from 0 to 1023
Outputs:
- d_values: bfloat16 [65536, 256], P('dp', 'head')
- loss: float32 [], replicated
Inputs may be any that keep to these rules, and one draw needn't show every extreme that they name: `lengths`: each row sums to 512.
All inputs are finite; a program needn't handle non-finite values.
Results may differ from a plain program's by a relative error of at most 0.0072.
Values may be sent and summed in bfloat16 or wider, within the bound.
No kernel may reach another device: no remote copies, remote signals or barrier semaphores. Data moves between devices by JAX's collectives and lax.ppermute only.
A program may use at most 64 MiB of HBM per device.

v0:
```python
import math

import jax
import jax.numpy as jnp
from jax import lax
from jax.sharding import Mesh
from jax.sharding import PartitionSpec as P

HEADS = 12
KV_HEADS = 2
HD = 128
DP = ("dp_0", "dp_1", "dp_2", "dp_3")


sim_scale = 20.0
loss_scale = 32768.0


def cut_along(value, dim, count):
    shape = value.shape
    parts = value.reshape(*shape[:dim], count, shape[dim] // count, *shape[dim + 1 :])
    return jnp.moveaxis(parts, dim, 0)


def sent_and_summed(value, axis, dim):
    count = lax.axis_size(axis)
    parts = lax.all_to_all(cut_along(value, dim, count), axis, 0, 0, tiled=True)
    return jnp.sum(parts, axis=0)


def copy_for_each(value, axis):
    copies = jnp.broadcast_to(value, (lax.axis_size(axis), *value.shape))
    return lax.all_to_all(copies, axis, split_axis=0, concat_axis=0, tiled=True)


def over_copies(value, axis):
    return copy_for_each(value, axis).sum(axis=0)


def joined_along(parts, dim):
    parts = jnp.moveaxis(parts, 0, dim)
    shape = parts.shape
    return parts.reshape(*shape[:dim], shape[dim] * shape[dim + 1], *shape[dim + 2 :])


def all_blocks(value, axes, turns):
    parts = value
    for k in turns:
        parts = lax.all_gather(parts, axes[k])
    done = turns[::-1]
    back = [done.index(k) for k in range(len(axes))]
    parts = parts.transpose(*back, *range(len(axes), parts.ndim))
    return parts.reshape(-1, *value.shape)


def whole_of(value, axes, turns, dim):
    return joined_along(all_blocks(value, axes, turns), dim)


def gathered_once(value, axis):
    leaves = jax.tree.leaves(value)
    turns = sorted(range(len(leaves)), key=lambda k: -leaves[k].size)
    width = (1, *leaves[turns[0]].shape)[-1]
    lines = [
        jnp.pad(leaves[k].reshape(-1), (0, -leaves[k].size % width)).reshape(-1, width)
        for k in turns
    ]
    both, at, found = (lax.all_gather(jnp.concatenate(lines), axis), 0, {})
    for k, line in zip(turns, lines):
        slab = both[:, at : at + len(line)].reshape(len(both), -1)
        found[k] = slab[:, : leaves[k].size].reshape(-1, *leaves[k].shape)
        at += len(line)
    numbers = iter(range(len(leaves)))
    return jax.tree.map(lambda _: found[next(numbers)], value)


def merged_by_axis(value, axes, combine):
    for axis in axes:
        pieces = gathered_once(value, axis)
        value = jax.tree.map(lambda part: part[0], pieces)
        for k in range(1, lax.axis_size(axis)):
            value = combine(value, jax.tree.map(lambda part: part[k], pieces))
    return value


def gathered_copies(value, axis, dim):
    return joined_along(copy_for_each(value, axis), dim)


def swapped(block, axis, apart):
    count = lax.axis_size(axis)
    route = []
    for low in range(count):
        high = low | 1 << apart
        if high != low and high < count:
            route += [(low, high), (high, low)]
    return lax.ppermute(block, axis, route)


def segment_ids(lens, count):
    ends = jnp.cumsum(lens)
    places = jnp.arange(count, dtype=jnp.int32)
    return jnp.sum((places[:, None] >= ends[None, :]).astype(jnp.int32), axis=1)


def combine_stats(earlier, later):
    top = jnp.maximum(earlier[0], later[0])
    total = earlier[1] * jnp.exp(earlier[0] - top) + later[1] * jnp.exp(later[0] - top)
    return (top, total, earlier[2] + later[2])


def per_device(attn_queries, keys, values, out_weight, lengths, queries, positives):
    seq_len = attn_queries.shape[0]
    width = attn_queries.shape[1]
    heads = width // HD
    group = HEADS // KV_HEADS
    head_index = lax.axis_index("head")
    kv_head = head_index * heads // group
    docs = lengths.shape[1]
    lens = lengths[0]
    seg = segment_ids(lens, seq_len)
    places = jnp.arange(seq_len, dtype=jnp.int32)
    queries_h = attn_queries.reshape(seq_len, heads, HD)
    keys_g = lax.dynamic_slice_in_dim(keys, kv_head * HD, HD, 1)
    values_g = lax.dynamic_slice_in_dim(values, kv_head * HD, HD, 1)
    block = min(512, seq_len)
    scores = jnp.einsum(
        "qhd,kd->hqk", queries_h, keys_g, preferred_element_type=jnp.float32
    ) / math.sqrt(HD)
    allowed = (seg[:, None] == seg[None, :]) & (places[None, :] <= places[:, None])
    scores = jnp.where(allowed[None], scores, -1e30)
    top = jnp.max(scores, axis=-1, keepdims=True)
    expo = jnp.exp(scores - top)
    probs = (expo / jnp.sum(expo, axis=-1, keepdims=True)).astype(jnp.bfloat16)
    prob_blocks = [probs]
    context = jnp.einsum("hqk,kd->qhd", probs, values_g, preferred_element_type=jnp.float32)
    context_blocks = context.astype(jnp.bfloat16).reshape(block, width)
    context = context_blocks
    member = jnp.arange(docs, dtype=jnp.int32)[:, None] == seg[None, :]
    sums = jnp.dot(member.astype(jnp.bfloat16), context, preferred_element_type=jnp.float32)
    pooled = sums / lens[:, None].astype(jnp.float32)
    weight = out_weight.astype(jnp.float32)
    partial_emb = jnp.dot(pooled, weight, precision=lax.Precision.HIGHEST)
    emb = sent_and_summed(partial_emb, "head", 1)
    squares = over_copies(jnp.sum(emb * emb, axis=1), "head")
    rnorm = 1.0 / jnp.sqrt(squares + 1e-06)
    unit = emb * rnorm[:, None]
    unit_b = unit.astype(jnp.bfloat16)
    dp_index = lax.axis_index(DP)
    every_query = whole_of(queries, DP, (2, 0, 1, 3), 0)
    partial_logits = jnp.dot(every_query, unit_b.T, preferred_element_type=jnp.float32)
    logits = sim_scale * over_copies(partial_logits, "head")
    owned = dp_index * docs + jnp.arange(docs, dtype=jnp.int32)
    chosen = (positives[:, None] == owned[None, :]).astype(jnp.float32)
    local_top = jnp.max(logits, axis=1)
    local_total = jnp.sum(jnp.exp(logits - local_top[:, None]), axis=1)
    local_pos = jnp.sum(logits * chosen, axis=1)
    top, total, pos_logit = merged_by_axis((local_top, local_total, local_pos), DP, combine_stats)
    lse = top + jnp.log(total)
    loss = jnp.mean(lse - pos_logit)
    dlogits = jnp.exp(logits - lse[:, None]) - chosen
    g_unit = sim_scale * jnp.dot(
        dlogits.T, every_query.astype(jnp.float32), precision=lax.Precision.HIGHEST
    )
    inner = over_copies(jnp.sum(unit * g_unit, axis=1), "head")
    g_emb = rnorm[:, None] * (g_unit - unit * inner[:, None])
    g_full = gathered_copies(g_emb, "head", 1)
    g_pooled = jnp.dot(g_full, weight.T, precision=lax.Precision.HIGHEST)
    scaled = g_pooled / lens[:, None].astype(jnp.float32) * loss_scale
    d_context = jnp.dot(
        member.astype(jnp.float32).T, scaled, precision=lax.Precision.HIGHEST
    ).astype(jnp.bfloat16)
    d_context_h = d_context.reshape(seq_len, heads, HD)
    grads = jnp.zeros((seq_len, HD), jnp.float32)
    for number, first in enumerate(range(0, seq_len, block)):
        grads = jnp.einsum(
            "hqk,qhd->kd", prob_blocks[number], d_context_h, preferred_element_type=jnp.float32
        )
    half = HD // 2
    my_half = head_index % 2
    outgoing = lax.dynamic_slice_in_dim(grads, (1 - my_half) * half, half, 1)
    incoming = swapped(outgoing, "head", 0)
    kept = lax.dynamic_slice_in_dim(grads, my_half * half, half, 1) + incoming
    d_values = kept.astype(jnp.bfloat16)
    return (d_values, loss)


def solution(mesh):
    torus = Mesh(
        mesh.devices.reshape(4, 8, 2, 2, mesh.shape["head"]),
        ("dp_0", "dp_1", "dp_2", "dp_3", "head"),
    )
    placed = (
        P(DP, "head"),
        P(DP, None),
        P(DP, None),
        P("head", None),
        P(DP, None),
        P(DP, "head"),
        P(),
    )
    return jax.shard_map(
        per_device, mesh=torus, in_specs=placed, out_specs=(P(DP, "head"), P()), check_vma=False
    )
```

profile of v0, /device:TPU:1, one launch (start us, length us, event | category | flops | bytes accessed | tf_op | source)
XLA Modules:
  0.0 166.8 jit_solution(8984367097177179035)
XLA Ops:
  1.4 0.8 reduce-window.8
  2.6 1.2 copy.56
  3.7 3.8 %fusion.96 = (f32[3,512]{1,0:T(4,128)S(1)}, f32[3,512,512]{1,2,0:T(8,128)}) fusion(pred[512,512]{0,1:T(8,128)(4,1)S(1)} %fusion.6, bf16[512,3,128]{0,2,1:T(8,128)(2,1)S(1)} %bitcast.350, bf16[512,256]{1,0:T(8,128)(2,1)} %param.8, s32[]{:T(128)S(6)} %select_n.26), kind=kOutput, calls=%fused_computation.158 | convolution fusion | flops 204472832 | bytes 3938308 | tf_op jit(solution)/shard_map/sub | solution.py:133
  7.5 2.4 %divide_convert_fusion = bf16[3,512,512]{1,2,0:T(8,128)(2,1)S(1)} fusion(f32[3,512,512]{1,2,0:T(8,128)} %get-tuple-element.18, f32[3,512]{1,0:T(4,128)S(1)} %get-tuple-element.17), kind=kLoop, calls=%fused_computation.2 | loop fusion | flops 1572864 | bytes 4724736 | tf_op jit(solution)/shard_map/convert_element_type | solution.py:134
  10.5 1.2 fusion.101
  11.8 5.4 %all-to-all-start = ((f32[4,8,384]{2,1,0:T(8,128)}), f32[4,8,384]{2,1,0:T(8,128)}, u32[]{:S(2)}, u32[]{:S(2)}) async-start(f32[4,8,384]{2,1,0:T(8,128)} %bitcast.10), calls=%async_computation | async-start | bytes 98304 | tf_op jit(solution)/shard_map/all_to_all | solution.py:27
  17.2 7.1 %all-gather.8 = bf16[2,4,384]{2,1,0:T(4,128)(2,1)S(1)} all-gather(bf16[1,4,384]{2,1,0:T(4,128)(2,1)S(1)} %bitcast.363), channel_id=2, replica_groups=mesh['dp_0'=4,'dp_1'=8,'dp_2'=2,'dp_3'=2,'head'=4] {'dp_2'}, dimensions={0}, use_global_device_ids=true | all-gather | bytes 9216 | tf_op jit(solution)/shard_map/all_gather | solution.py:49
  24.3 9.4 %all-gather.1 = bf16[8,4,384]{2,1,0:T(4,128)(2,1)S(1)} all-gather(bf16[2,4,384]{2,1,0:T(4,128)(2,1)S(1)} %all-gather.8), channel_id=3, replica_groups=mesh['dp_0'=4,'dp_1'=8,'dp_2'=2,'dp_3'=2,'head'=4] {'dp_0'}, dimensions={0}, use_global_device_ids=true | all-gather | bytes 30720 | tf_op jit(solution)/shard_map/all_gather | solution.py:49
  33.7 24.7 %all-gather.2 = bf16[32,2,4,384]{3,2,1,0:T(4,128)(2,1)S(1)} all-gather(bf16[4,2,4,384]{3,2,1,0:T(4,128)(2,1)S(1)} %bitcast.352), channel_id=4, replica_groups=mesh['dp_0'=4,'dp_1'=8,'dp_2'=2,'dp_3'=2,'head'=4] {'dp_1'}, dimensions={0}, use_global_device_ids=true | all-gather | bytes 221184 | tf_op jit(solution)/shard_map/all_gather | solution.py:49
  58.3 13.0 %all-gather.3 = bf16[16,4,2,4,384]{4,3,2,1,0:T(4,128)(2,1)S(1)} all-gather(bf16[8,4,2,4,384]{4,3,2,1,0:T(4,128)(2,1)S(1)} %bitcast.349), channel_id=5, replica_groups=mesh['dp_0'=4,'dp_1'=8,'dp_2'=2,'dp_3'=2,'head'=4] {'dp_3'}, dimensions={0}, use_global_device_ids=true | all-gather | bytes 589824 | tf_op jit(solution)/shard_map/all_gather | solution.py:49
  73.3 4.8 %all-to-all-start.1 = ((f32[4,1,8]{2,1,0:T(1,128)}), f32[4,1,8]{2,1,0:T(1,128)S(1)}, u32[]{:S(2)}, u32[]{:S(2)}) async-start(f32[4,1,8]{2,1,0:T(1,128)} %broadcast_in_dim.22), calls=%async_computation.1 | async-start | bytes 4096 | tf_op jit(solution)/shard_map/all_to_all | solution.py:33
  78.1 4.3 %all-to-all-done.1 = f32[4,1,8]{2,1,0:T(1,128)S(1)} async-done(((f32[4,1,8]{2,1,0:T(1,128)}), f32[4,1,8]{2,1,0:T(1,128)S(1)}, u32[]{:S(2)}, u32[]{:S(2)}) %all-to-all-start.1) | async-done | bytes 160 | tf_op jit(solution)/shard_map/all_to_all | solution.py:33
  83.3 3.3 %all-to-all-start.2 = ((f32[4,512,8]{1,2,0:T(8,128)}), f32[4,512,8]{1,2,0:T(8,128)S(1)}, u32[]{:S(2)}, u32[]{:S(2)}) async-start(f32[4,512,8]{1,2,0:T(8,128)} %broadcast_in_dim.23), calls=%async_computation.2 | async-start | bytes 131072 | tf_op jit(solution)/shard_map/all_to_all | solution.py:33
  86.7 4.5 %all-to-all-done.2 = f32[4,512,8]{1,2,0:T(8,128)S(1)} async-done(((f32[4,512,8]{1,2,0:T(8,128)}), f32[4,512,8]{1,2,0:T(8,128)S(1)}, u32[]{:S(2)}, u32[]{:S(2)}) %all-to-all-start.2) | async-done | bytes 65568 | tf_op jit(solution)/shard_map/all_to_all | solution.py:33
  91.3 9.0 %all-gather.9 = f32[4,3,512]{2,1,0:T(4,128)S(1)} all-gather(f32[1,3,512]{2,1,0:T(4,128)S(1)} %maximum_bitcast_fusion), channel_id=6, replica_groups=mesh['dp_0'=4,'dp_1'=8,'dp_2'=2,'dp_3'=2,'head'=4] {'dp_0'}, dimensions={0}, use_global_device_ids=true | all-gather | bytes 30720 | tf_op jit(solution)/shard_map/all_gather | solution.py:68
  100.4 18.2 %all-gather.10 = f32[8,3,512]{2,1,0:T(4,128)S(1)} all-gather(f32[1,3,512]{2,1,0:T(4,128)S(1)} %maximum_bitcast_fusion.1), channel_id=7, replica_groups=mesh['dp_0'=4,'dp_1'=8,'dp_2'=2,'dp_3'=2,'head'=4] {'dp_1'}, dimensions={0}, use_global_device_ids=true | all-gather | bytes 55296 | tf_op jit(solution)/shard_map/all_gather | solution.py:68
  118.7 7.1 %all-gather.11 = f32[2,3,512]{2,1,0:T(4,128)S(1)} all-gather(f32[1,3,512]{2,1,0:T(4,128)S(1)} %maximum_bitcast_fusion.2), channel_id=8, replica_groups=mesh['dp_0'=4,'dp_1'=8,'dp_2'=2,'dp_3'=2,'head'=4] {'dp_2'}, dimensions={0}, use_global_device_ids=true | all-gather | bytes 18432 | tf_op jit(solution)/shard_map/all_gather | solution.py:68
  125.9 14.8 %all-gather.12 = f32[2,3,512]{2,1,0:T(4,128)S(1)} all-gather(f32[1,3,512]{2,1,0:T(4,128)S(1)} %maximum_bitcast_fusion.3), channel_id=9, replica_groups=mesh['dp_0'=4,'dp_1'=8,'dp_2'=2,'dp_3'=2,'head'=4] {'dp_3'}, dimensions={0}, use_global_device_ids=true | all-gather | bytes 18432 | tf_op jit(solution)/shard_map/all_gather | solution.py:68
  141.8 6.7 %all_to_all.27 = f32[4,1,8]{2,1,0:T(1,128)S(1)} all-to-all(f32[4,1,8]{2,1,0:T(1,128)S(1)} %broadcast_in_dim.24), channel_id=1, replica_groups=mesh['dp_0'=4,'dp_1'=8,'dp_2'=2,'dp_3'=2,'head'=4] {'head'}, dimensions={0} | all-to-all | bytes 256 | tf_op jit(solution)/shard_map/all_to_all | solution.py:33
  149.3 3.3 %all-to-all-start.4 = ((f32[4,8,384]{2,1,0:T(8,128)}), f32[4,8,384]{2,1,0:T(8,128)S(1)}, u32[]{:S(2)}, u32[]{:S(2)}) async-start(f32[4,8,384]{2,1,0:T(8,128)} %broadcast_in_dim.25), calls=%async_computation.4 | async-start | bytes 98304 | tf_op jit(solution)/shard_map/all_to_all | solution.py:33
  152.6 4.5 %all-to-all-done.4 = f32[4,8,384]{2,1,0:T(8,128)S(1)} async-done(((f32[4,8,384]{2,1,0:T(8,128)}), f32[4,8,384]{2,1,0:T(8,128)S(1)}, u32[]{:S(2)}, u32[]{:S(2)}) %all-to-all-start.4) | async-done | bytes 49184 | tf_op jit(solution)/shard_map/all_to_all | solution.py:33
  157.1 1.0 fusion.5
  159.3 2.5 %collective-permute-start = (f32[512,64]{0,1:T(8,128)S(1)}, f32[512,64]{0,1:T(8,128)S(1)}, u32[]{:S(2)}, u32[]{:S(2)}) collective-permute-start(f32[512,64]{0,1:T(8,128)S(1)} %constant_dynamic-slice_fusion), channel_id=1, source_target_pairs={{0,1},{1,0},{2,3},{3,2},{4,5},{5,4},{6,7},{7,6},{8,9},{9,8},{10,11... | collective-permute-start | bytes 393224 | tf_op jit(solution)/shard_map/ppermute | solution.py:97
  162.4 2.6 %collective-permute-done = f32[512,64]{0,1:T(8,128)S(1)} collective-permute-done((f32[512,64]{0,1:T(8,128)S(1)}, f32[512,64]{0,1:T(8,128)S(1)}, u32[]{:S(2)}, u32[]{:S(2)}) %collective-permute-start) | collective-permute-done | bytes 131104 | tf_op jit(solution)/shard_map/ppermute | solution.py:97
  (49 shorter events, 8.4 us)
Async XLA Ops:
  0.6 9.9 %copy-start = (bf16[384,1536]{1,0:T(8,128)(2,1)S(1)}, bf16[384,1536]{1,0:T(8,128)(2,1)}, u32[]{:S(2)}) copy-start(bf16[384,1536]{1,0:T(8,128)(2,1)} %param.10) | copy-start | bytes 3538948
  7.5 2.4 %copy-start.1 = (bf16[512,256]{1,0:T(8,128)(2,1)S(1)}, bf16[512,256]{1,0:T(8,128)(2,1)}, u32[]{:S(2)}) copy-start(bf16[512,256]{1,0:T(8,128)(2,1)} %param.9) | copy-start | bytes 786436
  9.9 7.3 %copy-start.2 = (bf16[4,384]{1,0:T(4,128)(2,1)S(1)}, bf16[4,384]{1,0:T(4,128)(2,1)}, u32[]{:S(2)}) copy-start(bf16[4,384]{1,0:T(4,128)(2,1)} %param.12) | copy-start | bytes 9220
  11.8 60.0 %all-to-all-start = ((f32[4,8,384]{2,1,0:T(8,128)}), f32[4,8,384]{2,1,0:T(8,128)}, u32[]{:S(2)}, u32[]{:S(2)}) async-start(f32[4,8,384]{2,1,0:T(8,128)} %bitcast.10), calls=%async_computation | async-start | bytes 98304 | tf_op jit(solution)/shard_map/all_to_all | solution.py:27
  71.4 19.9 %copy-start.3 = (s32[512]{0:T(512)S(1)}, s32[512]{0:T(512)}, u32[]{:S(2)}) copy-start(s32[512]{0:T(512)} %param.13) | copy-start | bytes 6148
  73.3 9.2 %all-to-all-start.1 = ((f32[4,1,8]{2,1,0:T(1,128)}), f32[4,1,8]{2,1,0:T(1,128)S(1)}, u32[]{:S(2)}, u32[]{:S(2)}) async-start(f32[4,1,8]{2,1,0:T(1,128)} %broadcast_in_dim.22), calls=%async_computation.1 | async-start | bytes 4096 | tf_op jit(solution)/shard_map/all_to_all | solution.py:33
  83.3 7.9 %all-to-all-start.2 = ((f32[4,512,8]{1,2,0:T(8,128)}), f32[4,512,8]{1,2,0:T(8,128)S(1)}, u32[]{:S(2)}, u32[]{:S(2)}) async-start(f32[4,512,8]{1,2,0:T(8,128)} %broadcast_in_dim.23), calls=%async_computation.2 | async-start | bytes 131072 | tf_op jit(solution)/shard_map/all_to_all | solution.py:33
  149.3 7.8 %all-to-all-start.4 = ((f32[4,8,384]{2,1,0:T(8,128)}), f32[4,8,384]{2,1,0:T(8,128)S(1)}, u32[]{:S(2)}, u32[]{:S(2)}) async-start(f32[4,8,384]{2,1,0:T(8,128)} %broadcast_in_dim.25), calls=%async_computation.4 | async-start | bytes 98304 | tf_op jit(solution)/shard_map/all_to_all | solution.py:33
  159.3 5.7 %collective-permute-start = (f32[512,64]{0,1:T(8,128)S(1)}, f32[512,64]{0,1:T(8,128)S(1)}, u32[]{:S(2)}, u32[]{:S(2)}) collective-permute-start(f32[512,64]{0,1:T(8,128)S(1)} %constant_dynamic-slice_fusion), channel_id=1, source_target_pairs={{0,1},{1,0},{2,3},{3,2},{4,5},{5,4},{6,7},{7,6},{8,9},{9,8},{10,11... | collective-permute-start | bytes 393224 | tf_op jit(solution)/shard_map/ppermute | solution.py:97
where the time goes:
time: 169 us; the launch traced here: 167 us
  blocking collectives  110 us (65%)
  starting transfers between devices  19.3 us (11%)
  waiting for transfers between devices  16 us (9%)
  matrix products  8.43 us (5%)
  other arithmetic  6.86 us (4%)
  local copies, waits for them, and re-layouts  3.47 us (2%)
  between operations  2.7 us (2%)
    all_gather x4, blocking collectives, all_blocks(): parts = lax.all_gather(parts, axes[k])  54.2 us
    all_gather x4, blocking collectives, gathered_once(): both, at, found = (lax.all_gather(jnp.concatenate(lines), axis), 0, {})  49.2 us
    all_to_all x3, waiting for transfers between devices, copy_for_each(): return lax.all_to_all(copies, axis, split_axis=0, concat_axis=0, tiled=True)  13.4 us
    all_to_all x3, starting transfers between devices, copy_for_each(): return lax.all_to_all(copies, axis, split_axis=0, concat_axis=0, tiled=True)  11.4 us
    all_to_all x1, blocking collectives, copy_for_each(): return lax.all_to_all(copies, axis, split_axis=0, concat_axis=0, tiled=True)  6.74 us
    all_to_all x1, starting transfers between devices, sent_and_summed(): parts = lax.all_to_all(cut_along(value, dim, count), axis, 0, 0, tiled=True)  5.43 us
    sub x1, matrix products, per_device(): expo = jnp.exp(scores - top)  3.78 us
  transfers between devices with their start and end apart: 5, of which 4 were waited for; matrix products, arithmetic and copies ran while one was open for 0% of the time, Pallas kernels for 0%

commit v1 on v0

v1 whole, which is shorter than its diff:
```python
import math

import jax
import jax.numpy as jnp
from jax import lax
from jax.experimental import pallas as pl
from jax.experimental.pallas import tpu as pltpu
from jax.sharding import Mesh
from jax.sharding import PartitionSpec as P

HEADS = 12
KV_HEADS = 2
HD = 128
DP = ("dp_0", "dp_1", "dp_2", "dp_3")
LONGEST = 256

sim_scale = 20.0
loss_scale = 32768.0

NT = (((1,), (1,)), ((), ()))
TN = (((0,), (0,)), ((), ()))
VMEM = pl.BlockSpec(memory_space=pltpu.VMEM)
SMEM = pl.BlockSpec(memory_space=pltpu.SMEM)


def three_terms(value):
    high = value.astype(jnp.bfloat16)
    rest = value - high.astype(jnp.float32)
    mid = rest.astype(jnp.bfloat16)
    low = (rest - mid.astype(jnp.float32)).astype(jnp.bfloat16)
    return jnp.concatenate([high, mid, low], axis=0)


def of_three(value):
    rows = value.shape[0] // 3
    return value[:rows] + value[rows : 2 * rows] + value[2 * rows :]


def exact_dot(value, other, dims):
    return of_three(
        lax.dot_general(three_terms(value), other, dims, preferred_element_type=jnp.float32)
    )


def document_of(lens_ref, docs, shape, dim):
    place = lax.broadcasted_iota(jnp.int32, shape, dim)
    seg = jnp.zeros(shape, jnp.int32)
    start = jnp.zeros(shape, jnp.int32)
    end = jnp.int32(0)
    for j in range(docs):
        end = end + lens_ref[0, j]
        past = place >= end
        seg = seg + past.astype(jnp.int32)
        start = jnp.where(past, end, start)
    return seg, start


def lens_column(lens_ref, docs):
    row = lax.broadcasted_iota(jnp.int32, (docs, 1), 0)
    column = jnp.zeros((docs, 1), jnp.int32)
    for j in range(docs):
        column = jnp.where(row == j, lens_ref[0, j], column)
    return column.astype(jnp.float32)


def attend_kernel(lens_ref, q_ref, k_ref, v_ref, w_ref, out_ref, total):
    seq_len, width = q_ref.shape
    heads = width // HD
    docs = lens_ref.shape[1]
    features = w_ref.shape[1]
    kv_head = lax.axis_index("head") * heads // (HEADS // KV_HEADS)
    columns = pl.ds(pl.multiple_of(kv_head * HD, HD), HD)
    seg, start = document_of(lens_ref, docs, (1, seq_len), 1)
    total[...] = jnp.zeros_like(total)
    block = min(128, seq_len)
    factor = math.log2(math.e) / math.sqrt(HD)
    lane = lax.broadcasted_iota(jnp.int32, (block, HD), 1)
    for first in range(0, seq_len, block):
        low = max(0, (first - LONGEST + 1) // block * block)
        span = first + block - low
        k_block = k_ref[low : first + block, columns]
        k_place = low + lax.broadcasted_iota(jnp.int32, (span, block), 0)
        q_place = first + lax.broadcasted_iota(jnp.int32, (span, block), 1)
        allowed = (k_place <= q_place) & (k_place >= start[:, first : first + block])
        for h in range(heads):
            q_block = q_ref[first : first + block, h * HD : (h + 1) * HD]
            scores = lax.dot_general(k_block, q_block, NT, preferred_element_type=jnp.float32)
            scores = jnp.where(allowed, scores, -1e30)
            top = jnp.max(scores, axis=0, keepdims=True)
            expo = jnp.exp2((scores - top) * factor)
            norm = 1.0 / jnp.sum(expo, axis=0, keepdims=True)
            probs = (expo * norm).astype(jnp.bfloat16)
            pick = (lane == h).astype(jnp.bfloat16)
            total[low : first + block, :] += jnp.dot(
                probs, pick, preferred_element_type=jnp.float32
            )
    by_head = total[...].T
    member = lax.broadcasted_iota(jnp.int32, (docs, seq_len), 0) == seg
    shares = jnp.concatenate(
        [jnp.where(member, by_head[h : h + 1, :], 0.0) for h in range(heads)], axis=0
    )
    sums = exact_dot(shares, v_ref[:, columns], (((1,), (0,)), ((), ())))
    pooled = jnp.concatenate(
        [sums[h * docs : (h + 1) * docs] for h in range(heads)], axis=1
    ) / lens_column(lens_ref, docs)
    emb = exact_dot(pooled, w_ref[...], (((1,), (0,)), ((), ())))
    for k in range(out_ref.shape[0]):
        out_ref[k, :, :features] = emb
        out_ref[k, :, features:] = by_head[:docs, :]


def logits_kernel(emb_ref, q_ref, pos_ref, out_ref, logits_ref, unit_ref, rnorm_ref):
    docs = emb_ref.shape[1]
    features = q_ref.shape[1]
    emb = emb_ref[0, :, :features]
    for k in range(1, emb_ref.shape[0]):
        emb = emb + emb_ref[k, :, :features]
    rnorm = 1.0 / jnp.sqrt(jnp.sum(emb * emb, axis=1, keepdims=True) + 1e-06)
    unit = emb * rnorm
    logits = sim_scale * lax.dot_general(
        unit.astype(jnp.bfloat16), q_ref[...], NT, preferred_element_type=jnp.float32
    )
    chosen = positive_mask(pos_ref, docs)
    top = jnp.max(logits, axis=0, keepdims=True)
    lse = top + jnp.log(jnp.sum(jnp.exp(logits - top), axis=0, keepdims=True))
    positive = jnp.sum(jnp.where(chosen, logits, 0.0), axis=0, keepdims=True)
    out_ref[...] = jnp.broadcast_to(
        jnp.concatenate([lse, positive], axis=0)[None], out_ref.shape
    )
    logits_ref[...] = logits
    unit_ref[...] = unit
    rnorm_ref[...] = jnp.broadcast_to(rnorm, rnorm_ref.shape)


def positive_mask(pos_ref, docs):
    count = pos_ref.shape[1]
    positive = pos_ref[pl.ds(lax.axis_index("head"), 1), :]
    owned = lax.axis_index(DP) * docs + lax.broadcasted_iota(jnp.int32, (docs, count), 0)
    return positive == owned


def slopes_kernel(stats_ref, logits_ref, q_ref, pos_ref, out_ref):
    docs = logits_ref.shape[0]
    features = q_ref.shape[1]
    each = stats_ref[:, 0, :]
    top = jnp.max(each, axis=0, keepdims=True)
    lse = top + jnp.log(jnp.sum(jnp.exp(each - top), axis=0, keepdims=True))
    positive = jnp.sum(stats_ref[:, 1, :], axis=0, keepdims=True)
    chosen = positive_mask(pos_ref, docs)
    slopes = jnp.exp(logits_ref[...] - lse) - chosen.astype(jnp.float32)
    grads = sim_scale * exact_dot(slopes, q_ref[...], (((1,), (0,)), ((), ())))
    losses = jnp.broadcast_to(lse - positive, (docs, lse.shape[1]))
    for k in range(out_ref.shape[0]):
        out_ref[k, :, :features] = grads
        out_ref[k, :, features:] = losses


def context_kernel(lens_ref, grads_ref, unit_ref, rnorm_ref, w_ref, kept_ref, sent_ref, loss_ref):
    docs, features = unit_ref.shape
    heads = w_ref.shape[0] // HD
    half = HD // 2
    grads = grads_ref[0]
    for k in range(1, grads_ref.shape[0]):
        grads = grads + grads_ref[k]
    count = grads_ref.shape[0] * (grads.shape[1] - features)
    loss_ref[...] = jnp.sum(grads[:1, features:], axis=1, keepdims=True) / count
    grads = grads[:, :features]
    unit = unit_ref[...]
    inner = jnp.sum(unit * grads, axis=1, keepdims=True)
    g_emb = rnorm_ref[:, :1] * (grads - unit * inner)
    g_pooled = exact_dot(g_emb, w_ref[...], NT)
    scaled = (g_pooled / lens_column(lens_ref, docs) * loss_scale).astype(jnp.bfloat16)
    rows = jnp.concatenate(
        [scaled[:, h * HD : (h + 1) * HD] for h in range(heads)], axis=0
    )
    odd = lax.axis_index("head") % 2 == 1
    lower, upper = rows[:, :half], rows[:, half:]
    kept_ref[...] = jnp.where(odd, upper, lower)
    sent_ref[...] = jnp.where(odd, lower, upper)


def values_kernel(lens_ref, emb_ref, mine_ref, theirs_ref, out_ref):
    docs = emb_ref.shape[1]
    seq_len = out_ref.shape[0]
    heads = mine_ref.shape[0] // docs
    me = lax.axis_index("head")
    partner = me + 1 - 2 * (me % 2)
    seg, _ = document_of(lens_ref, docs, (1, seq_len), 1)
    member = lax.broadcasted_iota(jnp.int32, (docs, seq_len), 0) == seg
    features = emb_ref.shape[2] - seq_len
    shares = []
    for owner in (me, partner):
        by_head = emb_ref[owner, :, features:]
        shares += [jnp.where(member, by_head[h : h + 1, :], 0.0) for h in range(heads)]
    slopes = jnp.concatenate([mine_ref[...], theirs_ref[...]], axis=0)
    out = lax.dot_general(
        three_terms(jnp.concatenate(shares, axis=0)),
        jnp.concatenate([slopes] * 3, axis=0),
        TN,
        preferred_element_type=jnp.float32,
    )
    out_ref[...] = out.astype(jnp.bfloat16)


def per_device(attn_queries, keys, values, out_weight, lengths, queries, positives):
    seq_len, width = attn_queries.shape
    heads = width // HD
    docs = lengths.shape[1]
    features = out_weight.shape[1]
    split = lax.axis_size("head")
    cores = lax.axis_size(DP[3])
    others = lax.axis_size(DP[:3])
    n_dp = cores * others
    f32, bf16 = jnp.float32, jnp.bfloat16

    rows = jnp.broadcast_to(queries[None], (cores, *queries.shape)).reshape(cores * split, 1, -1)
    rows = lax.all_to_all(rows, (DP[3], "head"), 0, 0, tiled=True).reshape(cores, features)
    rows = jnp.broadcast_to(rows[None], (others, cores, features))
    every = lax.all_to_all(rows, DP[:3], 0, 0, tiled=True).reshape(n_dp, features)
    pos = positives.reshape(n_dp, split).T

    partial = pl.pallas_call(
        attend_kernel,
        out_shape=jax.ShapeDtypeStruct((split, docs, features + seq_len), f32),
        in_specs=[SMEM] + [VMEM] * 4,
        out_specs=VMEM,
        scratch_shapes=[pltpu.VMEM((seq_len, HD), f32)],
        compiler_params=pltpu.CompilerParams(vmem_limit_bytes=32 * 2**20),
        name="attend",
    )(lengths, attn_queries, keys, values, out_weight)
    partial = lax.all_to_all(partial, "head", 0, 0, tiled=True)

    stats, logits, unit, rnorm = pl.pallas_call(
        logits_kernel,
        out_shape=(
            jax.ShapeDtypeStruct((n_dp, 2, n_dp), f32),
            jax.ShapeDtypeStruct((docs, n_dp), f32),
            jax.ShapeDtypeStruct((docs, features), f32),
            jax.ShapeDtypeStruct((docs, HD), f32),
        ),
        in_specs=[VMEM] * 3,
        out_specs=(VMEM,) * 4,
        name="logits",
    )(partial, every, pos)
    stats = lax.all_to_all(stats, DP, 0, 0, tiled=True)

    grads = pl.pallas_call(
        slopes_kernel,
        out_shape=jax.ShapeDtypeStruct((split, docs, features + n_dp), f32),
        in_specs=[VMEM] * 4,
        out_specs=VMEM,
        name="slopes",
    )(stats, logits, every, pos)
    grads = lax.all_to_all(grads, "head", 0, 0, tiled=True)

    kept, sent, loss = pl.pallas_call(
        context_kernel,
        out_shape=(
            jax.ShapeDtypeStruct((heads * docs, HD // 2), bf16),
            jax.ShapeDtypeStruct((heads * docs, HD // 2), bf16),
            jax.ShapeDtypeStruct((1, 1), f32),
        ),
        in_specs=[SMEM] + [VMEM] * 4,
        out_specs=(VMEM,) * 3,
        name="context",
    )(lengths, grads, unit, rnorm, out_weight)
    got = lax.ppermute(sent, "head", [(i, i ^ 1) for i in range(split)])

    d_values = pl.pallas_call(
        values_kernel,
        out_shape=jax.ShapeDtypeStruct((seq_len, HD // 2), bf16),
        in_specs=[SMEM] + [VMEM] * 3,
        out_specs=VMEM,
        name="slopes_of_values",
    )(lengths, partial, kept, got)
    return d_values, loss.reshape(())


def solution(mesh):
    shape = (4, 8, 2, 2) if mesh.devices.size == 512 else (1, mesh.devices.size // 16, 2, 2)
    torus = Mesh(mesh.devices.reshape(*shape, mesh.shape["head"]), (*DP, "head"))
    placed = (
        P(DP, "head"),
        P(DP, None),
        P(DP, None),
        P("head", None),
        P(DP, None),
        P(DP, "head"),
        P(),
    )
    return jax.shard_map(
        per_device, mesh=torus, in_specs=placed, out_specs=(P(DP, "head"), P()), check_vma=False
    )
```

time: 169 us -> 114 us (0.67)
  blocking collectives: 110 us -> 49.4 us
  Pallas kernels: 0 us -> 11.6 us
  matrix products: 8.43 us -> 0 us
  local copies, waits for them, and re-layouts: 3.47 us -> 9.87 us
  other arithmetic: 6.86 us -> 0.73 us
  starting transfers between devices: 19.3 us -> 23.1 us
  between operations: 2.7 us -> 0.71 us
    all_gather x8 -> x0, blocking collectives: 103 us -> none  [the longest x4 54.2 us: all_blocks(): parts = lax.all_gather(parts, axes[k])]
    all_to_all x1 -> x3, blocking collectives: 6.74 us -> 49.4 us  [the longest x1 24.6 us: per_device(): stats = lax.all_to_all(stats, DP, 0, 0, tiled=True)]
    pallas_call x0 -> x5, Pallas kernels: none -> 11.6 us  [the longest x1 2.85 us: per_device(): pl.pallas_call(attend_kernel, out_shape=jax.ShapeDtypeStruct((split, docs...]
    unnamed x9 -> x19, local copies, waits for them, and re-layouts: 1.19 us -> 5.98 us
    dot_general x8 -> x0, matrix products: 4.65 us -> none  [the longest x1 1.22 us: per_device(): partial_emb = jnp.dot(pooled, weight, precision=lax.Precision.HIGHEST)]
    sub x1 -> x0, matrix products: 3.78 us -> none  [per_device(): expo = jnp.exp(scores - top)]
    convert_element_type x3 -> x0, other arithmetic: 3.76 us -> none  [the longest x1 2.36 us: per_device(): probs = (expo / jnp.sum(expo, axis=-1, keepdims=True)).astype(jnp.bfloat16)]
    all_to_all x4 -> x2, starting transfers between devices: 16.8 us -> 19.8 us  [the longest x1 13.4 us: per_device(): lax.all_to_all(rows, DP[:3], 0, 0, tiled=True).reshape(n_dp, features)]
  transfers between devices with their start and end apart: 5 -> 3, of which waited for: 4 -> 3; matrix products, arithmetic and copies ran while one was open for 0% -> 1% of each run, Pallas kernels for 0% -> 3%
where the time goes in v1:
time: 114 us; the launch traced here: 112 us
  blocking collectives  49.4 us (43%)
  starting transfers between devices  23.1 us (20%)
  waiting for transfers between devices  16.5 us (14%)
  Pallas kernels  11.6 us (10%)
  local copies, waits for them, and re-layouts  9.87 us (9%)
    all_to_all x1, blocking collectives, per_device(): stats = lax.all_to_all(stats, DP, 0, 0, tiled=True)  24.6 us
    all_to_all x1, blocking collectives, per_device(): lax.all_to_all(rows, (DP[3], 'head'), 0, 0, tiled=True)  14.4 us
    all_to_all x1, starting transfers between devices, per_device(): lax.all_to_all(rows, DP[:3], 0, 0, tiled=True).reshape(n_dp, features)  13.4 us
    all_to_all x1, blocking collectives, per_device(): grads = lax.all_to_all(grads, 'head', 0, 0, tiled=True)  10.3 us
    all_to_all x1, waiting for transfers between devices, per_device(): lax.all_to_all(rows, DP[:3], 0, 0, tiled=True).reshape(n_dp, features)  9.26 us
    all_to_all x1, starting transfers between devices, per_device(): partial = lax.all_to_all(partial, 'head', 0, 0, tiled=True)  6.44 us
    unnamed x19, local copies, waits for them, and re-layouts  5.98 us
    all_to_all x1, waiting for transfers between devices, per_device(): partial = lax.all_to_all(partial, 'head', 0, 0, tiled=True)  5.93 us
  transfers between devices with their start and end apart: 3, of which 3 were waited for; matrix products, arithmetic and copies ran while one was open for 1% of the time, Pallas kernels for 3%

profile of v1, /device:TPU:1, one launch (start us, length us, event | category | flops | bytes accessed | tf_op | source)
XLA Modules:
  0.0 111.9 jit_solution(10296012304282155474)
XLA Ops:
  0.7 0.8 broadcast_in_dim.6
  2.0 0.7 reduce.1
  2.7 14.4 %all_to_all.25 = bf16[8,2,192]{2,1,0:T(2,128)(2,1)S(1)} all-to-all(bf16[8,2,192]{2,1,0:T(2,128)(2,1)S(1)} %reshape.24), channel_id=1, replica_groups=mesh['dp_0'=4,'dp_1'=8,'dp_2'=2,'dp_3'=2,'head'=4] {'dp_3','head'}, dimensions={0} | all-to-all | bytes 12288 | tf_op jit(solution)/shard_map/all_to_all | solution.py:217
  17.3 0.9 broadcast_in_dim.15
  18.3 13.4 %all-to-all-start.2 = ((bf16[64,2,1536]{2,1,0:T(2,128)(2,1)}), bf16[64,2,1536]{2,1,0:T(2,128)(2,1)S(1)}, u32[]{:S(2)}, u32[]{:S(2)}) async-start(bf16[64,2,1536]{2,1,0:T(2,128)(2,1)} %broadcast_in_dim.15), calls=%async_computation.2 | async-start | bytes 786432 | tf_op jit(solution)/shard_map/all_to_all | solution.py:219
  31.7 1.0 copy-done.1
  32.7 0.9 copy-done.2
  33.6 0.9 copy-done.3
  34.6 2.9 %attend.1 = f32[4,8,2048]{2,1,0:T(8,128)} custom-call(s32[1,8]{1,0:T(1,128)S(1)} %copy-done.4, bf16[512,384]{1,0:T(8,128)(2,1)S(1)} %copy-done.1, bf16[512,256]{1,0:T(8,128)(2,1)S(1)} %copy-done.2, bf16[512,256]{1,0:T(8,128)(2,1)S(1)} %copy-done.3, bf16[384,1536]{1,0:T(8,128)(2,1)S(1)} %copy-done), custom_call_target="tpu_custom_call" | custom-call | tf_op jit(solution)/shard_map/attend/pallas_call | solution.py:222
  37.4 9.3 %all-to-all-done.2 = bf16[64,2,1536]{2,1,0:T(2,128)(2,1)S(1)} async-done(((bf16[64,2,1536]{2,1,0:T(2,128)(2,1)}), bf16[64,2,1536]{2,1,0:T(2,128)(2,1)S(1)}, u32[]{:S(2)}, u32[]{:S(2)}) %all-to-all-start.2) | async-done | bytes 393248 | tf_op jit(solution)/shard_map/all_to_all | solution.py:219
  46.7 6.4 %all-to-all-start = ((f32[4,8,2048]{2,1,0:T(8,128)}), f32[4,8,2048]{2,1,0:T(8,128)S(1)}, u32[]{:S(2)}, u32[]{:S(2)}) async-start(f32[4,8,2048]{2,1,0:T(8,128)} %attend.1), calls=%async_computation | async-start | bytes 524288 | tf_op jit(solution)/shard_map/all_to_all | solution.py:231
  53.3 0.6 copy.15
  53.9 0.9 reshape.19.q_ref
  54.8 5.9 %all-to-all-done.emb_ref = f32[4,8,2048]{2,1,0:T(8,128)S(1)} async-done(((f32[4,8,2048]{2,1,0:T(8,128)}), f32[4,8,2048]{2,1,0:T(8,128)S(1)}, u32[]{:S(2)}, u32[]{:S(2)}) %all-to-all-start) | async-done | bytes 262176 | tf_op jit(solution)/shard_map/all_to_all | solution.py:231
  60.7 0.7 copy-done.5
  61.4 2.1 %logits.1 = (f32[128,2,128]{2,1,0:T(2,128)}, f32[8,128]{1,0:T(8,128)}, f32[8,1536]{1,0:T(8,128)}, f32[8,128]{1,0:T(8,128)}) custom-call(f32[4,8,2048]{2,1,0:T(8,128)} %copy-done.5, bf16[128,1536]{1,0:T(8,128)(2,1)} %reshape.19.q_ref, s32[4,128]{1,0:T(4,128)} %bitcast.2), custom_call_target="tpu_custom_call" | custom-call | tf_op jit(solution)/shard_map/logits/pallas_call | solution.py:233
  63.5 24.6 %all_to_all.26.stats_ref = f32[128,2,128]{2,1,0:T(2,128)} all-to-all(f32[128,2,128]{2,1,0:T(2,128)} %get-tuple-element.9), channel_id=1, replica_groups=mesh['dp_0'=4,'dp_1'=8,'dp_2'=2,'dp_3'=2,'head'=4] {'dp_0','dp_1','dp_2'..., dimensions={0} | all-to-all | bytes 262144 | tf_op jit(solution)/shard_map/all_to_all | solution.py:245
  88.1 2.1 %slopes.1 = f32[4,8,1664]{2,1,0:T(8,128)} custom-call(f32[128,2,128]{2,1,0:T(2,128)} %all_to_all.26.stats_ref, f32[8,128]{1,0:T(8,128)} %get-tuple-element.10.logits_ref, bf16[128,1536]{1,0:T(8,128)(2,1)} %reshape.19.q_ref, s32[4,128]{1,0:T(4,128)} %bitcast.3), custom_call_target="tpu_custom_call" | custom-call | tf_op jit(solution)/shard_map/slopes/pallas_call | solution.py:247
  90.2 10.3 %all_to_all.27.grads_ref = f32[4,8,1664]{2,1,0:T(8,128)} all-to-all(f32[4,8,1664]{2,1,0:T(8,128)} %slopes.1), channel_id=1, replica_groups=mesh['dp_0'=4,'dp_1'=8,'dp_2'=2,'dp_3'=2,'head'=4] {'head'}, dimensions={0} | all-to-all | bytes 425984 | tf_op jit(solution)/shard_map/all_to_all | solution.py:254
  100.5 2.7 %context.1 = (bf16[24,64]{1,0:T(8,128)(2,1)}, bf16[24,64]{1,0:T(8,128)(2,1)}, f32[1,1]{1,0:T(1,128)}) custom-call(s32[1,8]{1,0:T(1,128)} %lens_ref.5, f32[4,8,1664]{2,1,0:T(8,128)} %all_to_all.27.grads_ref, f32[8,1536]{1,0:T(8,128)} %get-tuple-element.11.unit_ref, f32[8,128]{1,0:T(8,128)} %get-tuple-element.12.rnorm_ref, bf16[384,1536]{1,0:T(8,128)(2,1)} %w_ref.3), custom_call_target="tpu_custom_call" | custom-call | tf_op jit(solution)/shard_map/context/pallas_call | solution.py:256
  103.2 3.2 %collective-permute-start = (bf16[24,64]{1,0:T(8,128)(2,1)}, bf16[24,64]{1,0:T(8,128)(2,1)S(1)}, u32[]{:S(2)}, u32[]{:S(2)}) collective-permute-start(bf16[24,64]{1,0:T(8,128)(2,1)} %get-tuple-element.14), channel_id=1, source_target_pairs={{0,1},{1,0},{2,3},{3,2},{4,5},{5,4},{6,7},{7,6},{8,9},{9,8},{10,11... | collective-permute-start | bytes 9224 | tf_op jit(solution)/shard_map/ppermute | solution.py:267
  106.4 1.3 %collective-permute-done.theirs_ref = bf16[24,64]{1,0:T(8,128)(2,1)S(1)} collective-permute-done((bf16[24,64]{1,0:T(8,128)(2,1)}, bf16[24,64]{1,0:T(8,128)(2,1)S(1)}, u32[]{:S(2)}, u32[]{:S(2)}) %collective-permute-start) | collective-permute-done | bytes 3104 | tf_op jit(solution)/shard_map/ppermute | solution.py:267
  108.3 1.9 %slopes_of_values.1 = bf16[512,64]{1,0:T(8,128)(2,1)} custom-call(s32[1,8]{1,0:T(1,128)} %lens_ref.5, f32[4,8,2048]{2,1,0:T(8,128)} %copy-done.5, bf16[24,64]{1,0:T(8,128)(2,1)} %get-tuple-element.13.mine_ref, bf16[24,64]{1,0:T(8,128)(2,1)} %copy-done.6), custom_call_target="tpu_custom_call" | custom-call | tf_op jit(solution)/shard_map/slopes_of_values/pallas_call | solution.py:269
  110.3 1.6 %copy.16 = bf16[512,64]{0,1:T(8,128)(2,1)} copy(bf16[512,64]{1,0:T(8,128)(2,1)} %slopes_of_values.1) | data formatting | bytes 131072
  (19 shorter events, 1.5 us)
Async XLA Ops:
  0.6 31.0 %copy-start = (bf16[384,1536]{1,0:T(8,128)(2,1)S(1)}, bf16[384,1536]{1,0:T(8,128)(2,1)}, u32[]{:S(2)}) copy-start(bf16[384,1536]{1,0:T(8,128)(2,1)} %w_ref.3) | copy-start | bytes 3538948
  0.6 31.0 %copy-start.4 = (s32[1,8]{1,0:T(1,128)S(1)}, s32[1,8]{1,0:T(1,128)}, u32[]{:S(2)}) copy-start(s32[1,8]{1,0:T(1,128)} %lens_ref.5) | copy-start | bytes 100
  18.3 28.4 %all-to-all-start.2 = ((bf16[64,2,1536]{2,1,0:T(2,128)(2,1)}), bf16[64,2,1536]{2,1,0:T(2,128)(2,1)S(1)}, u32[]{:S(2)}, u32[]{:S(2)}) async-start(bf16[64,2,1536]{2,1,0:T(2,128)(2,1)} %broadcast_in_dim.15), calls=%async_computation.2 | async-start | bytes 786432 | tf_op jit(solution)/shard_map/all_to_all | solution.py:219
  31.7 1.0 copy-start.1
  32.7 0.9 copy-start.2
  33.6 0.9 copy-start.3
  34.6 18.6 %copy-start.7 = (s32[512]{0:T(512)S(1)}, s32[512]{0:T(512)}, u32[]{:S(2)}) copy-start(s32[512]{0:T(512)} %param.13) | copy-start | bytes 6148
  46.7 14.0 %all-to-all-start = ((f32[4,8,2048]{2,1,0:T(8,128)}), f32[4,8,2048]{2,1,0:T(8,128)S(1)}, u32[]{:S(2)}, u32[]{:S(2)}) async-start(f32[4,8,2048]{2,1,0:T(8,128)} %attend.1), calls=%async_computation | async-start | bytes 524288 | tf_op jit(solution)/shard_map/all_to_all | solution.py:231
  60.7 0.7 copy-start.5
  103.2 4.6 %collective-permute-start = (bf16[24,64]{1,0:T(8,128)(2,1)}, bf16[24,64]{1,0:T(8,128)(2,1)S(1)}, u32[]{:S(2)}, u32[]{:S(2)}) collective-permute-start(bf16[24,64]{1,0:T(8,128)(2,1)} %get-tuple-element.14), channel_id=1, source_target_pairs={{0,1},{1,0},{2,3},{3,2},{4,5},{5,4},{6,7},{7,6},{8,9},{9,8},{10,11... | collective-permute-start | bytes 9224 | tf_op jit(solution)/shard_map/ppermute | solution.py:267
  107.7 0.6 copy-start.6

commit v2 on v1

--- a/solution.py
+++ b/solution.py
@@ -63,11 +63,10 @@
     return column.astype(jnp.float32)
 
 
-def attend_kernel(lens_ref, q_ref, k_ref, v_ref, w_ref, out_ref, total):
+def attend_kernel(lens_ref, q_ref, k_ref, v_ref, w_ref, out_ref, sums_ref, total):
     seq_len, width = q_ref.shape
     heads = width // HD
     docs = lens_ref.shape[1]
-    features = w_ref.shape[1]
     kv_head = lax.axis_index("head") * heads // (HEADS // KV_HEADS)
     columns = pl.ds(pl.multiple_of(kv_head * HD, HD), HD)
     seg, start = document_of(lens_ref, docs, (1, seq_len), 1)
@@ -104,23 +103,35 @@
         [sums[h * docs : (h + 1) * docs] for h in range(heads)], axis=1
     ) / lens_column(lens_ref, docs)
     emb = exact_dot(pooled, w_ref[...], (((1,), (0,)), ((), ())))
-    for k in range(out_ref.shape[0]):
-        out_ref[k, :, :features] = emb
-        out_ref[k, :, features:] = by_head[:docs, :]
+    out_ref[...] = emb
+    sums_ref[...] = by_head[:docs, :]
+
+
+def pair_logits(unit, q_ref):
+    half = q_ref.shape[1]
+    docs = unit.shape[0]
+    both = jnp.concatenate([unit[:, :half], unit[:, half:]], axis=0)
+    parts = lax.dot_general(both, q_ref[...], NT, preferred_element_type=jnp.float32)
+    even = lax.broadcasted_iota(jnp.int32, (docs, q_ref.shape[0]), 1) % 2 == 0
+    mine = jnp.where(even, parts[:docs], parts[docs:])
+    width = mine.shape[1]
+    other = jnp.where(even, pltpu.roll(mine, width - 1, 1), pltpu.roll(mine, 1, 1))
+    return sim_scale * (mine + other)
+
+
+def positive_mask(pos_ref, docs):
+    count = pos_ref.shape[1]
+    positive = pos_ref[pl.ds(lax.axis_index((DP[3], "head")), 1), :]
+    owned = lax.axis_index(DP[:3]) * docs + lax.broadcasted_iota(jnp.int32, (docs, count), 0)
+    return positive == owned
 
 
 def logits_kernel(emb_ref, q_ref, pos_ref, out_ref, logits_ref, unit_ref, rnorm_ref):
-    docs = emb_ref.shape[1]
-    features = q_ref.shape[1]
-    emb = emb_ref[0, :, :features]
-    for k in range(1, emb_ref.shape[0]):
-        emb = emb + emb_ref[k, :, :features]
+    emb = jnp.concatenate([emb_ref[k] for k in range(emb_ref.shape[0])], axis=0)
     rnorm = 1.0 / jnp.sqrt(jnp.sum(emb * emb, axis=1, keepdims=True) + 1e-06)
     unit = emb * rnorm
-    logits = sim_scale * lax.dot_general(
-        unit.astype(jnp.bfloat16), q_ref[...], NT, preferred_element_type=jnp.float32
-    )
-    chosen = positive_mask(pos_ref, docs)
+    logits = pair_logits(unit.astype(jnp.bfloat16), q_ref)
+    chosen = positive_mask(pos_ref, emb.shape[0])
     top = jnp.max(logits, axis=0, keepdims=True)
     lse = top + jnp.log(jnp.sum(jnp.exp(logits - top), axis=0, keepdims=True))
     positive = jnp.sum(jnp.where(chosen, logits, 0.0), axis=0, keepdims=True)
@@ -132,43 +143,50 @@
     rnorm_ref[...] = jnp.broadcast_to(rnorm, rnorm_ref.shape)
 
 
-def positive_mask(pos_ref, docs):
-    count = pos_ref.shape[1]
-    positive = pos_ref[pl.ds(lax.axis_index("head"), 1), :]
-    owned = lax.axis_index(DP) * docs + lax.broadcasted_iota(jnp.int32, (docs, count), 0)
-    return positive == owned
-
-
-def slopes_kernel(stats_ref, logits_ref, q_ref, pos_ref, out_ref):
-    docs = logits_ref.shape[0]
-    features = q_ref.shape[1]
+def slopes_kernel(stats_ref, logits_ref, unit_ref, rnorm_ref, q_ref, pos_ref, out_ref):
+    pair_docs = logits_ref.shape[0]
+    half = q_ref.shape[1]
+    features = 2 * half
+    split = out_ref.shape[0] // 2
+    docs = pair_docs // 2
     each = stats_ref[:, 0, :]
     top = jnp.max(each, axis=0, keepdims=True)
     lse = top + jnp.log(jnp.sum(jnp.exp(each - top), axis=0, keepdims=True))
     positive = jnp.sum(stats_ref[:, 1, :], axis=0, keepdims=True)
-    chosen = positive_mask(pos_ref, docs)
+    chosen = positive_mask(pos_ref, pair_docs)
     slopes = jnp.exp(logits_ref[...] - lse) - chosen.astype(jnp.float32)
-    grads = sim_scale * exact_dot(slopes, q_ref[...], (((1,), (0,)), ((), ())))
+    even = lax.broadcasted_iota(jnp.int32, slopes.shape, 1) % 2 == 0
+    both = jnp.concatenate([jnp.where(even, slopes, 0.0), jnp.where(even, 0.0, slopes)], axis=0)
+    parts = sim_scale * exact_dot(both, q_ref[...], (((1,), (0,)), ((), ())))
+    grads = jnp.concatenate([parts[:pair_docs], parts[pair_docs:]], axis=1)
+    unit = unit_ref[...]
+    inner = jnp.sum(unit * grads, axis=1, keepdims=True)
+    grads = (rnorm_ref[:, :1] * (grads - unit * inner)).astype(jnp.bfloat16)
     losses = jnp.broadcast_to(lse - positive, (docs, lse.shape[1]))
-    for k in range(out_ref.shape[0]):
-        out_ref[k, :, :features] = grads
-        out_ref[k, :, features:] = losses
-
-
-def context_kernel(lens_ref, grads_ref, unit_ref, rnorm_ref, w_ref, kept_ref, sent_ref, loss_ref):
-    docs, features = unit_ref.shape
+    row = lax.broadcasted_iota(jnp.int32, losses.shape, 0)
+    high = losses.astype(jnp.bfloat16).astype(jnp.float32)
+    mid = (losses - high).astype(jnp.bfloat16).astype(jnp.float32)
+    losses = jnp.where(row == 0, high, jnp.where(row == 1, mid, losses - high - mid))
+    for k in range(2 * split):
+        core = k // split
+        out_ref[k, :, :features] = grads[core * docs : (core + 1) * docs]
+        out_ref[k, :, features:] = losses.astype(jnp.bfloat16)
+
+
+def context_kernel(lens_ref, grads_ref, w_ref, kept_ref, sent_ref, loss_ref):
+    docs = lens_ref.shape[1]
+    features = w_ref.shape[1]
     heads = w_ref.shape[0] // HD
     half = HD // 2
-    grads = grads_ref[0]
+    grads = grads_ref[0].astype(jnp.float32)
     for k in range(1, grads_ref.shape[0]):
-        grads = grads + grads_ref[k]
-    count = grads_ref.shape[0] * (grads.shape[1] - features)
-    loss_ref[...] = jnp.sum(grads[:1, features:], axis=1, keepdims=True) / count
-    grads = grads[:, :features]
-    unit = unit_ref[...]
-    inner = jnp.sum(unit * grads, axis=1, keepdims=True)
-    g_emb = rnorm_ref[:, :1] * (grads - unit * inner)
-    g_pooled = exact_dot(g_emb, w_ref[...], NT)
+        grads = grads + grads_ref[k].astype(jnp.float32)
+    lanes = grads.shape[1] - features
+    count = grads_ref.shape[0] * lanes
+    loss_ref[...] = (
+        jnp.sum(jnp.sum(grads[:3, features:], axis=0, keepdims=True), axis=1, keepdims=True) / count
+    )
+    g_pooled = exact_dot(grads[:, :features], w_ref[...], NT)
     scaled = (g_pooled / lens_column(lens_ref, docs) * loss_scale).astype(jnp.bfloat16)
     rows = jnp.concatenate(
         [scaled[:, h * HD : (h + 1) * HD] for h in range(heads)], axis=0
@@ -179,23 +197,19 @@
     sent_ref[...] = jnp.where(odd, lower, upper)
 
 
-def values_kernel(lens_ref, emb_ref, mine_ref, theirs_ref, out_ref):
-    docs = emb_ref.shape[1]
-    seq_len = out_ref.shape[0]
+def values_kernel(lens_ref, my_sums_ref, their_sums_ref, mine_ref, theirs_ref, out_ref):
+    docs = lens_ref.shape[1]
+    seq_len = out_ref.shape[1]
     heads = mine_ref.shape[0] // docs
-    me = lax.axis_index("head")
-    partner = me + 1 - 2 * (me % 2)
     seg, _ = document_of(lens_ref, docs, (1, seq_len), 1)
     member = lax.broadcasted_iota(jnp.int32, (docs, seq_len), 0) == seg
-    features = emb_ref.shape[2] - seq_len
     shares = []
-    for owner in (me, partner):
-        by_head = emb_ref[owner, :, features:]
-        shares += [jnp.where(member, by_head[h : h + 1, :], 0.0) for h in range(heads)]
+    for sums in (my_sums_ref, their_sums_ref):
+        shares += [jnp.where(member, sums[h : h + 1, :], 0.0) for h in range(heads)]
     slopes = jnp.concatenate([mine_ref[...], theirs_ref[...]], axis=0)
     out = lax.dot_general(
+        jnp.concatenate([slopes] * 3, axis=0),
         three_terms(jnp.concatenate(shares, axis=0)),
-        jnp.concatenate([slopes] * 3, axis=0),
         TN,
         preferred_element_type=jnp.float32,
     )
@@ -210,48 +224,56 @@
     split = lax.axis_size("head")
     cores = lax.axis_size(DP[3])
     others = lax.axis_size(DP[:3])
-    n_dp = cores * others
+    lanes = 2 * others
     f32, bf16 = jnp.float32, jnp.bfloat16
-
-    rows = jnp.broadcast_to(queries[None], (cores, *queries.shape)).reshape(cores * split, 1, -1)
-    rows = lax.all_to_all(rows, (DP[3], "head"), 0, 0, tiled=True).reshape(cores, features)
-    rows = jnp.broadcast_to(rows[None], (others, cores, features))
-    every = lax.all_to_all(rows, DP[:3], 0, 0, tiled=True).reshape(n_dp, features)
-    pos = positives.reshape(n_dp, split).T
-
-    partial = pl.pallas_call(
+    big = pltpu.CompilerParams(vmem_limit_bytes=60 * 2**20)
+
+    row = lax.all_to_all(queries.reshape(split, 1, -1), "head", 0, 0, tiled=True)
+    emb, sums = pl.pallas_call(
         attend_kernel,
-        out_shape=jax.ShapeDtypeStruct((split, docs, features + seq_len), f32),
+        out_shape=(
+            jax.ShapeDtypeStruct((docs, features), f32),
+            jax.ShapeDtypeStruct((docs, seq_len), f32),
+        ),
         in_specs=[SMEM] + [VMEM] * 4,
-        out_specs=VMEM,
+        out_specs=(VMEM, VMEM),
         scratch_shapes=[pltpu.VMEM((seq_len, HD), f32)],
-        compiler_params=pltpu.CompilerParams(vmem_limit_bytes=32 * 2**20),
+        compiler_params=big,
         name="attend",
     )(lengths, attn_queries, keys, values, out_weight)
-    partial = lax.all_to_all(partial, "head", 0, 0, tiled=True)
+    row, emb, sums = lax.optimization_barrier((row, emb, sums))
+    rows = jnp.broadcast_to(row.reshape(1, 2, features // 2), (others, 2, features // 2))
+    every = lax.all_to_all(rows, DP[:3], 0, 0, tiled=True).reshape(lanes, features // 2)
+    pos = jnp.repeat(positives.reshape(others, cores * split).T, 2, axis=1)
+
+    whole = emb
+    for apart in range(1, split):
+        whole = whole + lax.ppermute(emb, "head", [(i, i ^ apart) for i in range(split)])
+    their_sums = lax.ppermute(sums, "head", [(i, i ^ 1) for i in range(split)])
+    pair = lax.all_gather(whole, DP[3])
 
     stats, logits, unit, rnorm = pl.pallas_call(
         logits_kernel,
         out_shape=(
-            jax.ShapeDtypeStruct((n_dp, 2, n_dp), f32),
-            jax.ShapeDtypeStruct((docs, n_dp), f32),
-            jax.ShapeDtypeStruct((docs, features), f32),
-            jax.ShapeDtypeStruct((docs, HD), f32),
+            jax.ShapeDtypeStruct((others, 2, lanes), f32),
+            jax.ShapeDtypeStruct((cores * docs, lanes), f32),
+            jax.ShapeDtypeStruct((cores * docs, features), f32),
+            jax.ShapeDtypeStruct((cores * docs, HD), f32),
         ),
         in_specs=[VMEM] * 3,
         out_specs=(VMEM,) * 4,
         name="logits",
-    )(partial, every, pos)
-    stats = lax.all_to_all(stats, DP, 0, 0, tiled=True)
+    )(pair, every, pos)
+    stats = lax.all_to_all(stats, DP[:3], 0, 0, tiled=True)
 
     grads = pl.pallas_call(
         slopes_kernel,
-        out_shape=jax.ShapeDtypeStruct((split, docs, features + n_dp), f32),
-        in_specs=[VMEM] * 4,
+        out_shape=jax.ShapeDtypeStruct((cores * split, docs, features + lanes), bf16),
+        in_specs=[VMEM] * 6,
         out_specs=VMEM,
         name="slopes",
-    )(stats, logits, every, pos)
-    grads = lax.all_to_all(grads, "head", 0, 0, tiled=True)
+    )(stats, logits, unit, rnorm, every, pos)
+    grads = lax.all_to_all(grads, (DP[3], "head"), 0, 0, tiled=True)
 
     kept, sent, loss = pl.pallas_call(
         context_kernel,
@@ -260,20 +282,20 @@
             jax.ShapeDtypeStruct((heads * docs, HD // 2), bf16),
             jax.ShapeDtypeStruct((1, 1), f32),
         ),
-        in_specs=[SMEM] + [VMEM] * 4,
+        in_specs=[SMEM] + [VMEM] * 2,
         out_specs=(VMEM,) * 3,
         name="context",
-    )(lengths, grads, unit, rnorm, out_weight)
+    )(lengths, grads, out_weight)
     got = lax.ppermute(sent, "head", [(i, i ^ 1) for i in range(split)])
 
     d_values = pl.pallas_call(
         values_kernel,
-        out_shape=jax.ShapeDtypeStruct((seq_len, HD // 2), bf16),
-        in_specs=[SMEM] + [VMEM] * 3,
+        out_shape=jax.ShapeDtypeStruct((HD // 2, seq_len), bf16),
+        in_specs=[SMEM] + [VMEM] * 4,
         out_specs=VMEM,
         name="slopes_of_values",
-    )(lengths, partial, kept, got)
-    return d_values, loss.reshape(())
+    )(lengths, sums, their_sums, kept, got)
+    return d_values.T, loss.reshape(())
 
 
 def solution(mesh):

time: 114 us -> 106 us (0.930)
  blocking collectives: 49.4 us -> 24.6 us
  starting transfers between devices: 23.1 us -> 44.4 us
  local copies, waits for them, and re-layouts: 9.87 us -> 4.9 us
  other arithmetic: 0.73 us -> 2.19 us
    all_to_all x3 -> x1, blocking collectives: 49.4 us -> 20 us  [per_device(): stats = lax.all_to_all(stats, DP[:3], 0, 0, tiled=True)]
    ppermute x0 -> x4, starting transfers between devices: none -> 12.5 us  [the longest x3 9.26 us: per_device(): lax.ppermute(emb, 'head', [(i, i ^ apart) for i in range(split)])]
    all_to_all x2 -> x3, starting transfers between devices: 19.8 us -> 30 us  [the longest x1 17.4 us: per_device(): lax.all_to_all(rows, DP[:3], 0, 0, tiled=True).reshape(lanes, features // 2)]
    all_gather x0 -> x1, blocking collectives: none -> 4.6 us  [per_device(): pair = lax.all_gather(whole, DP[3])]
    unnamed x19 -> x11, local copies, waits for them, and re-layouts: 5.98 us -> 1.96 us
    all_to_all x2 -> x3, waiting for transfers between devices: 15.2 us -> 13.3 us  [the longest x1 7.96 us: per_device(): lax.all_to_all(rows, DP[:3], 0, 0, tiled=True).reshape(lanes, features // 2)]
    ppermute x1, starting transfers between devices: 3.24 us -> 1.91 us  [per_device(): got = lax.ppermute(sent, 'head', [(i, i ^ 1) for i in range(split)])]
    ppermute x1, waiting for transfers between devices: 1.32 us -> 2.64 us  [per_device(): got = lax.ppermute(sent, 'head', [(i, i ^ 1) for i in range(split)])]
  transfers between devices with their start and end apart: 3 -> 8, of which waited for: 3 -> 4; matrix products, arithmetic and copies ran while one was open for 1% -> 2% of each run, Pallas kernels for 3% -> 6%
where the time goes in v2:
time: 106 us; the launch traced here: 105 us
  starting transfers between devices  44.4 us (42%)
  blocking collectives  24.6 us (23%)
  waiting for transfers between devices  15.9 us (15%)
  Pallas kernels  12.2 us (12%)
  local copies, waits for them, and re-layouts  4.9 us (5%)
  other arithmetic  2.19 us (2%)
    all_to_all x1, blocking collectives, per_device(): stats = lax.all_to_all(stats, DP[:3], 0, 0, tiled=True)  20 us
    all_to_all x1, starting transfers between devices, per_device(): lax.all_to_all(rows, DP[:3], 0, 0, tiled=True).reshape(lanes, features // 2)  17.4 us
    ppermute x3, starting transfers between devices, per_device(): lax.ppermute(emb, 'head', [(i, i ^ apart) for i in range(split)])  9.26 us
    all_to_all x1, waiting for transfers between devices, per_device(): lax.all_to_all(rows, DP[:3], 0, 0, tiled=True).reshape(lanes, features // 2)  7.96 us
    all_to_all x1, starting transfers between devices, per_device(): grads = lax.all_to_all(grads, (DP[3], 'head'), 0, 0, tiled=True)  7.2 us
    all_to_all x1, starting transfers between devices, per_device(): lax.all_to_all(queries.reshape(split, 1, -1), 'head', 0, 0, tiled=True)  5.42 us
    all_to_all x1, waiting for transfers between devices, per_device(): grads = lax.all_to_all(grads, (DP[3], 'head'), 0, 0, tiled=True)  4.72 us
    all_gather x1, blocking collectives, per_device(): pair = lax.all_gather(whole, DP[3])  4.6 us
  transfers between devices with their start and end apart: 8, of which 4 were waited for; matrix products, arithmetic and copies ran while one was open for 2% of the time, Pallas kernels for 6%

profile of v2, /device:TPU:1, one launch (start us, length us, event | category | flops | bytes accessed | tf_op | source)
XLA Modules:
  0.0 105.0 jit_solution(6563187804333322633)
XLA Ops:
  1.2 1.3 %reduce.1 = bf16[4,384]{1,0:T(4,128)(2,1)S(1)} reduce(bf16[4,1,384]{2,0,1:T(4,128)(2,1)} %bitcast.10, bf16[]{:T(256)} %broadcast.1), dimensions={1}, to_apply=%copy.13.reduce_sub_computation | reduce | bytes 6146 | tf_op jit(solution)/shard_map/reshape | solution.py:231
  2.5 0.7 reshape.28
  3.2 5.4 %all-to-all-start = ((bf16[4,2,192]{2,1,0:T(2,128)(2,1)}), bf16[4,2,192]{2,1,0:T(2,128)(2,1)S(1)}, u32[]{:S(2)}, u32[]{:S(2)}) async-start(bf16[4,2,192]{2,1,0:T(2,128)(2,1)} %reshape.28), calls=%async_computation | async-start | bytes 8192 | tf_op jit(solution)/shard_map/all_to_all | solution.py:231
  8.6 3.8 %attend.1 = (f32[8,1536]{1,0:T(8,128)}, f32[8,512]{1,0:T(8,128)}) custom-call(s32[1,8]{1,0:T(1,128)} %lens_ref.5, bf16[512,384]{1,0:T(8,128)(2,1)} %q_ref.1, bf16[512,256]{1,0:T(8,128)(2,1)} %k_ref.1, bf16[512,256]{1,0:T(8,128)(2,1)} %v_ref.1, bf16[384,1536]{1,0:T(8,128)(2,1)} %w_ref.3), custom_call_target="tpu_custom_call" | custom-call | tf_op jit(solution)/shard_map/attend/pallas_call | solution.py:232
  13.1 2.8 %collective-permute-start.1 = (f32[8,1536]{1,0:T(8,128)}, f32[8,1536]{1,0:T(8,128)S(1)}, u32[]{:S(2)}, u32[]{:S(2)}) collective-permute-start(f32[8,1536]{1,0:T(8,128)} %get-tuple-element.17), channel_id=1, source_target_pairs={{0,1},{1,0},{2,3},{3,2},{4,5},{5,4},{6,7},{7,6},{8,9},{9,8},{10,11... | collective-permute-start | bytes 147464 | tf_op jit(solution)/shard_map/ppermute | solution.py:251
  15.9 4.0 %collective-permute-start.2 = (f32[8,1536]{1,0:T(8,128)}, f32[8,1536]{1,0:T(8,128)S(1)}, u32[]{:S(2)}, u32[]{:S(2)}) collective-permute-start(f32[8,1536]{1,0:T(8,128)} %get-tuple-element.17), channel_id=1, source_target_pairs={{0,2},{1,3},{2,0},{3,1},{4,6},{5,7},{6,4},{7,5},{8,10},{9,11},{10,... | collective-permute-start | bytes 147464 | tf_op jit(solution)/shard_map/ppermute | solution.py:251
  19.9 2.5 %collective-permute-start.3 = (f32[8,1536]{1,0:T(8,128)}, f32[8,1536]{1,0:T(8,128)S(1)}, u32[]{:S(2)}, u32[]{:S(2)}) collective-permute-start(f32[8,1536]{1,0:T(8,128)} %get-tuple-element.17), channel_id=1, source_target_pairs={{0,3},{1,2},{2,1},{3,0},{4,7},{5,6},{6,5},{7,4},{8,11},{9,10},{10,... | collective-permute-start | bytes 147464 | tf_op jit(solution)/shard_map/ppermute | solution.py:251
  23.2 0.8 broadcast_in_dim.11
  24.0 17.4 %all-to-all-start.1 = ((bf16[64,2,768]{2,1,0:T(2,128)(2,1)}), bf16[64,2,768]{2,1,0:T(2,128)(2,1)S(1)}, u32[]{:S(2)}, u32[]{:S(2)}) async-start(bf16[64,2,768]{2,1,0:T(2,128)(2,1)} %broadcast_in_dim.11), calls=%async_computation.1 | async-start | bytes 393216 | tf_op jit(solution)/shard_map/all_to_all | solution.py:246
  41.4 0.8 add_add_fusion
  42.2 4.6 %all-gather = f32[16,1536]{1,0:T(8,128)} all-gather(f32[8,1536]{1,0:T(8,128)S(1)} %add_add_fusion), channel_id=2, replica_groups=mesh['dp_0'=4,'dp_1'=8,'dp_2'=2,'dp_3'=2,'head'=4] {'dp_3'}, dimensions={0}, use_global_device_ids=true | all-gather | bytes 147456 | tf_op jit(solution)/shard_map/all_gather | solution.py:253
  46.8 8.0 %all-to-all-done.1 = bf16[64,2,768]{2,1,0:T(2,128)(2,1)S(1)} async-done(((bf16[64,2,768]{2,1,0:T(2,128)(2,1)}), bf16[64,2,768]{2,1,0:T(2,128)(2,1)S(1)}, u32[]{:S(2)}, u32[]{:S(2)}) %all-to-all-start.1) | async-done | bytes 196640 | tf_op jit(solution)/shard_map/all_to_all | solution.py:246
  54.8 0.8 reshape.22.q_ref
  55.6 2.0 %logits.1 = (f32[64,2,128]{2,1,0:T(2,128)}, f32[16,128]{1,0:T(8,128)}, f32[16,1536]{1,0:T(8,128)}, f32[16,128]{1,0:T(8,128)}) custom-call(f32[2,8,1536]{2,1,0:T(8,128)} %bitcast.6, bf16[128,768]{1,0:T(8,128)(2,1)} %reshape.22.q_ref, s32[8,128]{1,0:T(8,128)} %copy.14.pos_ref), custom_call_target="tpu_custom_call" | custom-call | tf_op jit(solution)/shard_map/logits/pallas_call | solution.py:255
  57.6 20.0 %all_to_all.20.stats_ref = f32[64,2,128]{2,1,0:T(2,128)} all-to-all(f32[64,2,128]{2,1,0:T(2,128)} %get-tuple-element.19), channel_id=1, replica_groups=mesh['dp_0'=4,'dp_1'=8,'dp_2'=2,'dp_3'=2,'head'=4] {'dp_0','dp_1','dp_2'}, dimensions={0} | all-to-all | bytes 131072 | tf_op jit(solution)/shard_map/all_to_all | solution.py:267
  77.6 2.1 %slopes.1 = bf16[8,8,1664]{2,1,0:T(8,128)(2,1)} custom-call(f32[64,2,128]{2,1,0:T(2,128)} %all_to_all.20.stats_ref, f32[16,128]{1,0:T(8,128)} %get-tuple-element.20.logits_ref, f32[16,1536]{1,0:T(8,128)} %get-tuple-element.21.unit_ref, f32[16,128]{1,0:T(8,128)} %get-tuple-element.22.rnorm_ref, bf16[128,768]{1,0:T(8,128)(2,1)} %reshape.22.q_ref, ...), custom_call_target="tpu_custom_call" | custom-call | tf_op jit(solution)/shard_map/slopes/pallas_call | solution.py:269
  79.7 7.2 %all-to-all-start.3 = ((bf16[8,8,1664]{2,1,0:T(8,128)(2,1)}), bf16[8,8,1664]{2,1,0:T(8,128)(2,1)S(1)}, u32[]{:S(2)}, u32[]{:S(2)}) async-start(bf16[8,8,1664]{2,1,0:T(8,128)(2,1)} %slopes.1), calls=%async_computation.3 | async-start | bytes 425984 | tf_op jit(solution)/shard_map/all_to_all | solution.py:276
  86.9 3.3 %collective-permute-start = (f32[8,512]{1,0:T(8,128)S(1)}, f32[8,512]{1,0:T(8,128)S(1)}, u32[]{:S(2)}, u32[]{:S(2)}) collective-permute-start(f32[8,512]{1,0:T(8,128)S(1)} %copy-done.1), channel_id=1, source_target_pairs={{0,1},{1,0},{2,3},{3,2},{4,5},{5,4},{6,7},{7,6},{8,9},{9,8},{10,11... | collective-permute-start | bytes 49160 | tf_op jit(solution)/shard_map/ppermute | solution.py:252
  90.2 4.7 %all-to-all-done.3.grads_ref = bf16[8,8,1664]{2,1,0:T(8,128)(2,1)S(1)} async-done(((bf16[8,8,1664]{2,1,0:T(8,128)(2,1)}), bf16[8,8,1664]{2,1,0:T(8,128)(2,1)S(1)}, u32[]{:S(2)}, u32[]{:S(2)}) %all-to-all-start.3) | async-done | bytes 213024 | tf_op jit(solution)/shard_map/all_to_all | solution.py:276
  94.9 0.7 copy-done
  95.6 2.6 %context.1 = (bf16[24,64]{1,0:T(8,128)(2,1)}, bf16[24,64]{1,0:T(8,128)(2,1)}, f32[1,1]{1,0:T(1,128)}) custom-call(s32[1,8]{1,0:T(1,128)} %lens_ref.5, bf16[8,8,1664]{2,1,0:T(8,128)(2,1)} %copy-done, bf16[384,1536]{1,0:T(8,128)(2,1)} %w_ref.3), custom_call_target="tpu_custom_call" | custom-call | tf_op jit(solution)/shard_map/context/pallas_call | solution.py:278
  98.2 1.9 %collective-permute-start.4 = (bf16[24,64]{1,0:T(8,128)(2,1)}, bf16[24,64]{1,0:T(8,128)(2,1)S(1)}, u32[]{:S(2)}, u32[]{:S(2)}) collective-permute-start(bf16[24,64]{1,0:T(8,128)(2,1)} %get-tuple-element.24), channel_id=1, source_target_pairs={{0,1},{1,0},{2,3},{3,2},{4,5},{5,4},{6,7},{7,6},{8,9},{9,8},{10,11... | collective-permute-start | bytes 9224 | tf_op jit(solution)/shard_map/ppermute | solution.py:289
  100.1 2.6 %collective-permute-done.4.theirs_ref = bf16[24,64]{1,0:T(8,128)(2,1)S(1)} collective-permute-done((bf16[24,64]{1,0:T(8,128)(2,1)}, bf16[24,64]{1,0:T(8,128)(2,1)S(1)}, u32[]{:S(2)}, u32[]{:S(2)}) %collective-permute-start.4) | collective-permute-done | bytes 3104 | tf_op jit(solution)/shard_map/ppermute | solution.py:289
  103.4 1.6 %slopes_of_values.1 = bf16[64,512]{1,0:T(8,128)(2,1)} custom-call(s32[1,8]{1,0:T(1,128)} %lens_ref.5, f32[8,512]{1,0:T(8,128)} %get-tuple-element.16.my_sums_ref, f32[8,512]{1,0:T(8,128)} %copy-done.2, bf16[24,64]{1,0:T(8,128)(2,1)} %get-tuple-element.23.mine_ref, bf16[24,64]{1,0:T(8,128)(2,1)} %copy-done.3), custom_call_target="tpu_custom_call" | custom-call | tf_op jit(solution)/shard_map/slopes_of_values/pallas_call | solution.py:291
  (21 shorter events, 2.6 us)
Async XLA Ops:
  0.6 21.8 %copy-start.4 = (s32[512]{0:T(512)S(1)}, s32[512]{0:T(512)}, u32[]{:S(2)}) copy-start(s32[512]{0:T(512)} %param.13) | copy-start | bytes 6148
  3.2 9.8 %all-to-all-start = ((bf16[4,2,192]{2,1,0:T(2,128)(2,1)}), bf16[4,2,192]{2,1,0:T(2,128)(2,1)S(1)}, u32[]{:S(2)}, u32[]{:S(2)}) async-start(bf16[4,2,192]{2,1,0:T(2,128)(2,1)} %reshape.28), calls=%async_computation | async-start | bytes 8192 | tf_op jit(solution)/shard_map/all_to_all | solution.py:231
  13.1 28.3 %collective-permute-start.1 = (f32[8,1536]{1,0:T(8,128)}, f32[8,1536]{1,0:T(8,128)S(1)}, u32[]{:S(2)}, u32[]{:S(2)}) collective-permute-start(f32[8,1536]{1,0:T(8,128)} %get-tuple-element.17), channel_id=1, source_target_pairs={{0,1},{1,0},{2,3},{3,2},{4,5},{5,4},{6,7},{7,6},{8,9},{9,8},{10,11... | collective-permute-start | bytes 147464 | tf_op jit(solution)/shard_map/ppermute | solution.py:251
  15.9 25.5 %collective-permute-start.2 = (f32[8,1536]{1,0:T(8,128)}, f32[8,1536]{1,0:T(8,128)S(1)}, u32[]{:S(2)}, u32[]{:S(2)}) collective-permute-start(f32[8,1536]{1,0:T(8,128)} %get-tuple-element.17), channel_id=1, source_target_pairs={{0,2},{1,3},{2,0},{3,1},{4,6},{5,7},{6,4},{7,5},{8,10},{9,11},{10,... | collective-permute-start | bytes 147464 | tf_op jit(solution)/shard_map/ppermute | solution.py:251
  19.9 21.6 %collective-permute-start.3 = (f32[8,1536]{1,0:T(8,128)}, f32[8,1536]{1,0:T(8,128)S(1)}, u32[]{:S(2)}, u32[]{:S(2)}) collective-permute-start(f32[8,1536]{1,0:T(8,128)} %get-tuple-element.17), channel_id=1, source_target_pairs={{0,3},{1,2},{2,1},{3,0},{4,7},{5,6},{6,5},{7,4},{8,11},{9,10},{10,... | collective-permute-start | bytes 147464 | tf_op jit(solution)/shard_map/ppermute | solution.py:251
  24.0 30.8 %all-to-all-start.1 = ((bf16[64,2,768]{2,1,0:T(2,128)(2,1)}), bf16[64,2,768]{2,1,0:T(2,128)(2,1)S(1)}, u32[]{:S(2)}, u32[]{:S(2)}) async-start(bf16[64,2,768]{2,1,0:T(2,128)(2,1)} %broadcast_in_dim.11), calls=%async_computation.1 | async-start | bytes 393216 | tf_op jit(solution)/shard_map/all_to_all | solution.py:246
  41.4 45.5 %copy-start.1 = (f32[8,512]{1,0:T(8,128)S(1)}, f32[8,512]{1,0:T(8,128)}, u32[]{:S(2)}) copy-start(f32[8,512]{1,0:T(8,128)} %get-tuple-element.16.my_sums_ref) | copy-start | bytes 49156
  79.7 15.2 %all-to-all-start.3 = ((bf16[8,8,1664]{2,1,0:T(8,128)(2,1)}), bf16[8,8,1664]{2,1,0:T(8,128)(2,1)S(1)}, u32[]{:S(2)}, u32[]{:S(2)}) async-start(bf16[8,8,1664]{2,1,0:T(8,128)(2,1)} %slopes.1), calls=%async_computation.3 | async-start | bytes 425984 | tf_op jit(solution)/shard_map/all_to_all | solution.py:276
  86.9 13.2 %collective-permute-start = (f32[8,512]{1,0:T(8,128)S(1)}, f32[8,512]{1,0:T(8,128)S(1)}, u32[]{:S(2)}, u32[]{:S(2)}) collective-permute-start(f32[8,512]{1,0:T(8,128)S(1)} %copy-done.1), channel_id=1, source_target_pairs={{0,1},{1,0},{2,3},{3,2},{4,5},{5,4},{6,7},{7,6},{8,9},{9,8},{10,11... | collective-permute-start | bytes 49160 | tf_op jit(solution)/shard_map/ppermute | solution.py:252
  94.9 0.7 copy-start
  98.2 4.6 %collective-permute-start.4 = (bf16[24,64]{1,0:T(8,128)(2,1)}, bf16[24,64]{1,0:T(8,128)(2,1)S(1)}, u32[]{:S(2)}, u32[]{:S(2)}) collective-permute-start(bf16[24,64]{1,0:T(8,128)(2,1)} %get-tuple-element.24), channel_id=1, source_target_pairs={{0,1},{1,0},{2,3},{3,2},{4,5},{5,4},{6,7},{7,6},{8,9},{9,8},{10,11... | collective-permute-start | bytes 9224 | tf_op jit(solution)/shard_map/ppermute | solution.py:289
  100.1 2.6 %copy-start.2 = (f32[8,512]{1,0:T(8,128)}, f32[8,512]{1,0:T(8,128)S(1)}, u32[]{:S(2)}) copy-start(f32[8,512]{1,0:T(8,128)S(1)} %collective-permute-done.their_sums_ref) | copy-start | bytes 49156
  102.8 0.6 copy-start.3

commit v3 on v2

--- a/solution.py
+++ b/solution.py
@@ -13,6 +13,7 @@
 HD = 128
 DP = ("dp_0", "dp_1", "dp_2", "dp_3")
 LONGEST = 256
+HEAD = ("head_0", "head_1")
 
 sim_scale = 20.0
 loss_scale = 32768.0
@@ -63,11 +64,11 @@
     return column.astype(jnp.float32)
 
 
-def attend_kernel(lens_ref, q_ref, k_ref, v_ref, w_ref, out_ref, sums_ref, total):
+def attend_kernel(lens_ref, q_ref, k_ref, v_ref, w_ref, out_ref, total):
     seq_len, width = q_ref.shape
     heads = width // HD
     docs = lens_ref.shape[1]
-    kv_head = lax.axis_index("head") * heads // (HEADS // KV_HEADS)
+    kv_head = lax.axis_index(HEAD) * heads // (HEADS // KV_HEADS)
     columns = pl.ds(pl.multiple_of(kv_head * HD, HD), HD)
     seg, start = document_of(lens_ref, docs, (1, seq_len), 1)
     total[...] = jnp.zeros_like(total)
@@ -103,8 +104,30 @@
         [sums[h * docs : (h + 1) * docs] for h in range(heads)], axis=1
     ) / lens_column(lens_ref, docs)
     emb = exact_dot(pooled, w_ref[...], (((1,), (0,)), ((), ())))
-    out_ref[...] = emb
-    sums_ref[...] = by_head[:docs, :]
+    out_ref[:, : emb.shape[1]] = emb
+    out_ref[:, emb.shape[1] :] = by_head[:docs, :]
+
+
+def pack_kernel(q_ref, out_ref):
+    chunks = q_ref.shape[1] // HD
+    rows = q_ref[...].astype(jnp.float32)
+    rest = jnp.zeros((out_ref.shape[1] - chunks, HD), jnp.float32)
+    for k in range(q_ref.shape[0]):
+        parts = [rows[k : k + 1, c * HD : (c + 1) * HD] for c in range(chunks)]
+        out_ref[k] = jnp.concatenate([*parts, rest], axis=0).astype(jnp.bfloat16)
+
+
+def copies_kernel(row_ref, out_ref):
+    features = 2 * out_ref.shape[2]
+    chunks = features // row_ref.shape[0] // HD
+    parts = []
+    for k in range(row_ref.shape[0]):
+        block = row_ref[k].astype(jnp.float32)
+        parts += [block[c : c + 1, :] for c in range(chunks)]
+    middle = len(parts) // 2
+    halves = [jnp.concatenate(parts[:middle], axis=1), jnp.concatenate(parts[middle:], axis=1)]
+    both = jnp.concatenate(halves, axis=0).astype(jnp.bfloat16)
+    out_ref[...] = jnp.broadcast_to(both[None], out_ref.shape)
 
 
 def pair_logits(unit, q_ref):
@@ -120,13 +143,26 @@
 
 
 def positive_mask(pos_ref, docs):
-    count = pos_ref.shape[1]
-    positive = pos_ref[pl.ds(lax.axis_index((DP[3], "head")), 1), :]
-    owned = lax.axis_index(DP[:3]) * docs + lax.broadcasted_iota(jnp.int32, (docs, count), 0)
-    return positive == owned
-
-
-def logits_kernel(emb_ref, q_ref, pos_ref, out_ref, logits_ref, unit_ref, rnorm_ref):
+    count, classes = pos_ref.shape
+    mine = lax.broadcasted_iota(jnp.int32, (count, classes), 1) == lax.axis_index((DP[3], *HEAD))
+    lane = lax.broadcasted_iota(jnp.int32, (count, 2 * count), 1)
+    row = lax.broadcasted_iota(jnp.int32, (count, 2 * count), 0)
+    spread = (lane // 2 == row).astype(jnp.bfloat16)
+    pos = jnp.where(mine, pos_ref[...], 0)
+
+    def spread_out(digit):
+        lines = lax.dot_general(
+            digit.astype(jnp.float32).astype(jnp.bfloat16), spread, TN,
+            preferred_element_type=jnp.float32,
+        )
+        return jnp.sum(lines, axis=0, keepdims=True)
+
+    positive = 128.0 * spread_out(pos // 128) + spread_out(pos % 128)
+    owned = lax.axis_index(DP[:3]) * docs + lax.broadcasted_iota(jnp.int32, (docs, 2 * count), 0)
+    return (positive == owned.astype(jnp.float32)).astype(jnp.float32)
+
+
+def logits_kernel(emb_ref, q_ref, pos_ref, out_ref, logits_ref, chosen_ref, unit_ref, rnorm_ref):
     emb = jnp.concatenate([emb_ref[k] for k in range(emb_ref.shape[0])], axis=0)
     rnorm = 1.0 / jnp.sqrt(jnp.sum(emb * emb, axis=1, keepdims=True) + 1e-06)
     unit = emb * rnorm
@@ -134,16 +170,17 @@
     chosen = positive_mask(pos_ref, emb.shape[0])
     top = jnp.max(logits, axis=0, keepdims=True)
     lse = top + jnp.log(jnp.sum(jnp.exp(logits - top), axis=0, keepdims=True))
-    positive = jnp.sum(jnp.where(chosen, logits, 0.0), axis=0, keepdims=True)
+    positive = jnp.sum(logits * chosen, axis=0, keepdims=True)
     out_ref[...] = jnp.broadcast_to(
         jnp.concatenate([lse, positive], axis=0)[None], out_ref.shape
     )
     logits_ref[...] = logits
+    chosen_ref[...] = chosen
     unit_ref[...] = unit
     rnorm_ref[...] = jnp.broadcast_to(rnorm, rnorm_ref.shape)
 
 
-def slopes_kernel(stats_ref, logits_ref, unit_ref, rnorm_ref, q_ref, pos_ref, out_ref):
+def slopes_kernel(stats_ref, logits_ref, chosen_ref, unit_ref, rnorm_ref, q_ref, out_ref):
     pair_docs = logits_ref.shape[0]
     half = q_ref.shape[1]
     features = 2 * half
@@ -153,8 +190,7 @@
     top = jnp.max(each, axis=0, keepdims=True)
     lse = top + jnp.log(jnp.sum(jnp.exp(each - top), axis=0, keepdims=True))
     positive = jnp.sum(stats_ref[:, 1, :], axis=0, keepdims=True)
-    chosen = positive_mask(pos_ref, pair_docs)
-    slopes = jnp.exp(logits_ref[...] - lse) - chosen.astype(jnp.float32)
+    slopes = jnp.exp(logits_ref[...] - lse) - chosen_ref[...]
     even = lax.broadcasted_iota(jnp.int32, slopes.shape, 1) % 2 == 0
     both = jnp.concatenate([jnp.where(even, slopes, 0.0), jnp.where(even, 0.0, slopes)], axis=0)
     parts = sim_scale * exact_dot(both, q_ref[...], (((1,), (0,)), ((), ())))
@@ -173,42 +209,39 @@
         out_ref[k, :, features:] = losses.astype(jnp.bfloat16)
 
 
-def context_kernel(lens_ref, grads_ref, w_ref, kept_ref, sent_ref, loss_ref):
+def values_kernel(
+    lens_ref, grads_ref, my_rows_ref, their_rows_ref, my_sums_ref, their_sums_ref, out_ref, loss_ref
+):
     docs = lens_ref.shape[1]
-    features = w_ref.shape[1]
-    heads = w_ref.shape[0] // HD
+    features = my_rows_ref.shape[1]
+    seq_len = out_ref.shape[1]
     half = HD // 2
+    heads = my_rows_ref.shape[0] // HD
+    low = lax.axis_index(HEAD[1])
     grads = grads_ref[0].astype(jnp.float32)
     for k in range(1, grads_ref.shape[0]):
         grads = grads + grads_ref[k].astype(jnp.float32)
     lanes = grads.shape[1] - features
-    count = grads_ref.shape[0] * lanes
-    loss_ref[...] = (
-        jnp.sum(jnp.sum(grads[:3, features:], axis=0, keepdims=True), axis=1, keepdims=True) / count
-    )
-    g_pooled = exact_dot(grads[:, :features], w_ref[...], NT)
-    scaled = (g_pooled / lens_column(lens_ref, docs) * loss_scale).astype(jnp.bfloat16)
-    rows = jnp.concatenate(
-        [scaled[:, h * HD : (h + 1) * HD] for h in range(heads)], axis=0
-    )
-    odd = lax.axis_index("head") % 2 == 1
-    lower, upper = rows[:, :half], rows[:, half:]
-    kept_ref[...] = jnp.where(odd, upper, lower)
-    sent_ref[...] = jnp.where(odd, lower, upper)
-
-
-def values_kernel(lens_ref, my_sums_ref, their_sums_ref, mine_ref, theirs_ref, out_ref):
-    docs = lens_ref.shape[1]
-    seq_len = out_ref.shape[1]
-    heads = mine_ref.shape[0] // docs
+    loss_ref[...] = jnp.sum(
+        jnp.sum(grads[:3, features:], axis=0, keepdims=True), axis=1, keepdims=True
+    ) / (grads_ref.shape[0] * lanes)
+    terms = three_terms(grads[:, :features])
+    factor = loss_scale / lens_column(lens_ref, docs)
+    slopes = []
+    for h in range(heads):
+        rows = my_rows_ref[pl.ds(pl.multiple_of(h * HD + low * half, half), half), :]
+        slopes.append(lax.dot_general(terms, rows, NT, preferred_element_type=jnp.float32))
+    for h in range(heads):
+        rows = their_rows_ref[1 - low, h * half : (h + 1) * half, :]
+        slopes.append(lax.dot_general(terms, rows, NT, preferred_element_type=jnp.float32))
+    slopes = [(of_three(part) * factor).astype(jnp.bfloat16) for part in slopes]
     seg, _ = document_of(lens_ref, docs, (1, seq_len), 1)
     member = lax.broadcasted_iota(jnp.int32, (docs, seq_len), 0) == seg
     shares = []
     for sums in (my_sums_ref, their_sums_ref):
-        shares += [jnp.where(member, sums[h : h + 1, :], 0.0) for h in range(heads)]
-    slopes = jnp.concatenate([mine_ref[...], theirs_ref[...]], axis=0)
+        shares += [jnp.where(member, sums[h : h + 1, features:], 0.0) for h in range(heads)]
     out = lax.dot_general(
-        jnp.concatenate([slopes] * 3, axis=0),
+        jnp.concatenate(slopes * 3, axis=0),
         three_terms(jnp.concatenate(shares, axis=0)),
         TN,
         preferred_element_type=jnp.float32,
@@ -221,95 +254,111 @@
     heads = width // HD
     docs = lengths.shape[1]
     features = out_weight.shape[1]
-    split = lax.axis_size("head")
+    split = lax.axis_size(HEAD)
     cores = lax.axis_size(DP[3])
     others = lax.axis_size(DP[:3])
     lanes = 2 * others
     f32, bf16 = jnp.float32, jnp.bfloat16
     big = pltpu.CompilerParams(vmem_limit_bytes=60 * 2**20)
-
-    row = lax.all_to_all(queries.reshape(split, 1, -1), "head", 0, 0, tiled=True)
-    emb, sums = pl.pallas_call(
+    small = pltpu.CompilerParams(vmem_limit_bytes=16 * 2**20)
+
+    half = HD // 2
+    low = lax.axis_index(HEAD[1])
+    rows_of = out_weight.reshape(heads, 2, half, features)
+    wanted = lax.dynamic_index_in_dim(rows_of, 1 - low, 1, keepdims=False)
+    their_rows = lax.all_gather(wanted.reshape(heads * half, features), HEAD[1])
+
+    row = pl.pallas_call(
+        pack_kernel,
+        out_shape=jax.ShapeDtypeStruct((split, 16, HD), bf16),
+        in_specs=[VMEM],
+        out_specs=VMEM,
+        compiler_params=small,
+        name="pack",
+    )(queries)
+    row = lax.all_to_all(row, HEAD, 0, 0, tiled=True)
+    partial = pl.pallas_call(
         attend_kernel,
-        out_shape=(
-            jax.ShapeDtypeStruct((docs, features), f32),
-            jax.ShapeDtypeStruct((docs, seq_len), f32),
-        ),
+        out_shape=jax.ShapeDtypeStruct((docs, features + seq_len), f32),
         in_specs=[SMEM] + [VMEM] * 4,
-        out_specs=(VMEM, VMEM),
+        out_specs=VMEM,
         scratch_shapes=[pltpu.VMEM((seq_len, HD), f32)],
         compiler_params=big,
         name="attend",
     )(lengths, attn_queries, keys, values, out_weight)
-    row, emb, sums = lax.optimization_barrier((row, emb, sums))
-    rows = jnp.broadcast_to(row.reshape(1, 2, features // 2), (others, 2, features // 2))
+    row, partial = lax.optimization_barrier((row, partial))
+    rows = pl.pallas_call(
+        copies_kernel,
+        out_shape=jax.ShapeDtypeStruct((others, 2, features // 2), bf16),
+        in_specs=[VMEM],
+        out_specs=VMEM,
+        compiler_params=small,
+        name="copies",
+    )(row)
     every = lax.all_to_all(rows, DP[:3], 0, 0, tiled=True).reshape(lanes, features // 2)
-    pos = jnp.repeat(positives.reshape(others, cores * split).T, 2, axis=1)
-
-    whole = emb
-    for apart in range(1, split):
-        whole = whole + lax.ppermute(emb, "head", [(i, i ^ apart) for i in range(split)])
-    their_sums = lax.ppermute(sums, "head", [(i, i ^ 1) for i in range(split)])
+    pos = positives.reshape(others, cores * split)
+
+    theirs = lax.ppermute(partial, HEAD, [(i, i ^ 1) for i in range(split)])
+    emb = partial[:, :features]
+    whole = emb + theirs[:, :features]
+    for apart in range(2, split):
+        whole = whole + lax.ppermute(emb, HEAD, [(i, i ^ apart) for i in range(split)])
     pair = lax.all_gather(whole, DP[3])
 
-    stats, logits, unit, rnorm = pl.pallas_call(
+    stats, logits, chosen, unit, rnorm = pl.pallas_call(
         logits_kernel,
         out_shape=(
             jax.ShapeDtypeStruct((others, 2, lanes), f32),
+            jax.ShapeDtypeStruct((cores * docs, lanes), f32),
             jax.ShapeDtypeStruct((cores * docs, lanes), f32),
             jax.ShapeDtypeStruct((cores * docs, features), f32),
             jax.ShapeDtypeStruct((cores * docs, HD), f32),
         ),
         in_specs=[VMEM] * 3,
-        out_specs=(VMEM,) * 4,
+        out_specs=(VMEM,) * 5,
+        compiler_params=small,
         name="logits",
     )(pair, every, pos)
     stats = lax.all_to_all(stats, DP[:3], 0, 0, tiled=True)
+    stats, their_rows = lax.optimization_barrier((stats, their_rows))
 
     grads = pl.pallas_call(
         slopes_kernel,
         out_shape=jax.ShapeDtypeStruct((cores * split, docs, features + lanes), bf16),
         in_specs=[VMEM] * 6,
         out_specs=VMEM,
+        compiler_params=small,
         name="slopes",
-    )(stats, logits, unit, rnorm, every, pos)
-    grads = lax.all_to_all(grads, (DP[3], "head"), 0, 0, tiled=True)
-
-    kept, sent, loss = pl.pallas_call(
-        context_kernel,
+    )(stats, logits, chosen, unit, rnorm, every)
+    grads = lax.all_to_all(grads, (DP[3], *HEAD), 0, 0, tiled=True)
+
+    d_values, loss = pl.pallas_call(
+        values_kernel,
         out_shape=(
-            jax.ShapeDtypeStruct((heads * docs, HD // 2), bf16),
-            jax.ShapeDtypeStruct((heads * docs, HD // 2), bf16),
+            jax.ShapeDtypeStruct((half, seq_len), bf16),
             jax.ShapeDtypeStruct((1, 1), f32),
         ),
-        in_specs=[SMEM] + [VMEM] * 2,
-        out_specs=(VMEM,) * 3,
-        name="context",
-    )(lengths, grads, out_weight)
-    got = lax.ppermute(sent, "head", [(i, i ^ 1) for i in range(split)])
-
-    d_values = pl.pallas_call(
-        values_kernel,
-        out_shape=jax.ShapeDtypeStruct((HD // 2, seq_len), bf16),
-        in_specs=[SMEM] + [VMEM] * 4,
-        out_specs=VMEM,
+        in_specs=[SMEM] + [VMEM] * 5,
+        out_specs=(VMEM, VMEM),
+        compiler_params=small,
         name="slopes_of_values",
-    )(lengths, sums, their_sums, kept, got)
+    )(lengths, grads, out_weight, their_rows, partial, theirs)
     return d_values.T, loss.reshape(())
 
 
 def solution(mesh):
     shape = (4, 8, 2, 2) if mesh.devices.size == 512 else (1, mesh.devices.size // 16, 2, 2)
-    torus = Mesh(mesh.devices.reshape(*shape, mesh.shape["head"]), (*DP, "head"))
+    head = mesh.shape["head"]
+    torus = Mesh(mesh.devices.reshape(*shape, head // 2, 2), (*DP, *HEAD))
     placed = (
-        P(DP, "head"),
+        P(DP, HEAD),
         P(DP, None),
         P(DP, None),
-        P("head", None),
+        P(HEAD, None),
         P(DP, None),
-        P(DP, "head"),
+        P(DP, HEAD),
         P(),
     )
     return jax.shard_map(
-        per_device, mesh=torus, in_specs=placed, out_specs=(P(DP, "head"), P()), check_vma=False
-    )
+        per_device, mesh=torus, in_specs=placed, out_specs=(P(DP, HEAD), P()), check_vma=False
+    )

time: 106 us -> 107 us (level)
  blocking collectives: 24.6 us -> 39.2 us
  between operations: 0.77 us -> 14.2 us
  starting transfers between devices: 44.4 us -> 32.1 us
  waiting for transfers between devices: 15.9 us -> 8.64 us
  Pallas kernels: 12.2 us -> 7.72 us
  other arithmetic: 2.19 us -> 0.9 us
    all_to_all x0 -> x1, blocking collectives: none -> 14.8 us  [per_device(): grads = lax.all_to_all(grads, (DP[3], *HEAD), 0, 0, tiled=True)]
    all_to_all x2 -> x1, starting transfers between devices: 12.6 us -> 5.42 us  [per_device(): row = lax.all_to_all(row, HEAD, 0, 0, tiled=True)]
    ppermute x5 -> x3, starting transfers between devices: 14.4 us -> 9.25 us  [the longest x2 6.52 us: per_device(): lax.ppermute(emb, HEAD, [(i, i ^ apart) for i in range(split)])]
    all_to_all x2 -> x1, waiting for transfers between devices: 5.33 us -> 0.63 us  [per_device(): row = lax.all_to_all(row, HEAD, 0, 0, tiled=True)]
    ppermute x5 -> x3, waiting for transfers between devices: 2.65 us -> 0.01 us  [the longest x2 0.01 us: per_device(): lax.ppermute(emb, HEAD, [(i, i ^ apart) for i in range(split)])]
    dynamic_slice x0 -> x1, local copies, waits for them, and re-layouts: none -> 1.95 us  [per_device(): wanted = lax.dynamic_index_in_dim(rows_of, 1 - low, 1, keepdims=False)]
    pallas_call x1, Pallas kernels: 2.07 us -> 0.35 us  [per_device(): pl.pallas_call(slopes_kernel, out_shape=jax.ShapeDtypeStruct((cores * spl...]
    pallas_call x1, Pallas kernels: 2.01 us -> 0.4 us  [per_device(): pl.pallas_call(logits_kernel, out_shape=(jax.ShapeDtypeStruct((others, 2,...]
  transfers between devices with their start and end apart: 8 -> 6, of which waited for: 4 -> 2; matrix products, arithmetic and copies ran while one was open for 2% -> 2% of each run, Pallas kernels for 6% -> 5%
where the time goes in v3:
time: 107 us
  blocking collectives  39.2 us (37%)
  starting transfers between devices  32.1 us (30%)
  between operations  14.2 us (13%)
  waiting for transfers between devices  8.64 us (8%)
  Pallas kernels  7.72 us (7%)
  local copies, waits for them, and re-layouts  4.22 us (4%)
    all_to_all x1, blocking collectives, per_device(): stats = lax.all_to_all(stats, DP[:3], 0, 0, tiled=True)  19.9 us
    all_to_all x1, starting transfers between devices, per_device(): lax.all_to_all(rows, DP[:3], 0, 0, tiled=True).reshape(lanes, features // 2)  17.4 us
    all_to_all x1, blocking collectives, per_device(): grads = lax.all_to_all(grads, (DP[3], *HEAD), 0, 0, tiled=True)  14.8 us
    all_to_all x1, waiting for transfers between devices, per_device(): lax.all_to_all(rows, DP[:3], 0, 0, tiled=True).reshape(lanes, features // 2)  7.98 us
    ppermute x2, starting transfers between devices, per_device(): lax.ppermute(emb, HEAD, [(i, i ^ apart) for i in range(split)])  6.52 us
    all_to_all x1, starting transfers between devices, per_device(): row = lax.all_to_all(row, HEAD, 0, 0, tiled=True)  5.42 us
    all_gather x1, blocking collectives, per_device(): pair = lax.all_gather(whole, DP[3])  4.47 us
    pallas_call x1, Pallas kernels, per_device(): pl.pallas_call(attend_kernel, out_shape=jax.ShapeDtypeStruct((docs, featu...  3.83 us
  transfers between devices with their start and end apart: 6, of which 2 were waited for; matrix products, arithmetic and copies ran while one was open for 2% of the time, Pallas kernels for 5%

profile of v3, /device:TPU:1, one launch (start us, length us, event | category | flops | bytes accessed | tf_op | source)
XLA Modules:
  0.0 106.9 jit_solution(13294406172309257234)
XLA Ops:
  7.2 0.0 all-gather.3.cloned.1.call-start
  7.2 1.9 %constant_dynamic-slice_fusion = bf16[3,1,64,1536]{3,2,1,0:T(8,128)(2,1)} fusion(bf16[3,2,64,1536]{3,2,1,0:T(8,128)(2,1)} %bitcast.7, s32[]{:T(128)S(6)} %select_n.4), kind=kLoop, calls=%fused_computation.3 | loop fusion | bytes 1179652 | tf_op jit(solution)/shard_map/jit(dynamic_index_in_dim)/dynamic_slice | solution.py:268
  9.2 0.0 all-gather.3.cloned.1.call-update
  9.2 0.6 pack.1
  9.8 5.4 %all-to-all-start = ((bf16[4,16,128]{2,1,0:T(8,128)(2,1)}), bf16[4,16,128]{2,1,0:T(8,128)(2,1)S(1)}, u32[]{:S(2)}, u32[]{:S(2)}) async-start(bf16[4,16,128]{2,1,0:T(8,128)(2,1)} %pack.1), calls=%async_computation | async-start | bytes 32768 | tf_op jit(solution)/shard_map/all_to_all | solution.py:279
  15.2 3.8 %attend.1.my_sums_ref = f32[8,2048]{1,0:T(8,128)} custom-call(s32[1,8]{1,0:T(1,128)} %lens_ref.3, bf16[512,384]{1,0:T(8,128)(2,1)} %q_ref.3, bf16[512,256]{1,0:T(8,128)(2,1)} %k_ref.1, bf16[512,256]{1,0:T(8,128)(2,1)} %v_ref.1, bf16[384,1536]{1,0:T(8,128)(2,1)} %my_rows_ref.1), custom_call_target="tpu_custom_call" | custom-call | tf_op jit(solution)/shard_map/attend/pallas_call | solution.py:280
  19.1 0.6 all-to-all-done.row_ref
  19.7 2.7 %collective-permute-start = (f32[8,2048]{1,0:T(8,128)}, f32[8,2048]{1,0:T(8,128)S(1)}, u32[]{:S(2)}, u32[]{:S(2)}) collective-permute-start(f32[8,2048]{1,0:T(8,128)} %attend.1.my_sums_ref), channel_id=1, source_target_pairs={{0,1},{1,0},{2,3},{3,2},{4,5},{5,4},{6,7},{7,6},{8,9},{9,8},{10,11... | collective-permute-start | bytes 196616 | tf_op jit(solution)/shard_map/ppermute | solution.py:301
  22.4 0.8 slice.6
  23.3 4.0 %collective-permute-start.1 = (f32[8,1536]{1,0:T(8,128)S(1)}, f32[8,1536]{1,0:T(8,128)S(1)}, u32[]{:S(2)}, u32[]{:S(2)}) collective-permute-start(f32[8,1536]{1,0:T(8,128)S(1)} %slice.6), channel_id=1, source_target_pairs={{0,2},{1,3},{2,0},{3,1},{4,6},{5,7},{6,4},{7,5},{8,10},{9,11},{10,... | collective-permute-start | bytes 147464 | tf_op jit(solution)/shard_map/ppermute | solution.py:305
  27.2 2.5 %collective-permute-start.2 = (f32[8,1536]{1,0:T(8,128)S(1)}, f32[8,1536]{1,0:T(8,128)S(1)}, u32[]{:S(2)}, u32[]{:S(2)}) collective-permute-start(f32[8,1536]{1,0:T(8,128)S(1)} %slice.6), channel_id=1, source_target_pairs={{0,3},{1,2},{2,1},{3,0},{4,7},{5,6},{6,5},{7,4},{8,11},{9,10},{10,... | collective-permute-start | bytes 147464 | tf_op jit(solution)/shard_map/ppermute | solution.py:305
  29.8 0.1 reshape.18.pos_ref
  29.9 0.7 copies.1
  30.6 17.4 %all-to-all-start.1 = ((bf16[64,2,768]{2,1,0:T(2,128)(2,1)}), bf16[64,2,768]{2,1,0:T(2,128)(2,1)S(1)}, u32[]{:S(2)}, u32[]{:S(2)}) async-start(bf16[64,2,768]{2,1,0:T(2,128)(2,1)} %copies.1), calls=%async_computation.1 | async-start | bytes 393216 | tf_op jit(solution)/shard_map/all_to_all | solution.py:298
  48.1 0.9 fusion.1
  49.0 4.5 %all-gather = f32[16,1536]{1,0:T(8,128)S(1)} all-gather(f32[8,1536]{1,0:T(8,128)S(1)} %fusion.1), channel_id=2, replica_groups=mesh['dp_0'=4,'dp_1'=8,'dp_2'=2,'dp_3'=2,'head_0'=2,'head_1'=2] {'dp_3'}, dimensions={0}, use_global_device_ids=true | all-gather | bytes 147456 | tf_op jit(solution)/shard_map/all_gather | solution.py:306
  53.5 8.0 %all-to-all-done.1 = bf16[64,2,768]{2,1,0:T(2,128)(2,1)S(1)} async-done(((bf16[64,2,768]{2,1,0:T(2,128)(2,1)}), bf16[64,2,768]{2,1,0:T(2,128)(2,1)S(1)}, u32[]{:S(2)}, u32[]{:S(2)}) %all-to-all-start.1) | async-done | bytes 196640 | tf_op jit(solution)/shard_map/all_to_all | solution.py:298
  61.4 0.1 reshape.17.q_ref
  61.5 0.4 logits.1
  61.9 19.9 %all_to_all.20.stats_ref = f32[64,2,128]{2,1,0:T(2,128)S(1)} all-to-all(f32[64,2,128]{2,1,0:T(2,128)S(1)} %get-tuple-element.15), channel_id=1, replica_groups=mesh['dp_0'=4,'dp_1'=8,'dp_2'=2,'dp_3'=2,'head_0'=2,'head_1'=2] {'dp_0',..., dimensions={0} | all-to-all | bytes 131072 | tf_op jit(solution)/shard_map/all_to_all | solution.py:322
  81.8 0.4 slopes.1
  82.2 14.8 %all_to_all.21.grads_ref = bf16[8,8,1664]{2,1,0:T(8,128)(2,1)S(1)} all-to-all(bf16[8,8,1664]{2,1,0:T(8,128)(2,1)S(1)} %slopes.1), channel_id=1, replica_groups=mesh['dp_0'=4,'dp_1'=8,'dp_2'=2,'dp_3'=2,'head_0'=2,'head_1'=2] {'dp_3',..., dimensions={0} | all-to-all | bytes 425984 | tf_op jit(solution)/shard_map/all_to_all | solution.py:333
  97.0 1.3 %copy-done.1 = bf16[2,192,1536]{2,1,0:T(8,128)(2,1)S(1)} copy-done((bf16[2,192,1536]{2,1,0:T(8,128)(2,1)S(1)}, bf16[2,192,1536]{2,1,0:T(8,128)(2,1)}, u32[]{:S(2)}) %copy-start.1) | copy-done | bytes 1179672
  98.3 1.8 %slopes_of_values.1 = (bf16[64,512]{1,0:T(8,128)(2,1)}, f32[1,1]{1,0:T(1,128)}) custom-call(s32[1,8]{1,0:T(1,128)S(1)} %copy-done.4, bf16[8,8,1664]{2,1,0:T(8,128)(2,1)S(1)} %all_to_all.21.grads_ref, bf16[384,1536]{1,0:T(8,128)(2,1)S(1)} %copy-done, bf16[2,192,1536]{2,1,0:T(8,128)(2,1)S(1)} %copy-done.1, f32[8,2048]{1,0:T(8,128)S(1)} %copy-done.2, ...), custom_call_target="tpu_custom_call" | custom-call | tf_op jit(solution)/shard_map/slopes_of_values/pallas_call | solution.py:335
  (15 shorter events, 0.0 us)
Async XLA Ops:
  7.2 2.0 %copy-start.3 = (bf16[4,384]{1,0:T(4,128)(2,1)S(1)}, bf16[4,384]{1,0:T(4,128)(2,1)}, u32[]{:S(2)}) copy-start(bf16[4,384]{1,0:T(4,128)(2,1)} %q_ref.2) | copy-start | bytes 9220
  7.2 74.6 %all-gather.3.cloned.1.call-start = ((), (), s32[]{:S(2)}) async-start(), calls=%async_computation.4 | async-start | bytes 1769472 | tf_op jit(solution)/shard_map/all_gather | solution.py:269
  9.2 20.6 %copy-start.5 = (s32[512]{0:T(512)S(1)}, s32[512]{0:T(512)}, u32[]{:S(2)}) copy-start(s32[512]{0:T(512)} %param.13) | copy-start | bytes 6148
  9.8 9.9 %all-to-all-start = ((bf16[4,16,128]{2,1,0:T(8,128)(2,1)}), bf16[4,16,128]{2,1,0:T(8,128)(2,1)S(1)}, u32[]{:S(2)}, u32[]{:S(2)}) async-start(bf16[4,16,128]{2,1,0:T(8,128)(2,1)} %pack.1), calls=%async_computation | async-start | bytes 32768 | tf_op jit(solution)/shard_map/all_to_all | solution.py:279
  19.7 28.4 %collective-permute-start = (f32[8,2048]{1,0:T(8,128)}, f32[8,2048]{1,0:T(8,128)S(1)}, u32[]{:S(2)}, u32[]{:S(2)}) collective-permute-start(f32[8,2048]{1,0:T(8,128)} %attend.1.my_sums_ref), channel_id=1, source_target_pairs={{0,1},{1,0},{2,3},{3,2},{4,5},{5,4},{6,7},{7,6},{8,9},{9,8},{10,11... | collective-permute-start | bytes 196616 | tf_op jit(solution)/shard_map/ppermute | solution.py:301
  23.3 24.8 %collective-permute-start.1 = (f32[8,1536]{1,0:T(8,128)S(1)}, f32[8,1536]{1,0:T(8,128)S(1)}, u32[]{:S(2)}, u32[]{:S(2)}) collective-permute-start(f32[8,1536]{1,0:T(8,128)S(1)} %slice.6), channel_id=1, source_target_pairs={{0,2},{1,3},{2,0},{3,1},{4,6},{5,7},{6,4},{7,5},{8,10},{9,11},{10,... | collective-permute-start | bytes 147464 | tf_op jit(solution)/shard_map/ppermute | solution.py:305
  27.2 20.8 %collective-permute-start.2 = (f32[8,1536]{1,0:T(8,128)S(1)}, f32[8,1536]{1,0:T(8,128)S(1)}, u32[]{:S(2)}, u32[]{:S(2)}) collective-permute-start(f32[8,1536]{1,0:T(8,128)S(1)} %slice.6), channel_id=1, source_target_pairs={{0,3},{1,2},{2,1},{3,0},{4,7},{5,6},{6,5},{7,4},{8,11},{9,10},{10,... | collective-permute-start | bytes 147464 | tf_op jit(solution)/shard_map/ppermute | solution.py:305
  30.6 30.8 %all-to-all-start.1 = ((bf16[64,2,768]{2,1,0:T(2,128)(2,1)}), bf16[64,2,768]{2,1,0:T(2,128)(2,1)S(1)}, u32[]{:S(2)}, u32[]{:S(2)}) async-start(bf16[64,2,768]{2,1,0:T(2,128)(2,1)} %copies.1), calls=%async_computation.1 | async-start | bytes 393216 | tf_op jit(solution)/shard_map/all_to_all | solution.py:298
  48.0 49.0 %copy-start = (bf16[384,1536]{1,0:T(8,128)(2,1)S(1)}, bf16[384,1536]{1,0:T(8,128)(2,1)}, u32[]{:S(2)}) copy-start(bf16[384,1536]{1,0:T(8,128)(2,1)} %my_rows_ref.1) | copy-start | bytes 3538948
  48.0 49.0 %copy-start.2 = (f32[8,2048]{1,0:T(8,128)S(1)}, f32[8,2048]{1,0:T(8,128)}, u32[]{:S(2)}) copy-start(f32[8,2048]{1,0:T(8,128)} %attend.1.my_sums_ref) | copy-start | bytes 196612
  48.0 48.9 %copy-start.4 = (s32[1,8]{1,0:T(1,128)S(1)}, s32[1,8]{1,0:T(1,128)}, u32[]{:S(2)}) copy-start(s32[1,8]{1,0:T(1,128)} %lens_ref.3) | copy-start | bytes 100
  97.0 1.3 %copy-start.1 = (bf16[2,192,1536]{2,1,0:T(8,128)(2,1)S(1)}, bf16[2,192,1536]{2,1,0:T(8,128)(2,1)}, u32[]{:S(2)}) copy-start(bf16[2,192,1536]{2,1,0:T(8,128)(2,1)} %all-gather.3.cloned.1.call-done.their_rows_ref) | copy-start | bytes 3538948
Sparse Core Ops, SparseCore 0:
  10.1 37.9 all-gather.2

commit v4 on v3

--- a/solution.py
+++ b/solution.py
@@ -22,6 +22,19 @@
 TN = (((0,), (0,)), ((), ()))
 VMEM = pl.BlockSpec(memory_space=pltpu.VMEM)
 SMEM = pl.BlockSpec(memory_space=pltpu.SMEM)
+
+
+def query_class():
+    return lax.axis_index(HEAD) ^ (2 * lax.axis_index(DP[2]))
+
+
+def class_groups():
+    split, uppers = lax.axis_size(HEAD), lax.axis_size(DP[2])
+    blocks = lax.axis_size(DP[:2])
+    return [
+        [(b * uppers + u) * split + (k ^ (2 * u)) for b in range(blocks) for u in range(uppers)]
+        for k in range(split)
+    ]
 
 
 def three_terms(value):
@@ -64,7 +77,10 @@
     return column.astype(jnp.float32)
 
 
-def attend_kernel(lens_ref, q_ref, k_ref, v_ref, w_ref, out_ref, total):
+def attend_kernel(
+    lens_ref, q_ref, k_ref, v_ref, w_ref, queries_ref, *out_refs
+):
+    *sent_refs, rows_ref, total = out_refs
     seq_len, width = q_ref.shape
     heads = width // HD
     docs = lens_ref.shape[1]
@@ -104,30 +120,44 @@
         [sums[h * docs : (h + 1) * docs] for h in range(heads)], axis=1
     ) / lens_column(lens_ref, docs)
     emb = exact_dot(pooled, w_ref[...], (((1,), (0,)), ((), ())))
-    out_ref[:, : emb.shape[1]] = emb
-    out_ref[:, emb.shape[1] :] = by_head[:docs, :]
-
-
-def pack_kernel(q_ref, out_ref):
-    chunks = q_ref.shape[1] // HD
-    rows = q_ref[...].astype(jnp.float32)
-    rest = jnp.zeros((out_ref.shape[1] - chunks, HD), jnp.float32)
-    for k in range(q_ref.shape[0]):
-        parts = [rows[k : k + 1, c * HD : (c + 1) * HD] for c in range(chunks)]
-        out_ref[k] = jnp.concatenate([*parts, rest], axis=0).astype(jnp.bfloat16)
-
-
-def copies_kernel(row_ref, out_ref):
-    features = 2 * out_ref.shape[2]
-    chunks = features // row_ref.shape[0] // HD
+    features = emb.shape[1]
+    queries = queries_ref[...].astype(jnp.float32)
+    place = lax.broadcasted_iota(jnp.int32, queries.shape, 0)
+    rest = jnp.zeros((docs - heads - 1, seq_len), jnp.float32)
+    tail = jnp.zeros((1, seq_len - width), jnp.float32)
+    for apart, sent_ref in enumerate(sent_refs):
+        row = jnp.where(place == (query_class() ^ apart), queries, 0.0)
+        row = jnp.concatenate([jnp.sum(row, axis=0, keepdims=True), tail], axis=1)
+        sent_ref[:, :features] = emb
+        sent_ref[:, features:] = jnp.concatenate([by_head[:heads], row, rest], axis=0)
+    half = HD // 2
+    for h in range(heads):
+        wanted = pl.ds(pl.multiple_of(h * HD + (1 - lax.axis_index(HEAD[1])) * half, half), half)
+        rows_ref[h * half : (h + 1) * half, :] = w_ref[wanted, :]
+
+
+def copies_kernel(*refs):
+    *partial_refs, out_ref, whole_ref = refs
+    docs, features = whole_ref.shape
+    split = len(partial_refs)
+    width = features // split
+    row = HEADS // split
+    me = lax.axis_index(HEAD)
+    slices = [ref[row : row + 1, features : features + width] for ref in partial_refs]
     parts = []
-    for k in range(row_ref.shape[0]):
-        block = row_ref[k].astype(jnp.float32)
-        parts += [block[c : c + 1, :] for c in range(chunks)]
-    middle = len(parts) // 2
+    for owner in range(split):
+        part = jnp.zeros_like(slices[0])
+        for apart in range(split):
+            part = jnp.where(me == owner ^ apart, slices[apart], part)
+        parts.append(part)
+    middle = split // 2
     halves = [jnp.concatenate(parts[:middle], axis=1), jnp.concatenate(parts[middle:], axis=1)]
     both = jnp.concatenate(halves, axis=0).astype(jnp.bfloat16)
     out_ref[...] = jnp.broadcast_to(both[None], out_ref.shape)
+    whole = partial_refs[0][:, :features]
+    for ref in partial_refs[1:]:
+        whole = whole + ref[:, :features]
+    whole_ref[...] = whole
 
 
 def pair_logits(unit, q_ref):
@@ -144,7 +174,9 @@
 
 def positive_mask(pos_ref, docs):
     count, classes = pos_ref.shape
-    mine = lax.broadcasted_iota(jnp.int32, (count, classes), 1) == lax.axis_index((DP[3], *HEAD))
+    mine = lax.broadcasted_iota(jnp.int32, (count, classes), 1) == (
+        lax.axis_size(HEAD) * lax.axis_index(DP[3]) + query_class()
+    )
     lane = lax.broadcasted_iota(jnp.int32, (count, 2 * count), 1)
     row = lax.broadcasted_iota(jnp.int32, (count, 2 * count), 0)
     spread = (lane // 2 == row).astype(jnp.bfloat16)
@@ -232,7 +264,7 @@
         rows = my_rows_ref[pl.ds(pl.multiple_of(h * HD + low * half, half), half), :]
         slopes.append(lax.dot_general(terms, rows, NT, preferred_element_type=jnp.float32))
     for h in range(heads):
-        rows = their_rows_ref[1 - low, h * half : (h + 1) * half, :]
+        rows = their_rows_ref[h * half : (h + 1) * half, :]
         slopes.append(lax.dot_general(terms, rows, NT, preferred_element_type=jnp.float32))
     slopes = [(of_three(part) * factor).astype(jnp.bfloat16) for part in slopes]
     seg, _ = document_of(lens_ref, docs, (1, seq_len), 1)
@@ -263,46 +295,37 @@
     small = pltpu.CompilerParams(vmem_limit_bytes=16 * 2**20)
 
     half = HD // 2
-    low = lax.axis_index(HEAD[1])
-    rows_of = out_weight.reshape(heads, 2, half, features)
-    wanted = lax.dynamic_index_in_dim(rows_of, 1 - low, 1, keepdims=False)
-    their_rows = lax.all_gather(wanted.reshape(heads * half, features), HEAD[1])
-
-    row = pl.pallas_call(
-        pack_kernel,
-        out_shape=jax.ShapeDtypeStruct((split, 16, HD), bf16),
-        in_specs=[VMEM],
-        out_specs=VMEM,
-        compiler_params=small,
-        name="pack",
-    )(queries)
-    row = lax.all_to_all(row, HEAD, 0, 0, tiled=True)
-    partial = pl.pallas_call(
+    line = (*DP[:3], *HEAD)
+    groups = class_groups()
+    pairs = [[(i, i ^ apart) for i in range(split)] for apart in range(split)]
+
+    *partials, wanted = pl.pallas_call(
         attend_kernel,
-        out_shape=jax.ShapeDtypeStruct((docs, features + seq_len), f32),
-        in_specs=[SMEM] + [VMEM] * 4,
-        out_specs=VMEM,
+        out_shape=(jax.ShapeDtypeStruct((docs, features + seq_len), f32),) * split
+        + (jax.ShapeDtypeStruct((heads * half, features), bf16),),
+        in_specs=[SMEM] + [VMEM] * 5,
+        out_specs=(VMEM,) * (split + 1),
         scratch_shapes=[pltpu.VMEM((seq_len, HD), f32)],
         compiler_params=big,
         name="attend",
-    )(lengths, attn_queries, keys, values, out_weight)
-    row, partial = lax.optimization_barrier((row, partial))
-    rows = pl.pallas_call(
+    )(lengths, attn_queries, keys, values, out_weight, queries)
+    own = partials[0]
+    got = [lax.ppermute(partials[apart], HEAD, pairs[apart]) for apart in range(1, split)]
+    their_rows = lax.ppermute(wanted, HEAD, pairs[1])
+    rows, whole = pl.pallas_call(
         copies_kernel,
-        out_shape=jax.ShapeDtypeStruct((others, 2, features // 2), bf16),
-        in_specs=[VMEM],
-        out_specs=VMEM,
+        out_shape=(
+            jax.ShapeDtypeStruct((others, 2, features // 2), bf16),
+            jax.ShapeDtypeStruct((docs, features), f32),
+        ),
+        in_specs=[VMEM] * split,
+        out_specs=(VMEM, VMEM),
         compiler_params=small,
         name="copies",
-    )(row)
-    every = lax.all_to_all(rows, DP[:3], 0, 0, tiled=True).reshape(lanes, features // 2)
+    )(own, *got)
+    every = lax.all_to_all(rows, line, 0, 0, axis_index_groups=groups, tiled=True)
+    every = every.reshape(lanes, features // 2)
     pos = positives.reshape(others, cores * split)
-
-    theirs = lax.ppermute(partial, HEAD, [(i, i ^ 1) for i in range(split)])
-    emb = partial[:, :features]
-    whole = emb + theirs[:, :features]
-    for apart in range(2, split):
-        whole = whole + lax.ppermute(emb, HEAD, [(i, i ^ apart) for i in range(split)])
     pair = lax.all_gather(whole, DP[3])
 
     stats, logits, chosen, unit, rnorm = pl.pallas_call(
@@ -319,8 +342,7 @@
         compiler_params=small,
         name="logits",
     )(pair, every, pos)
-    stats = lax.all_to_all(stats, DP[:3], 0, 0, tiled=True)
-    stats, their_rows = lax.optimization_barrier((stats, their_rows))
+    stats = lax.all_to_all(stats, line, 0, 0, axis_index_groups=groups, tiled=True)
 
     grads = pl.pallas_call(
         slopes_kernel,
@@ -342,7 +364,7 @@
         out_specs=(VMEM, VMEM),
         compiler_params=small,
         name="slopes_of_values",
-    )(lengths, grads, out_weight, their_rows, partial, theirs)
+    )(lengths, grads, out_weight, their_rows, own, got[0])
     return d_values.T, loss.reshape(())
 
 

time: 107 us -> 86.3 us (0.81)
  between operations: 14.2 us -> 0.73 us
  blocking collectives: 39.2 us -> 26.4 us
  waiting for transfers between devices: 8.64 us -> 15.4 us
  local copies, waits for them, and re-layouts: 4.22 us -> 1.01 us
  starting transfers between devices: 32.1 us -> 34.2 us
    all_to_all x2 -> x1, blocking collectives: 34.7 us -> 22 us  [per_device(): lax.all_to_all(stats, line, 0, 0, axis_index_groups=groups, tiled=True)]
    ppermute x3 -> x4, starting transfers between devices: 9.25 us -> 15 us  [the longest x3 10.2 us: per_device(): lax.ppermute(partials[apart], HEAD, pairs[apart])]
    ppermute x3 -> x4, waiting for transfers between devices: 0.01 us -> 5.15 us  [the longest x3 5.15 us: per_device(): lax.ppermute(partials[apart], HEAD, pairs[apart])]
    all_to_all x2, starting transfers between devices: 22.8 us -> 19.2 us  [the longest x1 14.1 us: per_device(): lax.all_to_all(rows, line, 0, 0, axis_index_groups=groups, tiled=True)]
    dynamic_slice x1 -> x0, local copies, waits for them, and re-layouts: 1.95 us -> none  [per_device(): wanted = lax.dynamic_index_in_dim(rows_of, 1 - low, 1, keepdims=False)]
    all_to_all x2, waiting for transfers between devices: 8.61 us -> 10.3 us  [the longest x1 7.99 us: per_device(): grads = lax.all_to_all(grads, (DP[3], *HEAD), 0, 0, tiled=True)]
    pallas_call x3 -> x2, Pallas kernels: 5.15 us -> 4.77 us  [the longest x1 4.05 us: per_device(): pl.pallas_call(attend_kernel, out_shape=(jax.ShapeDtypeStruct((docs, feat...]
  transfers between devices with their start and end apart: 6 -> 6, of which waited for: 2 -> 4; matrix products, arithmetic and copies ran while one was open for 2% -> 0% of each run, Pallas kernels for 5% -> 2%
where the time goes in v4:
time: 86.3 us; the launch traced here: 85.8 us
  starting transfers between devices  34.2 us (40%)
  blocking collectives  26.4 us (31%)
  waiting for transfers between devices  15.4 us (18%)
  Pallas kernels  8.03 us (9%)
  local copies, waits for them, and re-layouts  1.01 us (1%)
    all_to_all x1, blocking collectives, per_device(): lax.all_to_all(stats, line, 0, 0, axis_index_groups=groups, tiled=True)  22 us
    all_to_all x1, starting transfers between devices, per_device(): lax.all_to_all(rows, line, 0, 0, axis_index_groups=groups, tiled=True)  14.1 us
    ppermute x3, starting transfers between devices, per_device(): lax.ppermute(partials[apart], HEAD, pairs[apart])  10.2 us
    all_to_all x1, waiting for transfers between devices, per_device(): grads = lax.all_to_all(grads, (DP[3], *HEAD), 0, 0, tiled=True)  7.99 us
    ppermute x3, waiting for transfers between devices, per_device(): lax.ppermute(partials[apart], HEAD, pairs[apart])  5.15 us
    all_to_all x1, starting transfers between devices, per_device(): grads = lax.all_to_all(grads, (DP[3], *HEAD), 0, 0, tiled=True)  5.09 us
    ppermute x1, starting transfers between devices, per_device(): their_rows = lax.ppermute(wanted, HEAD, pairs[1])  4.84 us
    all_gather x1, blocking collectives, per_device(): pair = lax.all_gather(whole, DP[3])  4.4 us
  transfers between devices with their start and end apart: 6, of which 4 were waited for; matrix products, arithmetic and copies ran while one was open for 0% of the time, Pallas kernels for 2%

profile of v4, /device:TPU:1, one launch (start us, length us, event | category | flops | bytes accessed | tf_op | source)
XLA Modules:
  0.0 85.8 jit_solution(18012031954646996300)
XLA Ops:
  0.6 0.0 copy-start.4
  0.6 4.1 %attend.1 = (f32[8,2048]{1,0:T(8,128)}, f32[8,2048]{1,0:T(8,128)}, f32[8,2048]{1,0:T(8,128)}, f32[8,2048]{1,0:T(8,128)}, bf16[192,1536]{1,0:T(8,128)(2,1)}) custom-call(s32[1,8]{1,0:T(1,128)} %lens_ref.3, bf16[512,384]{1,0:T(8,128)(2,1)} %q_ref.1, bf16[512,256]{1,0:T(8,128)(2,1)} %k_ref.1, bf16[512,256]{1,0:T(8,128)(2,1)} %v_ref.1, ...), custom_call_target="tpu_custom_call" | custom-call | tf_op jit(solution)/shard_map/attend/pallas_call | solution.py:302
  4.7 4.0 %collective-permute-start = (f32[8,2048]{1,0:T(8,128)}, f32[8,2048]{1,0:T(8,128)S(1)}, u32[]{:S(2)}, u32[]{:S(2)}) collective-permute-start(f32[8,2048]{1,0:T(8,128)} %get-tuple-element.17), channel_id=1, source_target_pairs={{0,1},{1,0},{2,3},{3,2},{4,5},{5,4},{6,7},{7,6},{8,9},{9,8},{10,11... | collective-permute-start | bytes 196616 | tf_op jit(solution)/shard_map/ppermute | solution.py:313
  8.7 4.2 %collective-permute-start.1 = (f32[8,2048]{1,0:T(8,128)}, f32[8,2048]{1,0:T(8,128)S(1)}, u32[]{:S(2)}, u32[]{:S(2)}) collective-permute-start(f32[8,2048]{1,0:T(8,128)} %get-tuple-element.18), channel_id=1, source_target_pairs={{0,2},{1,3},{2,0},{3,1},{4,6},{5,7},{6,4},{7,5},{8,10},{9,11},{10,... | collective-permute-start | bytes 196616 | tf_op jit(solution)/shard_map/ppermute | solution.py:313
  13.0 1.9 %collective-permute-start.2 = (f32[8,2048]{1,0:T(8,128)}, f32[8,2048]{1,0:T(8,128)S(1)}, u32[]{:S(2)}, u32[]{:S(2)}) collective-permute-start(f32[8,2048]{1,0:T(8,128)} %get-tuple-element.19), channel_id=1, source_target_pairs={{0,3},{1,2},{2,1},{3,0},{4,7},{5,6},{6,5},{7,4},{8,11},{9,10},{10,... | collective-permute-start | bytes 196616 | tf_op jit(solution)/shard_map/ppermute | solution.py:313
  14.9 0.0 collective-permute-done.refs_1_.their_sums_ref
  14.9 0.5 collective-permute-done.1.refs_2_
  15.4 4.6 %collective-permute-done.2.refs_3_ = f32[8,2048]{1,0:T(8,128)S(1)} collective-permute-done((f32[8,2048]{1,0:T(8,128)}, f32[8,2048]{1,0:T(8,128)S(1)}, u32[]{:S(2)}, u32[]{:S(2)}) %collective-permute-start.2) | collective-permute-done | bytes 65568 | tf_op jit(solution)/shard_map/ppermute | solution.py:313
  20.0 0.8 copy-done.1
  20.9 0.7 copies.1
  21.6 14.1 %all-to-all-start = ((bf16[64,2,768]{2,1,0:T(2,128)(2,1)}), bf16[64,2,768]{2,1,0:T(2,128)(2,1)S(1)}, u32[]{:S(2)}, u32[]{:S(2)}) async-start(bf16[64,2,768]{2,1,0:T(2,128)(2,1)} %get-tuple-element.21), calls=%async_computation | async-start | bytes 393216 | tf_op jit(solution)/shard_map/all_to_all | solution.py:326
  35.7 4.8 %collective-permute-start.3 = (bf16[192,1536]{1,0:T(8,128)(2,1)}, bf16[192,1536]{1,0:T(8,128)(2,1)S(1)}, u32[]{:S(2)}, u32[]{:S(2)}) collective-permute-start(bf16[192,1536]{1,0:T(8,128)(2,1)} %get-tuple-element.27), channel_id=1, source_target_pairs={{0,1},{1,0},{2,3},{3,2},{4,5},{5,4},{6,7},{7,6},{8,9},{9,8},{10,11... | collective-permute-start | bytes 1769480 | tf_op jit(solution)/shard_map/ppermute | solution.py:314
  40.6 0.0 copy-done.4
  40.6 0.1 reshape.14.pos_ref
  40.7 4.4 %all-gather = f32[16,1536]{1,0:T(8,128)S(1)} all-gather(f32[8,1536]{1,0:T(8,128)S(1)} %get-tuple-element.20), channel_id=2, replica_groups=mesh['dp_0'=4,'dp_1'=8,'dp_2'=2,'dp_3'=2,'head_0'=2,'head_1'=2] {'dp_3'}, dimensions={0}, use_global_device_ids=true | all-gather | bytes 147456 | tf_op jit(solution)/shard_map/all_gather | solution.py:329
  45.1 2.3 %all-to-all-done = bf16[64,2,768]{2,1,0:T(2,128)(2,1)S(1)} async-done(((bf16[64,2,768]{2,1,0:T(2,128)(2,1)}), bf16[64,2,768]{2,1,0:T(2,128)(2,1)S(1)}, u32[]{:S(2)}, u32[]{:S(2)}) %all-to-all-start) | async-done | bytes 196640 | tf_op jit(solution)/shard_map/all_to_all | solution.py:326
  47.4 0.1 reshape.13.q_ref
  47.4 0.4 logits.1
  47.9 22.0 %all_to_all.15.stats_ref = f32[64,2,128]{2,1,0:T(2,128)S(1)} all-to-all(f32[64,2,128]{2,1,0:T(2,128)S(1)} %get-tuple-element.22), channel_id=1, replica_groups={{0,10,16,26,32,42,48,58,64,74,80,90,96,106,112,122,128,138,144,154,160,..., dimensions={0} | all-to-all | bytes 131072 | tf_op jit(solution)/shard_map/all_to_all | solution.py:345
  69.8 1.0 %slopes.1 = bf16[8,8,1664]{2,1,0:T(8,128)(2,1)} custom-call(f32[64,2,128]{2,1,0:T(2,128)S(1)} %all_to_all.15.stats_ref, f32[16,128]{1,0:T(8,128)S(1)} %get-tuple-element.23.logits_ref, f32[16,128]{1,0:T(8,128)S(1)} %get-tuple-element.24.chosen_ref, f32[16,1536]{1,0:T(8,128)S(1)} %get-tuple-element.25.unit_ref, f32[16,128]{1,0:T(8,128)S(1)} %get-tuple-element.26.rnorm_ref, ...), custom_call_target="tpu_custom_call" | custom-call | tf_op jit(solution)/shard_map/slopes/pallas_call | solution.py:347
  70.8 5.1 %all-to-all-start.2 = ((bf16[8,8,1664]{2,1,0:T(8,128)(2,1)}), bf16[8,8,1664]{2,1,0:T(8,128)(2,1)S(1)}, u32[]{:S(2)}, u32[]{:S(2)}) async-start(bf16[8,8,1664]{2,1,0:T(8,128)(2,1)} %slopes.1), calls=%async_computation.2 | async-start | bytes 425984 | tf_op jit(solution)/shard_map/all_to_all | solution.py:355
  75.9 0.0 collective-permute-done.3.their_rows_ref
  75.9 8.0 %all-to-all-done.2.grads_ref = bf16[8,8,1664]{2,1,0:T(8,128)(2,1)S(1)} async-done(((bf16[8,8,1664]{2,1,0:T(8,128)(2,1)}), bf16[8,8,1664]{2,1,0:T(8,128)(2,1)S(1)}, u32[]{:S(2)}, u32[]{:S(2)}) %all-to-all-start.2) | async-done | bytes 213024 | tf_op jit(solution)/shard_map/all_to_all | solution.py:355
  83.9 1.8 %slopes_of_values.1 = (bf16[64,512]{1,0:T(8,128)(2,1)}, f32[1,1]{1,0:T(1,128)}) custom-call(s32[1,8]{1,0:T(1,128)S(1)} %copy-done.3, bf16[8,8,1664]{2,1,0:T(8,128)(2,1)S(1)} %all-to-all-done.2.grads_ref, bf16[384,1536]{1,0:T(8,128)(2,1)S(1)} %copy-done, bf16[192,1536]{1,0:T(8,128)(2,1)S(1)} %collective-permute-done.3.their_rows_ref, ...), custom_call_target="tpu_custom_call" | custom-call | tf_op jit(solution)/shard_map/slopes_of_values/pallas_call | solution.py:357
  (7 shorter events, 0.0 us)
Async XLA Ops:
  0.6 39.9 %copy-start.4 = (s32[512]{0:T(512)S(1)}, s32[512]{0:T(512)}, u32[]{:S(2)}) copy-start(s32[512]{0:T(512)} %param.13) | copy-start | bytes 6148
  4.7 10.2 %collective-permute-start = (f32[8,2048]{1,0:T(8,128)}, f32[8,2048]{1,0:T(8,128)S(1)}, u32[]{:S(2)}, u32[]{:S(2)}) collective-permute-start(f32[8,2048]{1,0:T(8,128)} %get-tuple-element.17), channel_id=1, source_target_pairs={{0,1},{1,0},{2,3},{3,2},{4,5},{5,4},{6,7},{7,6},{8,9},{9,8},{10,11... | collective-permute-start | bytes 196616 | tf_op jit(solution)/shard_map/ppermute | solution.py:313
  8.7 6.7 %collective-permute-start.1 = (f32[8,2048]{1,0:T(8,128)}, f32[8,2048]{1,0:T(8,128)S(1)}, u32[]{:S(2)}, u32[]{:S(2)}) collective-permute-start(f32[8,2048]{1,0:T(8,128)} %get-tuple-element.18), channel_id=1, source_target_pairs={{0,2},{1,3},{2,0},{3,1},{4,6},{5,7},{6,4},{7,5},{8,10},{9,11},{10,... | collective-permute-start | bytes 196616 | tf_op jit(solution)/shard_map/ppermute | solution.py:313
  13.0 7.1 %collective-permute-start.2 = (f32[8,2048]{1,0:T(8,128)}, f32[8,2048]{1,0:T(8,128)S(1)}, u32[]{:S(2)}, u32[]{:S(2)}) collective-permute-start(f32[8,2048]{1,0:T(8,128)} %get-tuple-element.19), channel_id=1, source_target_pairs={{0,3},{1,2},{2,1},{3,0},{4,7},{5,6},{6,5},{7,4},{8,11},{9,10},{10,... | collective-permute-start | bytes 196616 | tf_op jit(solution)/shard_map/ppermute | solution.py:313
  20.0 0.8 copy-start.1
  21.6 62.3 %copy-start = (bf16[384,1536]{1,0:T(8,128)(2,1)S(1)}, bf16[384,1536]{1,0:T(8,128)(2,1)}, u32[]{:S(2)}) copy-start(bf16[384,1536]{1,0:T(8,128)(2,1)} %my_rows_ref.1) | copy-start | bytes 3538948
  21.6 62.3 %copy-start.2 = (f32[8,2048]{1,0:T(8,128)S(1)}, f32[8,2048]{1,0:T(8,128)}, u32[]{:S(2)}) copy-start(f32[8,2048]{1,0:T(8,128)} %get-tuple-element.16.refs_0_.my_sums_ref) | copy-start | bytes 196612
  21.6 62.3 %copy-start.3 = (s32[1,8]{1,0:T(1,128)S(1)}, s32[1,8]{1,0:T(1,128)}, u32[]{:S(2)}) copy-start(s32[1,8]{1,0:T(1,128)} %lens_ref.3) | copy-start | bytes 100
  21.6 25.8 %all-to-all-start = ((bf16[64,2,768]{2,1,0:T(2,128)(2,1)}), bf16[64,2,768]{2,1,0:T(2,128)(2,1)S(1)}, u32[]{:S(2)}, u32[]{:S(2)}) async-start(bf16[64,2,768]{2,1,0:T(2,128)(2,1)} %get-tuple-element.21), calls=%async_computation | async-start | bytes 393216 | tf_op jit(solution)/shard_map/all_to_all | solution.py:326
  35.7 40.2 %collective-permute-start.3 = (bf16[192,1536]{1,0:T(8,128)(2,1)}, bf16[192,1536]{1,0:T(8,128)(2,1)S(1)}, u32[]{:S(2)}, u32[]{:S(2)}) collective-permute-start(bf16[192,1536]{1,0:T(8,128)(2,1)} %get-tuple-element.27), channel_id=1, source_target_pairs={{0,1},{1,0},{2,3},{3,2},{4,5},{5,4},{6,7},{7,6},{8,9},{9,8},{10,11... | collective-permute-start | bytes 1769480 | tf_op jit(solution)/shard_map/ppermute | solution.py:314
  70.8 13.1 %all-to-all-start.2 = ((bf16[8,8,1664]{2,1,0:T(8,128)(2,1)}), bf16[8,8,1664]{2,1,0:T(8,128)(2,1)S(1)}, u32[]{:S(2)}, u32[]{:S(2)}) async-start(bf16[8,8,1664]{2,1,0:T(8,128)(2,1)} %slopes.1), calls=%async_computation.2 | async-start | bytes 425984 | tf_op jit(solution)/shard_map/all_to_all | solution.py:355

commit v5 on v4

--- a/solution.py
+++ b/solution.py
@@ -21,6 +21,7 @@
 NT = (((1,), (1,)), ((), ()))
 TN = (((0,), (0,)), ((), ()))
 VMEM = pl.BlockSpec(memory_space=pltpu.VMEM)
+HBM = pl.BlockSpec(memory_space=pl.ANY)
 SMEM = pl.BlockSpec(memory_space=pltpu.SMEM)
 
 
@@ -78,9 +79,17 @@
 
 
 def attend_kernel(
-    lens_ref, q_ref, k_ref, v_ref, w_ref, queries_ref, *out_refs
+    lens_ref, q_hbm, k_hbm, v_hbm, w_hbm, queries_ref, sent_ref, rows_ref,
+    q_ref, k_ref, v_ref, w_ref, total, done,
 ):
-    *sent_refs, rows_ref, total = out_refs
+    copies = [
+        pltpu.make_async_copy(source, target, done.at[i])
+        for i, (source, target) in enumerate(
+            ((q_hbm, q_ref), (k_hbm, k_ref), (v_hbm, v_ref), (w_hbm, w_ref))
+        )
+    ]
+    for copy in copies:
+        copy.start()
     seq_len, width = q_ref.shape
     heads = width // HD
     docs = lens_ref.shape[1]
@@ -91,6 +100,8 @@
     block = min(128, seq_len)
     factor = math.log2(math.e) / math.sqrt(HD)
     lane = lax.broadcasted_iota(jnp.int32, (block, HD), 1)
+    copies[0].wait()
+    copies[1].wait()
     for first in range(0, seq_len, block):
         low = max(0, (first - LONGEST + 1) // block * block)
         span = first + block - low
@@ -115,48 +126,54 @@
     shares = jnp.concatenate(
         [jnp.where(member, by_head[h : h + 1, :], 0.0) for h in range(heads)], axis=0
     )
+    copies[2].wait()
     sums = exact_dot(shares, v_ref[:, columns], (((1,), (0,)), ((), ())))
     pooled = jnp.concatenate(
         [sums[h * docs : (h + 1) * docs] for h in range(heads)], axis=1
     ) / lens_column(lens_ref, docs)
+    copies[3].wait()
     emb = exact_dot(pooled, w_ref[...], (((1,), (0,)), ((), ())))
     features = emb.shape[1]
     queries = queries_ref[...].astype(jnp.float32)
     place = lax.broadcasted_iota(jnp.int32, queries.shape, 0)
-    rest = jnp.zeros((docs - heads - 1, seq_len), jnp.float32)
-    tail = jnp.zeros((1, seq_len - width), jnp.float32)
-    for apart, sent_ref in enumerate(sent_refs):
-        row = jnp.where(place == (query_class() ^ apart), queries, 0.0)
-        row = jnp.concatenate([jnp.sum(row, axis=0, keepdims=True), tail], axis=1)
-        sent_ref[:, :features] = emb
-        sent_ref[:, features:] = jnp.concatenate([by_head[:heads], row, rest], axis=0)
+    middle = seq_len // 2
+    pad = jnp.zeros((1, 2 * middle - width), jnp.float32)
+    for k in range(sent_ref.shape[0]):
+        row = jnp.where(place == k ^ (2 * lax.axis_index(DP[2])), queries, 0.0)
+        row = jnp.sum(row, axis=0, keepdims=True)
+        sent_ref[k, :, :features] = emb
+        sent_ref[k, :, features:] = jnp.concatenate(
+            [
+                by_head[:heads, :middle],
+                by_head[:heads, middle:],
+                row[:, :middle],
+                jnp.concatenate([row[:, middle:], pad], axis=1),
+            ],
+            axis=0,
+        )
     half = HD // 2
     for h in range(heads):
         wanted = pl.ds(pl.multiple_of(h * HD + (1 - lax.axis_index(HEAD[1])) * half, half), half)
         rows_ref[h * half : (h + 1) * half, :] = w_ref[wanted, :]
 
 
-def copies_kernel(*refs):
-    *partial_refs, out_ref, whole_ref = refs
+def copies_kernel(got_ref, out_ref, whole_ref):
     docs, features = whole_ref.shape
-    split = len(partial_refs)
+    split = got_ref.shape[0]
     width = features // split
-    row = HEADS // split
-    me = lax.axis_index(HEAD)
-    slices = [ref[row : row + 1, features : features + width] for ref in partial_refs]
+    place = 2 * (HEADS // split)
     parts = []
-    for owner in range(split):
-        part = jnp.zeros_like(slices[0])
-        for apart in range(split):
-            part = jnp.where(me == owner ^ apart, slices[apart], part)
-        parts.append(part)
-    middle = split // 2
+    for k in range(split):
+        line = got_ref[k, place:, features:]
+        middle = line.shape[1]
+        parts += [line[:1, :], line[1:, : width - middle]]
+    middle = split
     halves = [jnp.concatenate(parts[:middle], axis=1), jnp.concatenate(parts[middle:], axis=1)]
     both = jnp.concatenate(halves, axis=0).astype(jnp.bfloat16)
     out_ref[...] = jnp.broadcast_to(both[None], out_ref.shape)
-    whole = partial_refs[0][:, :features]
-    for ref in partial_refs[1:]:
-        whole = whole + ref[:, :features]
+    whole = got_ref[0, :, :features]
+    for k in range(1, split):
+        whole = whole + got_ref[k, :, :features]
     whole_ref[...] = whole
 
 
@@ -241,9 +258,7 @@
         out_ref[k, :, features:] = losses.astype(jnp.bfloat16)
 
 
-def values_kernel(
-    lens_ref, grads_ref, my_rows_ref, their_rows_ref, my_sums_ref, their_sums_ref, out_ref, loss_ref
-):
+def values_kernel(lens_ref, grads_ref, my_rows_ref, their_rows_ref, got_ref, out_ref, loss_ref):
     docs = lens_ref.shape[1]
     features = my_rows_ref.shape[1]
     seq_len = out_ref.shape[1]
@@ -257,25 +272,31 @@
     loss_ref[...] = jnp.sum(
         jnp.sum(grads[:3, features:], axis=0, keepdims=True), axis=1, keepdims=True
     ) / (grads_ref.shape[0] * lanes)
+    rows = [
+        my_rows_ref[pl.ds(pl.multiple_of(h * HD + low * half, half), half), :]
+        for h in range(heads)
+    ]
+    rows = jnp.concatenate([*rows, their_rows_ref[...]], axis=0)
     terms = three_terms(grads[:, :features])
-    factor = loss_scale / lens_column(lens_ref, docs)
-    slopes = []
-    for h in range(heads):
-        rows = my_rows_ref[pl.ds(pl.multiple_of(h * HD + low * half, half), half), :]
-        slopes.append(lax.dot_general(terms, rows, NT, preferred_element_type=jnp.float32))
-    for h in range(heads):
-        rows = their_rows_ref[h * half : (h + 1) * half, :]
-        slopes.append(lax.dot_general(terms, rows, NT, preferred_element_type=jnp.float32))
-    slopes = [(of_three(part) * factor).astype(jnp.bfloat16) for part in slopes]
+    slopes = lax.dot_general(rows, terms, NT, preferred_element_type=jnp.float32)
+    slopes = slopes[:, :docs] + slopes[:, docs : 2 * docs] + slopes[:, 2 * docs :]
+    lane = lax.broadcasted_iota(jnp.int32, (1, docs), 1)
+    lens = jnp.zeros((1, docs), jnp.int32)
+    for j in range(docs):
+        lens = jnp.where(lane == j, lens_ref[0, j], lens)
+    slopes = (slopes / lens.astype(jnp.float32) * loss_scale).astype(jnp.bfloat16)
+    slopes = [slopes[h * half : (h + 1) * half] for h in range(2 * heads)]
     seg, _ = document_of(lens_ref, docs, (1, seq_len), 1)
     member = lax.broadcasted_iota(jnp.int32, (docs, seq_len), 0) == seg
+    me = lax.axis_index(HEAD)
     shares = []
-    for sums in (my_sums_ref, their_sums_ref):
-        shares += [jnp.where(member, sums[h : h + 1, features:], 0.0) for h in range(heads)]
-    out = lax.dot_general(
-        jnp.concatenate(slopes * 3, axis=0),
+    for owner in (me, me ^ 1):
+        sums = got_ref[owner, :, features:]
+        sums = jnp.concatenate([sums[:heads], sums[heads : 2 * heads]], axis=1)
+        shares += [jnp.where(member, sums[h : h + 1], 0.0) for h in range(heads)]
+    out = jnp.dot(
+        jnp.concatenate(slopes * 3, axis=1),
         three_terms(jnp.concatenate(shares, axis=0)),
-        TN,
         preferred_element_type=jnp.float32,
     )
     out_ref[...] = out.astype(jnp.bfloat16)
@@ -297,32 +318,36 @@
     half = HD // 2
     line = (*DP[:3], *HEAD)
     groups = class_groups()
-    pairs = [[(i, i ^ apart) for i in range(split)] for apart in range(split)]
-
-    *partials, wanted = pl.pallas_call(
+
+    partial, wanted = pl.pallas_call(
         attend_kernel,
-        out_shape=(jax.ShapeDtypeStruct((docs, features + seq_len), f32),) * split
-        + (jax.ShapeDtypeStruct((heads * half, features), bf16),),
-        in_specs=[SMEM] + [VMEM] * 5,
-        out_specs=(VMEM,) * (split + 1),
-        scratch_shapes=[pltpu.VMEM((seq_len, HD), f32)],
+        out_shape=(
+            jax.ShapeDtypeStruct((split, docs, features + seq_len // 2), f32),
+            jax.ShapeDtypeStruct((heads * half, features), bf16),
+        ),
+        in_specs=[SMEM] + [HBM] * 4 + [VMEM],
+        out_specs=(VMEM, VMEM),
+        scratch_shapes=[
+            *(pltpu.VMEM(a.shape, a.dtype) for a in (attn_queries, keys, values, out_weight)),
+            pltpu.VMEM((seq_len, HD), f32),
+            pltpu.SemaphoreType.DMA((4,)),
+        ],
         compiler_params=big,
         name="attend",
     )(lengths, attn_queries, keys, values, out_weight, queries)
-    own = partials[0]
-    got = [lax.ppermute(partials[apart], HEAD, pairs[apart]) for apart in range(1, split)]
-    their_rows = lax.ppermute(wanted, HEAD, pairs[1])
+    got = lax.all_to_all(partial, HEAD, 0, 0, tiled=True)
+    their_rows = lax.ppermute(wanted, HEAD, [(i, i ^ 1) for i in range(split)])
     rows, whole = pl.pallas_call(
         copies_kernel,
         out_shape=(
             jax.ShapeDtypeStruct((others, 2, features // 2), bf16),
             jax.ShapeDtypeStruct((docs, features), f32),
         ),
-        in_specs=[VMEM] * split,
+        in_specs=[VMEM],
         out_specs=(VMEM, VMEM),
         compiler_params=small,
         name="copies",
-    )(own, *got)
+    )(got)
     every = lax.all_to_all(rows, line, 0, 0, axis_index_groups=groups, tiled=True)
     every = every.reshape(lanes, features // 2)
     pos = positives.reshape(others, cores * split)
@@ -360,11 +385,11 @@
             jax.ShapeDtypeStruct((half, seq_len), bf16),
             jax.ShapeDtypeStruct((1, 1), f32),
         ),
-        in_specs=[SMEM] + [VMEM] * 5,
+        in_specs=[SMEM] + [VMEM] * 4,
         out_specs=(VMEM, VMEM),
         compiler_params=small,
         name="slopes_of_values",
-    )(lengths, grads, out_weight, their_rows, own, got[0])
+    )(lengths, grads, out_weight, their_rows, got)
     return d_values.T, loss.reshape(())
 
 

time: 86.3 us -> 83.1 us (0.963)
  starting transfers between devices: 34.2 us -> 26.7 us
  blocking collectives: 26.4 us -> 33.8 us
  waiting for transfers between devices: 15.4 us -> 12.7 us
    ppermute x4 -> x1, starting transfers between devices: 15 us -> 3.75 us  [per_device(): their_rows = lax.ppermute(wanted, HEAD, [(i, i ^ 1) for i in range(split)])]
    all_to_all x0 -> x1, blocking collectives: none -> 11.2 us  [per_device(): got = lax.all_to_all(partial, HEAD, 0, 0, tiled=True)]
    ppermute x4 -> x1, waiting for transfers between devices: 5.15 us -> 0.01 us  [per_device(): their_rows = lax.ppermute(wanted, HEAD, [(i, i ^ 1) for i in range(split)])]
    all_to_all x1, starting transfers between devices: 14.1 us -> 17.6 us  [per_device(): lax.all_to_all(rows, line, 0, 0, axis_index_groups=groups, tiled=True)]
    all_to_all x1, waiting for transfers between devices: 2.3 us -> 4.68 us  [per_device(): lax.all_to_all(rows, line, 0, 0, axis_index_groups=groups, tiled=True)]
    all_to_all x1, blocking collectives: 22 us -> 19.6 us  [per_device(): lax.all_to_all(stats, line, 0, 0, axis_index_groups=groups, tiled=True)]
    all_gather x1, blocking collectives: 4.4 us -> 3.09 us  [per_device(): pair = lax.all_gather(whole, DP[3])]
  transfers between devices with their start and end apart: 6 -> 3, of which waited for: 4 -> 2; matrix products, arithmetic and copies ran while one was open for 0% -> 0% of each run, Pallas kernels for 2% -> 2%
where the time goes in v5:
time: 83.1 us; the launch traced here: 82.6 us
  blocking collectives  33.8 us (41%)
  starting transfers between devices  26.7 us (32%)
  waiting for transfers between devices  12.7 us (15%)
  Pallas kernels  8.48 us (10%)
    all_to_all x1, blocking collectives, per_device(): lax.all_to_all(stats, line, 0, 0, axis_index_groups=groups, tiled=True)  19.6 us
    all_to_all x1, starting transfers between devices, per_device(): lax.all_to_all(rows, line, 0, 0, axis_index_groups=groups, tiled=True)  17.6 us
    all_to_all x1, blocking collectives, per_device(): got = lax.all_to_all(partial, HEAD, 0, 0, tiled=True)  11.2 us
    all_to_all x1, waiting for transfers between devices, per_device(): grads = lax.all_to_all(grads, (DP[3], *HEAD), 0, 0, tiled=True)  8 us
    all_to_all x1, starting transfers between devices, per_device(): grads = lax.all_to_all(grads, (DP[3], *HEAD), 0, 0, tiled=True)  5.41 us
    all_to_all x1, waiting for transfers between devices, per_device(): lax.all_to_all(rows, line, 0, 0, axis_index_groups=groups, tiled=True)  4.68 us
    pallas_call x1, Pallas kernels, per_device(): pl.pallas_call(attend_kernel, out_shape=(jax.ShapeDtypeStruct((split, doc...  4.4 us
    ppermute x1, starting transfers between devices, per_device(): their_rows = lax.ppermute(wanted, HEAD, [(i, i ^ 1) for i in range(split)])  3.75 us
  transfers between devices with their start and end apart: 3, of which 2 were waited for; matrix products, arithmetic and copies ran while one was open for 0% of the time, Pallas kernels for 2%

profile of v5, /device:TPU:1, one launch (start us, length us, event | category | flops | bytes accessed | tf_op | source)
XLA Modules:
  0.0 82.6 jit_solution(16411895767732952890)
XLA Ops:
  0.6 0.0 copy-start.2
  0.6 4.4 %attend.1 = (f32[4,8,1792]{2,1,0:T(8,128)}, bf16[192,1536]{1,0:T(8,128)(2,1)}) custom-call(s32[1,8]{1,0:T(1,128)} %lens_ref.3, bf16[512,384]{1,0:T(8,128)(2,1)} %q_hbm.1, bf16[512,256]{1,0:T(8,128)(2,1)} %k_hbm.1, bf16[512,256]{1,0:T(8,128)(2,1)} %v_hbm.1, bf16[384,1536]{1,0:T(8,128)(2,1)} %my_rows_ref.1, bf16[4,384]{1,0:T(4,128)(2,1)} %queries_ref.1), custom_call_target="tpu_custom_call" | custom-call | tf_op jit(solution)/shard_map/attend/pallas_call | solution.py:322
  5.0 11.2 %all_to_all.20.got_ref = f32[4,8,1792]{2,1,0:T(8,128)S(1)} all-to-all(f32[4,8,1792]{2,1,0:T(8,128)} %get-tuple-element.13), channel_id=1, replica_groups=mesh['dp_0'=4,'dp_1'=8,'dp_2'=2,'dp_3'=2,'head_0'=2,'head_1'=2] {'head_0..., dimensions={0} | all-to-all | bytes 458752 | tf_op jit(solution)/shard_map/all_to_all | solution.py:338
  16.2 0.7 copies.1
  16.9 0.0 copy-start
  16.9 0.0 copy-start.1
  16.9 17.6 %all-to-all-start.1 = ((bf16[64,2,768]{2,1,0:T(2,128)(2,1)}), bf16[64,2,768]{2,1,0:T(2,128)(2,1)S(1)}, u32[]{:S(2)}, u32[]{:S(2)}) async-start(bf16[64,2,768]{2,1,0:T(2,128)(2,1)} %get-tuple-element.15), calls=%async_computation.1 | async-start | bytes 393216 | tf_op jit(solution)/shard_map/all_to_all | solution.py:351
  34.5 3.8 %collective-permute-start = (bf16[192,1536]{1,0:T(8,128)(2,1)}, bf16[192,1536]{1,0:T(8,128)(2,1)S(1)}, u32[]{:S(2)}, u32[]{:S(2)}) collective-permute-start(bf16[192,1536]{1,0:T(8,128)(2,1)} %get-tuple-element.21), channel_id=1, source_target_pairs={{0,1},{1,0},{2,3},{3,2},{4,5},{5,4},{6,7},{7,6},{8,9},{9,8},{10,11... | collective-permute-start | bytes 1769480 | tf_op jit(solution)/shard_map/ppermute | solution.py:339
  38.3 0.0 copy-done.2
  38.3 0.1 reshape.14.pos_ref
  38.4 3.1 %all-gather = f32[16,1536]{1,0:T(8,128)S(1)} all-gather(f32[8,1536]{1,0:T(8,128)S(1)} %get-tuple-element.14), channel_id=2, replica_groups=mesh['dp_0'=4,'dp_1'=8,'dp_2'=2,'dp_3'=2,'head_0'=2,'head_1'=2] {'dp_3'}, dimensions={0}, use_global_device_ids=true | all-gather | bytes 147456 | tf_op jit(solution)/shard_map/all_gather | solution.py:354
  41.5 4.7 %all-to-all-done.1 = bf16[64,2,768]{2,1,0:T(2,128)(2,1)S(1)} async-done(((bf16[64,2,768]{2,1,0:T(2,128)(2,1)}), bf16[64,2,768]{2,1,0:T(2,128)(2,1)S(1)}, u32[]{:S(2)}, u32[]{:S(2)}) %all-to-all-start.1) | async-done | bytes 196640 | tf_op jit(solution)/shard_map/all_to_all | solution.py:351
  46.1 0.1 reshape.13.q_ref
  46.2 0.4 logits.1
  46.6 19.6 %all_to_all.21.stats_ref = f32[64,2,128]{2,1,0:T(2,128)S(1)} all-to-all(f32[64,2,128]{2,1,0:T(2,128)S(1)} %get-tuple-element.16), channel_id=1, replica_groups={{0,10,16,26,32,42,48,58,64,74,80,90,96,106,112,122,128,138,144,154,160,..., dimensions={0} | all-to-all | bytes 131072 | tf_op jit(solution)/shard_map/all_to_all | solution.py:370
  66.2 1.0 %slopes.1 = bf16[8,8,1664]{2,1,0:T(8,128)(2,1)} custom-call(f32[64,2,128]{2,1,0:T(2,128)S(1)} %all_to_all.21.stats_ref, f32[16,128]{1,0:T(8,128)S(1)} %get-tuple-element.17.logits_ref, f32[16,128]{1,0:T(8,128)S(1)} %get-tuple-element.18.chosen_ref, f32[16,1536]{1,0:T(8,128)S(1)} %get-tuple-element.19.unit_ref, f32[16,128]{1,0:T(8,128)S(1)} %get-tuple-element.20.rnorm_ref, ...), custom_call_target="tpu_custom_call" | custom-call | tf_op jit(solution)/shard_map/slopes/pallas_call | solution.py:372
  67.2 5.4 %all-to-all-start.3 = ((bf16[8,8,1664]{2,1,0:T(8,128)(2,1)}), bf16[8,8,1664]{2,1,0:T(8,128)(2,1)S(1)}, u32[]{:S(2)}, u32[]{:S(2)}) async-start(bf16[8,8,1664]{2,1,0:T(8,128)(2,1)} %slopes.1), calls=%async_computation.3 | async-start | bytes 425984 | tf_op jit(solution)/shard_map/all_to_all | solution.py:380
  72.7 0.0 collective-permute-done.their_rows_ref
  72.7 8.0 %all-to-all-done.3.grads_ref = bf16[8,8,1664]{2,1,0:T(8,128)(2,1)S(1)} async-done(((bf16[8,8,1664]{2,1,0:T(8,128)(2,1)}), bf16[8,8,1664]{2,1,0:T(8,128)(2,1)S(1)}, u32[]{:S(2)}, u32[]{:S(2)}) %all-to-all-start.3) | async-done | bytes 213024 | tf_op jit(solution)/shard_map/all_to_all | solution.py:380
  80.7 0.0 copy-done
  80.7 0.0 copy-done.1
  80.7 1.9 %slopes_of_values.1 = (bf16[64,512]{1,0:T(8,128)(2,1)}, f32[1,1]{1,0:T(1,128)}) custom-call(s32[1,8]{1,0:T(1,128)S(1)} %copy-done.1, bf16[8,8,1664]{2,1,0:T(8,128)(2,1)S(1)} %all-to-all-done.3.grads_ref, bf16[384,1536]{1,0:T(8,128)(2,1)S(1)} %copy-done, bf16[192,1536]{1,0:T(8,128)(2,1)S(1)} %collective-permute-done.their_rows_ref, ...), custom_call_target="tpu_custom_call" | custom-call | tf_op jit(solution)/shard_map/slopes_of_values/pallas_call | solution.py:382
Async XLA Ops:
  0.6 37.6 %copy-start.2 = (s32[512]{0:T(512)S(1)}, s32[512]{0:T(512)}, u32[]{:S(2)}) copy-start(s32[512]{0:T(512)} %param.13) | copy-start | bytes 6148
  16.9 63.7 %copy-start = (bf16[384,1536]{1,0:T(8,128)(2,1)S(1)}, bf16[384,1536]{1,0:T(8,128)(2,1)}, u32[]{:S(2)}) copy-start(bf16[384,1536]{1,0:T(8,128)(2,1)} %my_rows_ref.1) | copy-start | bytes 3538948
  16.9 63.7 %copy-start.1 = (s32[1,8]{1,0:T(1,128)S(1)}, s32[1,8]{1,0:T(1,128)}, u32[]{:S(2)}) copy-start(s32[1,8]{1,0:T(1,128)} %lens_ref.3) | copy-start | bytes 100
  16.9 29.2 %all-to-all-start.1 = ((bf16[64,2,768]{2,1,0:T(2,128)(2,1)}), bf16[64,2,768]{2,1,0:T(2,128)(2,1)S(1)}, u32[]{:S(2)}, u32[]{:S(2)}) async-start(bf16[64,2,768]{2,1,0:T(2,128)(2,1)} %get-tuple-element.15), calls=%async_computation.1 | async-start | bytes 393216 | tf_op jit(solution)/shard_map/all_to_all | solution.py:351
  34.5 38.1 %collective-permute-start = (bf16[192,1536]{1,0:T(8,128)(2,1)}, bf16[192,1536]{1,0:T(8,128)(2,1)S(1)}, u32[]{:S(2)}, u32[]{:S(2)}) collective-permute-start(bf16[192,1536]{1,0:T(8,128)(2,1)} %get-tuple-element.21), channel_id=1, source_target_pairs={{0,1},{1,0},{2,3},{3,2},{4,5},{5,4},{6,7},{7,6},{8,9},{9,8},{10,11... | collective-permute-start | bytes 1769480 | tf_op jit(solution)/shard_map/ppermute | solution.py:339
  67.2 13.4 %all-to-all-start.3 = ((bf16[8,8,1664]{2,1,0:T(8,128)(2,1)}), bf16[8,8,1664]{2,1,0:T(8,128)(2,1)S(1)}, u32[]{:S(2)}, u32[]{:S(2)}) async-start(bf16[8,8,1664]{2,1,0:T(8,128)(2,1)} %slopes.1), calls=%async_computation.3 | async-start | bytes 425984 | tf_op jit(solution)/shard_map/all_to_all | solution.py:380

commit v6 on v5

--- a/solution.py
+++ b/solution.py
@@ -99,7 +99,9 @@
     total[...] = jnp.zeros_like(total)
     block = min(128, seq_len)
     factor = math.log2(math.e) / math.sqrt(HD)
-    lane = lax.broadcasted_iota(jnp.int32, (block, HD), 1)
+    lane = lax.broadcasted_iota(jnp.int32, (heads * block, HD), 1)
+    head = lax.broadcasted_iota(jnp.int32, (heads * block, HD), 0) // block
+    pick = (lane == head).astype(jnp.bfloat16)
     copies[0].wait()
     copies[1].wait()
     for first in range(0, seq_len, block):
@@ -109,18 +111,20 @@
         k_place = low + lax.broadcasted_iota(jnp.int32, (span, block), 0)
         q_place = first + lax.broadcasted_iota(jnp.int32, (span, block), 1)
         allowed = (k_place <= q_place) & (k_place >= start[:, first : first + block])
+        q_block = jnp.concatenate(
+            [q_ref[first : first + block, h * HD : (h + 1) * HD] for h in range(heads)], axis=0
+        )
+        scores = lax.dot_general(k_block, q_block, NT, preferred_element_type=jnp.float32)
+        probs = []
         for h in range(heads):
-            q_block = q_ref[first : first + block, h * HD : (h + 1) * HD]
-            scores = lax.dot_general(k_block, q_block, NT, preferred_element_type=jnp.float32)
-            scores = jnp.where(allowed, scores, -1e30)
-            top = jnp.max(scores, axis=0, keepdims=True)
-            expo = jnp.exp2((scores - top) * factor)
+            mine = jnp.where(allowed, scores[:, h * block : (h + 1) * block], -1e30)
+            top = jnp.max(mine, axis=0, keepdims=True)
+            expo = jnp.exp2((mine - top) * factor)
             norm = 1.0 / jnp.sum(expo, axis=0, keepdims=True)
-            probs = (expo * norm).astype(jnp.bfloat16)
-            pick = (lane == h).astype(jnp.bfloat16)
-            total[low : first + block, :] += jnp.dot(
-                probs, pick, preferred_element_type=jnp.float32
-            )
+            probs.append((expo * norm).astype(jnp.bfloat16))
+        total[low : first + block, :] += jnp.dot(
+            jnp.concatenate(probs, axis=1), pick, preferred_element_type=jnp.float32
+        )
     by_head = total[...].T
     member = lax.broadcasted_iota(jnp.int32, (docs, seq_len), 0) == seg
     shares = jnp.concatenate(
@@ -207,26 +211,37 @@
         return jnp.sum(lines, axis=0, keepdims=True)
 
     positive = 128.0 * spread_out(pos // 128) + spread_out(pos % 128)
-    owned = lax.axis_index(DP[:3]) * docs + lax.broadcasted_iota(jnp.int32, (docs, 2 * count), 0)
+    me = lax.axis_index(DP[:3])
+    row = lax.broadcasted_iota(jnp.int32, (docs, 2 * count), 0)
+    owned = jnp.concatenate([me * docs + row, (me ^ 1) * docs + row], axis=0)
     return (positive == owned.astype(jnp.float32)).astype(jnp.float32)
 
 
-def logits_kernel(emb_ref, q_ref, pos_ref, out_ref, logits_ref, chosen_ref, unit_ref, rnorm_ref):
-    emb = jnp.concatenate([emb_ref[k] for k in range(emb_ref.shape[0])], axis=0)
+def logits_kernel(
+    emb_ref, other_ref, q_ref, pos_ref, out_ref, logits_ref, chosen_ref, unit_ref, rnorm_ref
+):
+    docs = logits_ref.shape[0]
+    emb = [ref[k] for ref in (emb_ref, other_ref) for k in range(ref.shape[0])]
+    emb = jnp.concatenate(emb, axis=0)
     rnorm = 1.0 / jnp.sqrt(jnp.sum(emb * emb, axis=1, keepdims=True) + 1e-06)
     unit = emb * rnorm
     logits = pair_logits(unit.astype(jnp.bfloat16), q_ref)
-    chosen = positive_mask(pos_ref, emb.shape[0])
+    chosen = positive_mask(pos_ref, docs)
     top = jnp.max(logits, axis=0, keepdims=True)
-    lse = top + jnp.log(jnp.sum(jnp.exp(logits - top), axis=0, keepdims=True))
-    positive = jnp.sum(logits * chosen, axis=0, keepdims=True)
+    expo = jnp.exp(logits - top)
+    total = jnp.sum(expo[:docs], axis=0, keepdims=True) + jnp.sum(expo[docs:], axis=0, keepdims=True)
+    lse = top + jnp.log(total)
+    hits = logits * chosen
+    positive = jnp.sum(hits[:docs], axis=0, keepdims=True) + jnp.sum(
+        hits[docs:], axis=0, keepdims=True
+    )
     out_ref[...] = jnp.broadcast_to(
         jnp.concatenate([lse, positive], axis=0)[None], out_ref.shape
     )
-    logits_ref[...] = logits
-    chosen_ref[...] = chosen
-    unit_ref[...] = unit
-    rnorm_ref[...] = jnp.broadcast_to(rnorm, rnorm_ref.shape)
+    logits_ref[...] = logits[:docs]
+    chosen_ref[...] = chosen[:docs]
+    unit_ref[...] = unit[:docs]
+    rnorm_ref[...] = jnp.broadcast_to(rnorm[:docs], rnorm_ref.shape)
 
 
 def slopes_kernel(stats_ref, logits_ref, chosen_ref, unit_ref, rnorm_ref, q_ref, out_ref):
@@ -351,23 +366,28 @@
     every = lax.all_to_all(rows, line, 0, 0, axis_index_groups=groups, tiled=True)
     every = every.reshape(lanes, features // 2)
     pos = positives.reshape(others, cores * split)
+    whole, their_rows = lax.optimization_barrier((whole, their_rows))
+    uppers = lax.axis_size(DP[2])
+    across = [(i, i ^ (split + 2)) for i in range(uppers * split)]
+    other = lax.ppermute(whole, (DP[2], *HEAD), across)
     pair = lax.all_gather(whole, DP[3])
+    other = lax.all_gather(other, DP[3])
 
     stats, logits, chosen, unit, rnorm = pl.pallas_call(
         logits_kernel,
         out_shape=(
-            jax.ShapeDtypeStruct((others, 2, lanes), f32),
+            jax.ShapeDtypeStruct((others // uppers, 2, lanes), f32),
             jax.ShapeDtypeStruct((cores * docs, lanes), f32),
             jax.ShapeDtypeStruct((cores * docs, lanes), f32),
             jax.ShapeDtypeStruct((cores * docs, features), f32),
             jax.ShapeDtypeStruct((cores * docs, HD), f32),
         ),
-        in_specs=[VMEM] * 3,
+        in_specs=[VMEM] * 4,
         out_specs=(VMEM,) * 5,
         compiler_params=small,
         name="logits",
-    )(pair, every, pos)
-    stats = lax.all_to_all(stats, line, 0, 0, axis_index_groups=groups, tiled=True)
+    )(pair, other, every, pos)
+    stats = lax.all_to_all(stats, DP[:2], 0, 0, tiled=True)
 
     grads = pl.pallas_call(
         slopes_kernel,

time: 83.1 us -> 81.8 us (0.984)
  waiting for transfers between devices: 12.7 us -> 2.09 us
  blocking collectives: 33.8 us -> 39.8 us
  starting transfers between devices: 26.7 us -> 30.3 us
    all_to_all x1, waiting for transfers between devices: 8 us -> 2.08 us  [per_device(): got = lax.all_to_all(partial, HEAD, 0, 0, tiled=True)]
    ppermute x0 -> x1, starting transfers between devices: none -> 5.16 us  [per_device(): other = lax.ppermute(whole, (DP[2], *HEAD), across)]
    all_to_all x1, waiting for transfers between devices: 4.68 us -> 0.01 us  [per_device(): lax.all_to_all(rows, line, 0, 0, axis_index_groups=groups, tiled=True)]
    all_gather x0 -> x1, blocking collectives: none -> 2.39 us  [per_device(): other = lax.all_gather(other, DP[3])]
    all_gather x1, blocking collectives: 3.09 us -> 4.99 us  [per_device(): pair = lax.all_gather(whole, DP[3])]
    all_to_all x2, blocking collectives: 30.7 us -> 32.4 us  [the longest x1 18.1 us: per_device(): stats = lax.all_to_all(stats, DP[:2], 0, 0, tiled=True)]
    all_to_all x1, starting transfers between devices: 17.6 us -> 16.4 us  [per_device(): lax.all_to_all(rows, line, 0, 0, axis_index_groups=groups, tiled=True)]
  transfers between devices with their start and end apart: 3 -> 4, of which waited for: 2 -> 1; matrix products, arithmetic and copies ran while one was open for 0% -> 0% of each run, Pallas kernels for 2% -> 1%
where the time goes in v6:
time: 81.8 us; the launch traced here: 81.3 us
  blocking collectives  39.8 us (49%)
  starting transfers between devices  30.3 us (37%)
  Pallas kernels  8.23 us (10%)
  waiting for transfers between devices  2.09 us (3%)
    all_to_all x1, blocking collectives, per_device(): stats = lax.all_to_all(stats, DP[:2], 0, 0, tiled=True)  18.1 us
    all_to_all x1, starting transfers between devices, per_device(): lax.all_to_all(rows, line, 0, 0, axis_index_groups=groups, tiled=True)  16.4 us
    all_to_all x1, blocking collectives, per_device(): grads = lax.all_to_all(grads, (DP[3], *HEAD), 0, 0, tiled=True)  14.3 us
    all_to_all x1, starting transfers between devices, per_device(): got = lax.all_to_all(partial, HEAD, 0, 0, tiled=True)  5.43 us
    ppermute x1, starting transfers between devices, per_device(): other = lax.ppermute(whole, (DP[2], *HEAD), across)  5.16 us
    all_gather x1, blocking collectives, per_device(): pair = lax.all_gather(whole, DP[3])  4.99 us
    pallas_call x1, Pallas kernels, per_device(): pl.pallas_call(attend_kernel, out_shape=(jax.ShapeDtypeStruct((split, doc...  4.85 us
    ppermute x1, starting transfers between devices, per_device(): their_rows = lax.ppermute(wanted, HEAD, [(i, i ^ 1) for i in range(split)])  3.36 us
  transfers between devices with their start and end apart: 4, of which 1 were waited for; matrix products, arithmetic and copies ran while one was open for 0% of the time, Pallas kernels for 1%

profile of v6, /device:TPU:1, one launch (start us, length us, event | category | flops | bytes accessed | tf_op | source)
XLA Modules:
  0.0 81.3 jit_solution(15315627763053548383)
XLA Ops:
  0.6 0.0 copy-start.2
  0.6 4.8 %attend.1 = (f32[4,8,1792]{2,1,0:T(8,128)}, bf16[192,1536]{1,0:T(8,128)(2,1)}) custom-call(s32[1,8]{1,0:T(1,128)} %lens_ref.3, bf16[512,384]{1,0:T(8,128)(2,1)} %q_hbm.1, bf16[512,256]{1,0:T(8,128)(2,1)} %k_hbm.1, bf16[512,256]{1,0:T(8,128)(2,1)} %v_hbm.1, bf16[384,1536]{1,0:T(8,128)(2,1)} %my_rows_ref.1, bf16[4,384]{1,0:T(4,128)(2,1)} %queries_ref.1), custom_call_target="tpu_custom_call" | custom-call | tf_op jit(solution)/shard_map/attend/pallas_call | solution.py:337
  5.5 5.4 %all-to-all-start = ((f32[4,8,1792]{2,1,0:T(8,128)}), f32[4,8,1792]{2,1,0:T(8,128)S(1)}, u32[]{:S(2)}, u32[]{:S(2)}) async-start(f32[4,8,1792]{2,1,0:T(8,128)} %get-tuple-element.15), calls=%async_computation | async-start | bytes 458752 | tf_op jit(solution)/shard_map/all_to_all | solution.py:353
  10.9 3.4 %collective-permute-start = (bf16[192,1536]{1,0:T(8,128)(2,1)}, bf16[192,1536]{1,0:T(8,128)(2,1)S(1)}, u32[]{:S(2)}, u32[]{:S(2)}) collective-permute-start(bf16[192,1536]{1,0:T(8,128)(2,1)} %get-tuple-element.17), channel_id=1, source_target_pairs={{0,1},{1,0},{2,3},{3,2},{4,5},{5,4},{6,7},{7,6},{8,9},{9,8},{10,11... | collective-permute-start | bytes 1769480 | tf_op jit(solution)/shard_map/ppermute | solution.py:354
  14.3 2.1 %all-to-all-done.got_ref = f32[4,8,1792]{2,1,0:T(8,128)S(1)} async-done(((f32[4,8,1792]{2,1,0:T(8,128)}), f32[4,8,1792]{2,1,0:T(8,128)S(1)}, u32[]{:S(2)}, u32[]{:S(2)}) %all-to-all-start) | async-done | bytes 229408 | tf_op jit(solution)/shard_map/all_to_all | solution.py:353
  16.4 0.7 copies.1
  17.1 16.4 %all-to-all-start.1 = ((bf16[64,2,768]{2,1,0:T(2,128)(2,1)}), bf16[64,2,768]{2,1,0:T(2,128)(2,1)S(1)}, u32[]{:S(2)}, u32[]{:S(2)}) async-start(bf16[64,2,768]{2,1,0:T(2,128)(2,1)} %get-tuple-element.19), calls=%async_computation.1 | async-start | bytes 393216 | tf_op jit(solution)/shard_map/all_to_all | solution.py:366
  33.5 0.0 copy-start
  33.5 0.0 copy-start.1
  33.5 0.0 collective-permute-done.their_rows_ref
  33.5 5.2 %collective-permute-start.1 = (f32[8,1536]{1,0:T(8,128)S(1)}, f32[8,1536]{1,0:T(8,128)S(1)}, u32[]{:S(2)}, u32[]{:S(2)}) collective-permute-start(f32[8,1536]{1,0:T(8,128)S(1)} %get-tuple-element.18), channel_id=1, source_target_pairs={{0,10},{1,11},{2,8},{3,9},{8,2},{9,3},{10,0},{11,1},{4,14},{5,15},... | collective-permute-start | bytes 147464 | tf_op jit(solution)/shard_map/ppermute | solution.py:372
  38.7 0.0 copy-done.2
  38.7 0.1 reshape.14.pos_ref
  38.8 5.0 %all-gather = f32[16,1536]{1,0:T(8,128)S(1)} all-gather(f32[8,1536]{1,0:T(8,128)S(1)} %get-tuple-element.18), channel_id=2, replica_groups=mesh['dp_0'=4,'dp_1'=8,'dp_2'=2,'dp_3'=2,'head_0'=2,'head_1'=2] {'dp_3'}, dimensions={0}, use_global_device_ids=true | all-gather | bytes 147456 | tf_op jit(solution)/shard_map/all_gather | solution.py:373
  43.8 0.0 collective-permute-done.1
  43.8 2.4 %all-gather.1 = f32[16,1536]{1,0:T(8,128)S(1)} all-gather(f32[8,1536]{1,0:T(8,128)S(1)} %collective-permute-done.1), channel_id=3, replica_groups=mesh['dp_0'=4,'dp_1'=8,'dp_2'=2,'dp_3'=2,'head_0'=2,'head_1'=2] {'dp_3'}, dimensions={0}, use_global_device_ids=true | all-gather | bytes 147456 | tf_op jit(solution)/shard_map/all_gather | solution.py:374
  46.2 0.0 all-to-all-done.1
  46.2 0.1 reshape.13.q_ref
  46.2 0.4 logits.1
  46.6 18.1 %all_to_all.20.stats_ref = f32[32,2,128]{2,1,0:T(2,128)S(1)} all-to-all(f32[32,2,128]{2,1,0:T(2,128)S(1)} %get-tuple-element.20), channel_id=1, replica_groups=mesh['dp_0'=4,'dp_1'=8,'dp_2'=2,'dp_3'=2,'head_0'=2,'head_1'=2] {'dp_0',..., dimensions={0} | all-to-all | bytes 65536 | tf_op jit(solution)/shard_map/all_to_all | solution.py:390
  64.7 0.3 slopes.1
  65.1 14.3 %all_to_all.21.grads_ref = bf16[8,8,1664]{2,1,0:T(8,128)(2,1)S(1)} all-to-all(bf16[8,8,1664]{2,1,0:T(8,128)(2,1)S(1)} %slopes.1), channel_id=1, replica_groups=mesh['dp_0'=4,'dp_1'=8,'dp_2'=2,'dp_3'=2,'head_0'=2,'head_1'=2] {'dp_3',..., dimensions={0} | all-to-all | bytes 425984 | tf_op jit(solution)/shard_map/all_to_all | solution.py:400
  79.4 0.0 copy-done.1
  79.4 2.0 %slopes_of_values.1 = (bf16[64,512]{1,0:T(8,128)(2,1)}, f32[1,1]{1,0:T(1,128)}) custom-call(s32[1,8]{1,0:T(1,128)S(1)} %copy-done.1, bf16[8,8,1664]{2,1,0:T(8,128)(2,1)S(1)} %all_to_all.21.grads_ref, bf16[384,1536]{1,0:T(8,128)(2,1)S(1)} %copy-done, bf16[192,1536]{1,0:T(8,128)(2,1)S(1)} %collective-permute-done.their_rows_ref, ...), custom_call_target="tpu_custom_call" | custom-call | tf_op jit(solution)/shard_map/slopes_of_values/pallas_call | solution.py:402
  (1 shorter events, 0.0 us)
Async XLA Ops:
  0.6 38.0 %copy-start.2 = (s32[512]{0:T(512)S(1)}, s32[512]{0:T(512)}, u32[]{:S(2)}) copy-start(s32[512]{0:T(512)} %param.13) | copy-start | bytes 6148
  5.5 10.9 %all-to-all-start = ((f32[4,8,1792]{2,1,0:T(8,128)}), f32[4,8,1792]{2,1,0:T(8,128)S(1)}, u32[]{:S(2)}, u32[]{:S(2)}) async-start(f32[4,8,1792]{2,1,0:T(8,128)} %get-tuple-element.15), calls=%async_computation | async-start | bytes 458752 | tf_op jit(solution)/shard_map/all_to_all | solution.py:353
  10.9 22.6 %collective-permute-start = (bf16[192,1536]{1,0:T(8,128)(2,1)}, bf16[192,1536]{1,0:T(8,128)(2,1)S(1)}, u32[]{:S(2)}, u32[]{:S(2)}) collective-permute-start(bf16[192,1536]{1,0:T(8,128)(2,1)} %get-tuple-element.17), channel_id=1, source_target_pairs={{0,1},{1,0},{2,3},{3,2},{4,5},{5,4},{6,7},{7,6},{8,9},{9,8},{10,11... | collective-permute-start | bytes 1769480 | tf_op jit(solution)/shard_map/ppermute | solution.py:354
  17.1 29.1 %all-to-all-start.1 = ((bf16[64,2,768]{2,1,0:T(2,128)(2,1)}), bf16[64,2,768]{2,1,0:T(2,128)(2,1)S(1)}, u32[]{:S(2)}, u32[]{:S(2)}) async-start(bf16[64,2,768]{2,1,0:T(2,128)(2,1)} %get-tuple-element.19), calls=%async_computation.1 | async-start | bytes 393216 | tf_op jit(solution)/shard_map/all_to_all | solution.py:366
  33.5 45.9 %copy-start = (bf16[384,1536]{1,0:T(8,128)(2,1)S(1)}, bf16[384,1536]{1,0:T(8,128)(2,1)}, u32[]{:S(2)}) copy-start(bf16[384,1536]{1,0:T(8,128)(2,1)} %my_rows_ref.1) | copy-start | bytes 3538948
  33.5 45.9 %copy-start.1 = (s32[1,8]{1,0:T(1,128)S(1)}, s32[1,8]{1,0:T(1,128)}, u32[]{:S(2)}) copy-start(s32[1,8]{1,0:T(1,128)} %lens_ref.3) | copy-start | bytes 100
  33.5 10.3 %collective-permute-start.1 = (f32[8,1536]{1,0:T(8,128)S(1)}, f32[8,1536]{1,0:T(8,128)S(1)}, u32[]{:S(2)}, u32[]{:S(2)}) collective-permute-start(f32[8,1536]{1,0:T(8,128)S(1)} %get-tuple-element.18), channel_id=1, source_target_pairs={{0,10},{1,11},{2,8},{3,9},{8,2},{9,3},{10,0},{11,1},{4,14},{5,15},... | collective-permute-start | bytes 147464 | tf_op jit(solution)/shard_map/ppermute | solution.py:372

commit v7 on v6

--- a/solution.py
+++ b/solution.py
@@ -21,7 +21,6 @@
 NT = (((1,), (1,)), ((), ()))
 TN = (((0,), (0,)), ((), ()))
 VMEM = pl.BlockSpec(memory_space=pltpu.VMEM)
-HBM = pl.BlockSpec(memory_space=pl.ANY)
 SMEM = pl.BlockSpec(memory_space=pltpu.SMEM)
 
 
@@ -79,17 +78,8 @@
 
 
 def attend_kernel(
-    lens_ref, q_hbm, k_hbm, v_hbm, w_hbm, queries_ref, sent_ref, rows_ref,
-    q_ref, k_ref, v_ref, w_ref, total, done,
+    lens_ref, q_ref, k_ref, v_ref, w_ref, queries_ref, sent_ref, rows_ref, total
 ):
-    copies = [
-        pltpu.make_async_copy(source, target, done.at[i])
-        for i, (source, target) in enumerate(
-            ((q_hbm, q_ref), (k_hbm, k_ref), (v_hbm, v_ref), (w_hbm, w_ref))
-        )
-    ]
-    for copy in copies:
-        copy.start()
     seq_len, width = q_ref.shape
     heads = width // HD
     docs = lens_ref.shape[1]
@@ -99,11 +89,7 @@
     total[...] = jnp.zeros_like(total)
     block = min(128, seq_len)
     factor = math.log2(math.e) / math.sqrt(HD)
-    lane = lax.broadcasted_iota(jnp.int32, (heads * block, HD), 1)
-    head = lax.broadcasted_iota(jnp.int32, (heads * block, HD), 0) // block
-    pick = (lane == head).astype(jnp.bfloat16)
-    copies[0].wait()
-    copies[1].wait()
+    lane = lax.broadcasted_iota(jnp.int32, (block, HD), 1)
     for first in range(0, seq_len, block):
         low = max(0, (first - LONGEST + 1) // block * block)
         span = first + block - low
@@ -111,31 +97,27 @@
         k_place = low + lax.broadcasted_iota(jnp.int32, (span, block), 0)
         q_place = first + lax.broadcasted_iota(jnp.int32, (span, block), 1)
         allowed = (k_place <= q_place) & (k_place >= start[:, first : first + block])
-        q_block = jnp.concatenate(
-            [q_ref[first : first + block, h * HD : (h + 1) * HD] for h in range(heads)], axis=0
-        )
-        scores = lax.dot_general(k_block, q_block, NT, preferred_element_type=jnp.float32)
-        probs = []
         for h in range(heads):
-            mine = jnp.where(allowed, scores[:, h * block : (h + 1) * block], -1e30)
-            top = jnp.max(mine, axis=0, keepdims=True)
-            expo = jnp.exp2((mine - top) * factor)
+            q_block = q_ref[first : first + block, h * HD : (h + 1) * HD]
+            scores = lax.dot_general(k_block, q_block, NT, preferred_element_type=jnp.float32)
+            scores = jnp.where(allowed, scores, -1e30)
+            top = jnp.max(scores, axis=0, keepdims=True)
+            expo = jnp.exp2((scores - top) * factor)
             norm = 1.0 / jnp.sum(expo, axis=0, keepdims=True)
-            probs.append((expo * norm).astype(jnp.bfloat16))
-        total[low : first + block, :] += jnp.dot(
-            jnp.concatenate(probs, axis=1), pick, preferred_element_type=jnp.float32
-        )
+            probs = (expo * norm).astype(jnp.bfloat16)
+            pick = (lane == h).astype(jnp.bfloat16)
+            total[low : first + block, :] += jnp.dot(
+                probs, pick, preferred_element_type=jnp.float32
+            )
     by_head = total[...].T
     member = lax.broadcasted_iota(jnp.int32, (docs, seq_len), 0) == seg
     shares = jnp.concatenate(
         [jnp.where(member, by_head[h : h + 1, :], 0.0) for h in range(heads)], axis=0
     )
-    copies[2].wait()
     sums = exact_dot(shares, v_ref[:, columns], (((1,), (0,)), ((), ())))
     pooled = jnp.concatenate(
         [sums[h * docs : (h + 1) * docs] for h in range(heads)], axis=1
     ) / lens_column(lens_ref, docs)
-    copies[3].wait()
     emb = exact_dot(pooled, w_ref[...], (((1,), (0,)), ((), ())))
     features = emb.shape[1]
     queries = queries_ref[...].astype(jnp.float32)
@@ -157,8 +139,8 @@
         )
     half = HD // 2
     for h in range(heads):
-        wanted = pl.ds(pl.multiple_of(h * HD + (1 - lax.axis_index(HEAD[1])) * half, half), half)
-        rows_ref[h * half : (h + 1) * half, :] = w_ref[wanted, :]
+        place = pl.multiple_of(h * HD + (1 - lax.axis_index(HEAD[1])) * half, half)
+        rows_ref[h * half : (h + 1) * half, :] = w_ref[pl.ds(place, half), :]
 
 
 def copies_kernel(got_ref, out_ref, whole_ref):
@@ -218,10 +200,11 @@
 
 
 def logits_kernel(
-    emb_ref, other_ref, q_ref, pos_ref, out_ref, logits_ref, chosen_ref, unit_ref, rnorm_ref
+    emb_ref, q_ref, pos_ref, out_ref, logits_ref, chosen_ref, unit_ref, rnorm_ref
 ):
     docs = logits_ref.shape[0]
-    emb = [ref[k] for ref in (emb_ref, other_ref) for k in range(ref.shape[0])]
+    me = lax.axis_index(DP[2])
+    emb = [emb_ref[core, upper] for upper in (me, 1 - me) for core in range(emb_ref.shape[0])]
     emb = jnp.concatenate(emb, axis=0)
     rnorm = 1.0 / jnp.sqrt(jnp.sum(emb * emb, axis=1, keepdims=True) + 1e-06)
     unit = emb * rnorm
@@ -340,13 +323,9 @@
             jax.ShapeDtypeStruct((split, docs, features + seq_len // 2), f32),
             jax.ShapeDtypeStruct((heads * half, features), bf16),
         ),
-        in_specs=[SMEM] + [HBM] * 4 + [VMEM],
+        in_specs=[SMEM] + [VMEM] * 5,
         out_specs=(VMEM, VMEM),
-        scratch_shapes=[
-            *(pltpu.VMEM(a.shape, a.dtype) for a in (attn_queries, keys, values, out_weight)),
-            pltpu.VMEM((seq_len, HD), f32),
-            pltpu.SemaphoreType.DMA((4,)),
-        ],
+        scratch_shapes=[pltpu.VMEM((seq_len, HD), f32)],
         compiler_params=big,
         name="attend",
     )(lengths, attn_queries, keys, values, out_weight, queries)
@@ -368,10 +347,9 @@
     pos = positives.reshape(others, cores * split)
     whole, their_rows = lax.optimization_barrier((whole, their_rows))
     uppers = lax.axis_size(DP[2])
-    across = [(i, i ^ (split + 2)) for i in range(uppers * split)]
-    other = lax.ppermute(whole, (DP[2], *HEAD), across)
-    pair = lax.all_gather(whole, DP[3])
-    other = lax.all_gather(other, DP[3])
+    across = [[i, i ^ (split + 2)] for i in range(split)]
+    whole = lax.all_gather(whole, (DP[2], *HEAD), axis_index_groups=across)
+    whole = lax.all_gather(whole, DP[3])
 
     stats, logits, chosen, unit, rnorm = pl.pallas_call(
         logits_kernel,
@@ -382,11 +360,11 @@
             jax.ShapeDtypeStruct((cores * docs, features), f32),
             jax.ShapeDtypeStruct((cores * docs, HD), f32),
         ),
-        in_specs=[VMEM] * 4,
+        in_specs=[VMEM] * 3,
         out_specs=(VMEM,) * 5,
         compiler_params=small,
         name="logits",
-    )(pair, other, every, pos)
+    )(whole, every, pos)
     stats = lax.all_to_all(stats, DP[:2], 0, 0, tiled=True)
 
     grads = pl.pallas_call(

time: 81.8 us -> 79.8 us (0.976)
  starting transfers between devices: 30.3 us -> 25.2 us
  blocking collectives: 39.8 us -> 43.5 us
  Pallas kernels: 8.23 us -> 7.39 us
    ppermute x1 -> x0, starting transfers between devices: 5.16 us -> none  [per_device(): other = lax.ppermute(whole, (DP[2], *HEAD), across)]
    all_gather x2, blocking collectives: 7.37 us -> 11.5 us  [the longest x1 6.39 us: per_device(): whole = lax.all_gather(whole, (DP[2], *HEAD), axis_index_groups=across)]
    pallas_call x1, Pallas kernels: 4.85 us -> 4 us  [per_device(): pl.pallas_call(attend_kernel, out_shape=(jax.ShapeDtypeStruct((split, doc...]
  transfers between devices with their start and end apart: 4 -> 3, of which waited for: 1 -> 2; matrix products, arithmetic and copies ran while one was open for 0% -> 0% of each run, Pallas kernels for 1% -> 1%
where the time goes in v7:
time: 79.8 us; the launch traced here: 79.4 us
  blocking collectives  43.5 us (55%)
  starting transfers between devices  25.2 us (32%)
  Pallas kernels  7.39 us (9%)
  waiting for transfers between devices  2.5 us (3%)
    all_to_all x1, blocking collectives, per_device(): stats = lax.all_to_all(stats, DP[:2], 0, 0, tiled=True)  17.6 us
    all_to_all x1, starting transfers between devices, per_device(): lax.all_to_all(rows, line, 0, 0, axis_index_groups=groups, tiled=True)  16.4 us
    all_to_all x1, blocking collectives, per_device(): grads = lax.all_to_all(grads, (DP[3], *HEAD), 0, 0, tiled=True)  14.4 us
    all_gather x1, blocking collectives, per_device(): whole = lax.all_gather(whole, (DP[2], *HEAD), axis_index_groups=across)  6.39 us
    all_to_all x1, starting transfers between devices, per_device(): got = lax.all_to_all(partial, HEAD, 0, 0, tiled=True)  5.42 us
    all_gather x1, blocking collectives, per_device(): whole = lax.all_gather(whole, DP[3])  5.1 us
    pallas_call x1, Pallas kernels, per_device(): pl.pallas_call(attend_kernel, out_shape=(jax.ShapeDtypeStruct((split, doc...  4 us
    ppermute x1, starting transfers between devices, per_device(): their_rows = lax.ppermute(wanted, HEAD, [(i, i ^ 1) for i in range(split)])  3.36 us
  transfers between devices with their start and end apart: 3, of which 2 were waited for; matrix products, arithmetic and copies ran while one was open for 0% of the time, Pallas kernels for 1%

profile of v7, /device:TPU:1, one launch (start us, length us, event | category | flops | bytes accessed | tf_op | source)
XLA Modules:
  0.0 79.4 jit_solution(124925215814694055)
XLA Ops:
  0.6 0.0 copy-start.2
  0.6 4.0 %attend.1 = (f32[4,8,1792]{2,1,0:T(8,128)}, bf16[192,1536]{1,0:T(8,128)(2,1)}) custom-call(s32[1,8]{1,0:T(1,128)} %lens_ref.3, bf16[512,384]{1,0:T(8,128)(2,1)} %q_ref.1, bf16[512,256]{1,0:T(8,128)(2,1)} %k_ref.1, bf16[512,256]{1,0:T(8,128)(2,1)} %v_ref.1, bf16[384,1536]{1,0:T(8,128)(2,1)} %my_rows_ref.1, bf16[4,384]{1,0:T(4,128)(2,1)} %queries_ref.1), custom_call_target="tpu_custom_call" | custom-call | tf_op jit(solution)/shard_map/attend/pallas_call | solution.py:320
  4.6 5.4 %all-to-all-start = ((f32[4,8,1792]{2,1,0:T(8,128)}), f32[4,8,1792]{2,1,0:T(8,128)S(1)}, u32[]{:S(2)}, u32[]{:S(2)}) async-start(f32[4,8,1792]{2,1,0:T(8,128)} %get-tuple-element.15), calls=%async_computation | async-start | bytes 458752 | tf_op jit(solution)/shard_map/all_to_all | solution.py:332
  10.1 3.4 %collective-permute-start = (bf16[192,1536]{1,0:T(8,128)(2,1)}, bf16[192,1536]{1,0:T(8,128)(2,1)S(1)}, u32[]{:S(2)}, u32[]{:S(2)}) collective-permute-start(bf16[192,1536]{1,0:T(8,128)(2,1)} %get-tuple-element.17), channel_id=1, source_target_pairs={{0,1},{1,0},{2,3},{3,2},{4,5},{5,4},{6,7},{7,6},{8,9},{9,8},{10,11... | collective-permute-start | bytes 1769480 | tf_op jit(solution)/shard_map/ppermute | solution.py:333
  13.4 2.1 %all-to-all-done.got_ref = f32[4,8,1792]{2,1,0:T(8,128)S(1)} async-done(((f32[4,8,1792]{2,1,0:T(8,128)}), f32[4,8,1792]{2,1,0:T(8,128)S(1)}, u32[]{:S(2)}, u32[]{:S(2)}) %all-to-all-start) | async-done | bytes 229408 | tf_op jit(solution)/shard_map/all_to_all | solution.py:332
  15.5 0.7 copies.1
  16.2 16.4 %all-to-all-start.1 = ((bf16[64,2,768]{2,1,0:T(2,128)(2,1)}), bf16[64,2,768]{2,1,0:T(2,128)(2,1)S(1)}, u32[]{:S(2)}, u32[]{:S(2)}) async-start(bf16[64,2,768]{2,1,0:T(2,128)(2,1)} %get-tuple-element.19), calls=%async_computation.1 | async-start | bytes 393216 | tf_op jit(solution)/shard_map/all_to_all | solution.py:345
  32.6 0.0 copy-done.2
  32.6 0.0 copy-start
  32.6 0.0 copy-start.1
  32.6 0.1 reshape.14.pos_ref
  32.7 0.0 collective-permute-done.their_rows_ref
  32.7 6.4 %all-gather = f32[16,1536]{1,0:T(8,128)S(1)} all-gather(f32[8,1536]{1,0:T(8,128)S(1)} %get-tuple-element.18), channel_id=2, replica_groups={{0,10},{1,11},{2,8},{3,9},{4,14},{5,15},{6,12},{7,13},{16,26},{17,27},{..., dimensions={0}, use_global_device_ids=true | all-gather | bytes 147456 | tf_op jit(solution)/shard_map/all_gather | solution.py:351
  39.1 5.1 %all-gather.1 = f32[4,8,1536]{2,1,0:T(8,128)S(1)} all-gather(f32[2,8,1536]{2,1,0:T(8,128)S(1)} %bitcast.5), channel_id=3, replica_groups=mesh['dp_0'=4,'dp_1'=8,'dp_2'=2,'dp_3'=2,'head_0'=2,'head_1'=2] {'dp_3'}, dimensions={0}, use_global_device_ids=true | all-gather | bytes 294912 | tf_op jit(solution)/shard_map/all_gather | solution.py:352
  44.2 0.4 all-to-all-done.1
  44.6 0.1 reshape.13.q_ref
  44.7 0.4 logits.1
  45.1 17.6 %all_to_all.20.stats_ref = f32[32,2,128]{2,1,0:T(2,128)S(1)} all-to-all(f32[32,2,128]{2,1,0:T(2,128)S(1)} %get-tuple-element.20), channel_id=1, replica_groups=mesh['dp_0'=4,'dp_1'=8,'dp_2'=2,'dp_3'=2,'head_0'=2,'head_1'=2] {'dp_0',..., dimensions={0} | all-to-all | bytes 65536 | tf_op jit(solution)/shard_map/all_to_all | solution.py:368
  62.7 0.3 slopes.1
  63.1 14.4 %all_to_all.21.grads_ref = bf16[8,8,1664]{2,1,0:T(8,128)(2,1)S(1)} all-to-all(bf16[8,8,1664]{2,1,0:T(8,128)(2,1)S(1)} %slopes.1), channel_id=1, replica_groups=mesh['dp_0'=4,'dp_1'=8,'dp_2'=2,'dp_3'=2,'head_0'=2,'head_1'=2] {'dp_3',..., dimensions={0} | all-to-all | bytes 425984 | tf_op jit(solution)/shard_map/all_to_all | solution.py:378
  77.5 0.0 copy-done
  77.5 0.0 copy-done.1
  77.5 1.9 %slopes_of_values.1 = (bf16[64,512]{1,0:T(8,128)(2,1)}, f32[1,1]{1,0:T(1,128)}) custom-call(s32[1,8]{1,0:T(1,128)S(1)} %copy-done.1, bf16[8,8,1664]{2,1,0:T(8,128)(2,1)S(1)} %all_to_all.21.grads_ref, bf16[384,1536]{1,0:T(8,128)(2,1)S(1)} %copy-done, bf16[192,1536]{1,0:T(8,128)(2,1)S(1)} %collective-permute-done.their_rows_ref, ...), custom_call_target="tpu_custom_call" | custom-call | tf_op jit(solution)/shard_map/slopes_of_values/pallas_call | solution.py:380
Async XLA Ops:
  0.6 32.0 %copy-start.2 = (s32[512]{0:T(512)S(1)}, s32[512]{0:T(512)}, u32[]{:S(2)}) copy-start(s32[512]{0:T(512)} %param.13) | copy-start | bytes 6148
  4.6 10.9 %all-to-all-start = ((f32[4,8,1792]{2,1,0:T(8,128)}), f32[4,8,1792]{2,1,0:T(8,128)S(1)}, u32[]{:S(2)}, u32[]{:S(2)}) async-start(f32[4,8,1792]{2,1,0:T(8,128)} %get-tuple-element.15), calls=%async_computation | async-start | bytes 458752 | tf_op jit(solution)/shard_map/all_to_all | solution.py:332
  10.1 22.7 %collective-permute-start = (bf16[192,1536]{1,0:T(8,128)(2,1)}, bf16[192,1536]{1,0:T(8,128)(2,1)S(1)}, u32[]{:S(2)}, u32[]{:S(2)}) collective-permute-start(bf16[192,1536]{1,0:T(8,128)(2,1)} %get-tuple-element.17), channel_id=1, source_target_pairs={{0,1},{1,0},{2,3},{3,2},{4,5},{5,4},{6,7},{7,6},{8,9},{9,8},{10,11... | collective-permute-start | bytes 1769480 | tf_op jit(solution)/shard_map/ppermute | solution.py:333
  16.2 28.4 %all-to-all-start.1 = ((bf16[64,2,768]{2,1,0:T(2,128)(2,1)}), bf16[64,2,768]{2,1,0:T(2,128)(2,1)S(1)}, u32[]{:S(2)}, u32[]{:S(2)}) async-start(bf16[64,2,768]{2,1,0:T(2,128)(2,1)} %get-tuple-element.19), calls=%async_computation.1 | async-start | bytes 393216 | tf_op jit(solution)/shard_map/all_to_all | solution.py:345
  32.6 44.8 %copy-start = (bf16[384,1536]{1,0:T(8,128)(2,1)S(1)}, bf16[384,1536]{1,0:T(8,128)(2,1)}, u32[]{:S(2)}) copy-start(bf16[384,1536]{1,0:T(8,128)(2,1)} %my_rows_ref.1) | copy-start | bytes 3538948
  32.6 44.8 %copy-start.1 = (s32[1,8]{1,0:T(1,128)S(1)}, s32[1,8]{1,0:T(1,128)}, u32[]{:S(2)}) copy-start(s32[1,8]{1,0:T(1,128)} %lens_ref.3) | copy-start | bytes 100

commit v8 on v7

--- a/solution.py
+++ b/solution.py
@@ -199,16 +199,19 @@
     return (positive == owned.astype(jnp.float32)).astype(jnp.float32)
 
 
-def logits_kernel(
-    emb_ref, q_ref, pos_ref, out_ref, logits_ref, chosen_ref, unit_ref, rnorm_ref
-):
+def unit_kernel(emb_ref, unit_ref, rnorm_ref, rounded_ref):
+    emb = jnp.concatenate([emb_ref[core] for core in range(emb_ref.shape[0])], axis=0)
+    rnorm = 1.0 / jnp.sqrt(jnp.sum(emb * emb, axis=1, keepdims=True) + 1e-06)
+    unit = emb * rnorm
+    unit_ref[...] = unit
+    rnorm_ref[...] = jnp.broadcast_to(rnorm, rnorm_ref.shape)
+    rounded_ref[...] = unit.astype(jnp.bfloat16)
+
+
+def logits_kernel(units_ref, q_ref, pos_ref, out_ref, logits_ref, chosen_ref):
     docs = logits_ref.shape[0]
     me = lax.axis_index(DP[2])
-    emb = [emb_ref[core, upper] for upper in (me, 1 - me) for core in range(emb_ref.shape[0])]
-    emb = jnp.concatenate(emb, axis=0)
-    rnorm = 1.0 / jnp.sqrt(jnp.sum(emb * emb, axis=1, keepdims=True) + 1e-06)
-    unit = emb * rnorm
-    logits = pair_logits(unit.astype(jnp.bfloat16), q_ref)
+    logits = pair_logits(jnp.concatenate([units_ref[me], units_ref[1 - me]], axis=0), q_ref)
     chosen = positive_mask(pos_ref, docs)
     top = jnp.max(logits, axis=0, keepdims=True)
     expo = jnp.exp(logits - top)
@@ -223,8 +226,6 @@
     )
     logits_ref[...] = logits[:docs]
     chosen_ref[...] = chosen[:docs]
-    unit_ref[...] = unit[:docs]
-    rnorm_ref[...] = jnp.broadcast_to(rnorm[:docs], rnorm_ref.shape)
 
 
 def slopes_kernel(stats_ref, logits_ref, chosen_ref, unit_ref, rnorm_ref, q_ref, out_ref):
@@ -348,23 +349,33 @@
     whole, their_rows = lax.optimization_barrier((whole, their_rows))
     uppers = lax.axis_size(DP[2])
     across = [[i, i ^ (split + 2)] for i in range(split)]
-    whole = lax.all_gather(whole, (DP[2], *HEAD), axis_index_groups=across)
     whole = lax.all_gather(whole, DP[3])
-
-    stats, logits, chosen, unit, rnorm = pl.pallas_call(
+    unit, rnorm, rounded = pl.pallas_call(
+        unit_kernel,
+        out_shape=(
+            jax.ShapeDtypeStruct((cores * docs, features), f32),
+            jax.ShapeDtypeStruct((cores * docs, HD), f32),
+            jax.ShapeDtypeStruct((cores * docs, features), bf16),
+        ),
+        in_specs=[VMEM],
+        out_specs=(VMEM,) * 3,
+        compiler_params=small,
+        name="unit",
+    )(whole)
+    units = lax.all_gather(rounded, (DP[2], *HEAD), axis_index_groups=across)
+
+    stats, logits, chosen = pl.pallas_call(
         logits_kernel,
         out_shape=(
             jax.ShapeDtypeStruct((others // uppers, 2, lanes), f32),
             jax.ShapeDtypeStruct((cores * docs, lanes), f32),
             jax.ShapeDtypeStruct((cores * docs, lanes), f32),
-            jax.ShapeDtypeStruct((cores * docs, features), f32),
-            jax.ShapeDtypeStruct((cores * docs, HD), f32),
         ),
         in_specs=[VMEM] * 3,
-        out_specs=(VMEM,) * 5,
+        out_specs=(VMEM,) * 3,
         compiler_params=small,
         name="logits",
-    )(whole, every, pos)
+    )(units, every, pos)
     stats = lax.all_to_all(stats, DP[:2], 0, 0, tiled=True)
 
     grads = pl.pallas_call(

time: 79.8 us -> 79.8 us (level)
  blocking collectives: 43.5 us -> 42.6 us
where the time goes in v8:
time: 79.8 us; the launch traced here: 79.4 us
  blocking collectives  42.6 us (53%)
  starting transfers between devices  25.2 us (32%)
  Pallas kernels  7.43 us (9%)
  waiting for transfers between devices  3.28 us (4%)
    all_to_all x1, blocking collectives, per_device(): stats = lax.all_to_all(stats, DP[:2], 0, 0, tiled=True)  16.9 us
    all_to_all x1, starting transfers between devices, per_device(): lax.all_to_all(rows, line, 0, 0, axis_index_groups=groups, tiled=True)  16.4 us
    all_to_all x1, blocking collectives, per_device(): grads = lax.all_to_all(grads, (DP[3], *HEAD), 0, 0, tiled=True)  15.1 us
    all_gather x1, blocking collectives, per_device(): units = lax.all_gather(rounded, (DP[2], *HEAD), axis_index_groups=across)  6.02 us
    all_to_all x1, starting transfers between devices, per_device(): got = lax.all_to_all(partial, HEAD, 0, 0, tiled=True)  5.42 us
    all_gather x1, blocking collectives, per_device(): whole = lax.all_gather(whole, DP[3])  4.55 us
    pallas_call x1, Pallas kernels, per_device(): pl.pallas_call(attend_kernel, out_shape=(jax.ShapeDtypeStruct((split, doc...  4.02 us
    ppermute x1, starting transfers between devices, per_device(): their_rows = lax.ppermute(wanted, HEAD, [(i, i ^ 1) for i in range(split)])  3.36 us
  transfers between devices with their start and end apart: 3, of which 2 were waited for; matrix products, arithmetic and copies ran while one was open for 0% of the time, Pallas kernels for 1%

profile of v8, /device:TPU:1, one launch (start us, length us, event | category | flops | bytes accessed | tf_op | source)
XLA Modules:
  0.0 79.4 jit_solution(5310508672490369266)
XLA Ops:
  0.6 0.0 copy-start.2
  0.6 4.0 %attend.1 = (f32[4,8,1792]{2,1,0:T(8,128)}, bf16[192,1536]{1,0:T(8,128)(2,1)}) custom-call(s32[1,8]{1,0:T(1,128)} %lens_ref.3, bf16[512,384]{1,0:T(8,128)(2,1)} %q_ref.1, bf16[512,256]{1,0:T(8,128)(2,1)} %k_ref.1, bf16[512,256]{1,0:T(8,128)(2,1)} %v_ref.1, bf16[384,1536]{1,0:T(8,128)(2,1)} %my_rows_ref.1, bf16[4,384]{1,0:T(4,128)(2,1)} %queries_ref.1), custom_call_target="tpu_custom_call" | custom-call | tf_op jit(solution)/shard_map/attend/pallas_call | solution.py:321
  4.7 5.4 %all-to-all-start = ((f32[4,8,1792]{2,1,0:T(8,128)}), f32[4,8,1792]{2,1,0:T(8,128)S(1)}, u32[]{:S(2)}, u32[]{:S(2)}) async-start(f32[4,8,1792]{2,1,0:T(8,128)} %get-tuple-element.16), calls=%async_computation | async-start | bytes 458752 | tf_op jit(solution)/shard_map/all_to_all | solution.py:333
  10.1 3.4 %collective-permute-start = (bf16[192,1536]{1,0:T(8,128)(2,1)}, bf16[192,1536]{1,0:T(8,128)(2,1)S(1)}, u32[]{:S(2)}, u32[]{:S(2)}) collective-permute-start(bf16[192,1536]{1,0:T(8,128)(2,1)} %get-tuple-element.18), channel_id=1, source_target_pairs={{0,1},{1,0},{2,3},{3,2},{4,5},{5,4},{6,7},{7,6},{8,9},{9,8},{10,11... | collective-permute-start | bytes 1769480 | tf_op jit(solution)/shard_map/ppermute | solution.py:334
  13.4 2.1 %all-to-all-done.got_ref = f32[4,8,1792]{2,1,0:T(8,128)S(1)} async-done(((f32[4,8,1792]{2,1,0:T(8,128)}), f32[4,8,1792]{2,1,0:T(8,128)S(1)}, u32[]{:S(2)}, u32[]{:S(2)}) %all-to-all-start) | async-done | bytes 229408 | tf_op jit(solution)/shard_map/all_to_all | solution.py:333
  15.5 0.7 copies.1
  16.2 16.4 %all-to-all-start.1 = ((bf16[64,2,768]{2,1,0:T(2,128)(2,1)}), bf16[64,2,768]{2,1,0:T(2,128)(2,1)S(1)}, u32[]{:S(2)}, u32[]{:S(2)}) async-start(bf16[64,2,768]{2,1,0:T(2,128)(2,1)} %get-tuple-element.21), calls=%async_computation.1 | async-start | bytes 393216 | tf_op jit(solution)/shard_map/all_to_all | solution.py:346
  32.6 0.0 copy-done.2
  32.6 0.0 copy-start
  32.7 0.0 copy-start.1
  32.7 0.1 reshape.14.pos_ref
  32.8 0.0 collective-permute-done.their_rows_ref
  32.8 4.5 %all-gather = f32[16,1536]{1,0:T(8,128)S(1)} all-gather(f32[8,1536]{1,0:T(8,128)S(1)} %get-tuple-element.19), channel_id=2, replica_groups=mesh['dp_0'=4,'dp_1'=8,'dp_2'=2,'dp_3'=2,'head_0'=2,'head_1'=2] {'dp_3'}, dimensions={0}, use_global_device_ids=true | all-gather | bytes 147456 | tf_op jit(solution)/shard_map/all_gather | solution.py:352
  37.3 0.1 unit.1
  37.4 6.0 %all-gather.1 = bf16[32,1536]{1,0:T(8,128)(2,1)S(1)} all-gather(bf16[16,1536]{1,0:T(8,128)(2,1)S(1)} %get-tuple-element.20), channel_id=3, replica_groups={{0,10},{1,11},{2,8},{3,9},{4,14},{5,15},{6,12},{7,13},{16,26},{17,27},{..., dimensions={0}, use_global_device_ids=true | all-gather | bytes 147456 | tf_op jit(solution)/shard_map/all_gather | solution.py:365
  43.5 1.2 %all-to-all-done.1 = bf16[64,2,768]{2,1,0:T(2,128)(2,1)S(1)} async-done(((bf16[64,2,768]{2,1,0:T(2,128)(2,1)}), bf16[64,2,768]{2,1,0:T(2,128)(2,1)S(1)}, u32[]{:S(2)}, u32[]{:S(2)}) %all-to-all-start.1) | async-done | bytes 196640 | tf_op jit(solution)/shard_map/all_to_all | solution.py:346
  44.6 0.1 reshape.13.q_ref
  44.7 0.3 logits.1
  45.1 16.9 %all_to_all.20.stats_ref = f32[32,2,128]{2,1,0:T(2,128)S(1)} all-to-all(f32[32,2,128]{2,1,0:T(2,128)S(1)} %get-tuple-element.22), channel_id=1, replica_groups=mesh['dp_0'=4,'dp_1'=8,'dp_2'=2,'dp_3'=2,'head_0'=2,'head_1'=2] {'dp_0',..., dimensions={0} | all-to-all | bytes 65536 | tf_op jit(solution)/shard_map/all_to_all | solution.py:379
  62.0 0.3 slopes.1
  62.3 15.1 %all_to_all.21.grads_ref = bf16[8,8,1664]{2,1,0:T(8,128)(2,1)S(1)} all-to-all(bf16[8,8,1664]{2,1,0:T(8,128)(2,1)S(1)} %slopes.1), channel_id=1, replica_groups=mesh['dp_0'=4,'dp_1'=8,'dp_2'=2,'dp_3'=2,'head_0'=2,'head_1'=2] {'dp_3',..., dimensions={0} | all-to-all | bytes 425984 | tf_op jit(solution)/shard_map/all_to_all | solution.py:389
  77.4 0.0 copy-done
  77.4 0.0 copy-done.1
  77.4 2.0 %slopes_of_values.1 = (bf16[64,512]{1,0:T(8,128)(2,1)}, f32[1,1]{1,0:T(1,128)}) custom-call(s32[1,8]{1,0:T(1,128)S(1)} %copy-done.1, bf16[8,8,1664]{2,1,0:T(8,128)(2,1)S(1)} %all_to_all.21.grads_ref, bf16[384,1536]{1,0:T(8,128)(2,1)S(1)} %copy-done, bf16[192,1536]{1,0:T(8,128)(2,1)S(1)} %collective-permute-done.their_rows_ref, ...), custom_call_target="tpu_custom_call" | custom-call | tf_op jit(solution)/shard_map/slopes_of_values/pallas_call | solution.py:391
Async XLA Ops:
  0.6 32.0 %copy-start.2 = (s32[512]{0:T(512)S(1)}, s32[512]{0:T(512)}, u32[]{:S(2)}) copy-start(s32[512]{0:T(512)} %param.13) | copy-start | bytes 6148
  4.7 10.9 %all-to-all-start = ((f32[4,8,1792]{2,1,0:T(8,128)}), f32[4,8,1792]{2,1,0:T(8,128)S(1)}, u32[]{:S(2)}, u32[]{:S(2)}) async-start(f32[4,8,1792]{2,1,0:T(8,128)} %get-tuple-element.16), calls=%async_computation | async-start | bytes 458752 | tf_op jit(solution)/shard_map/all_to_all | solution.py:333
  10.1 22.7 %collective-permute-start = (bf16[192,1536]{1,0:T(8,128)(2,1)}, bf16[192,1536]{1,0:T(8,128)(2,1)S(1)}, u32[]{:S(2)}, u32[]{:S(2)}) collective-permute-start(bf16[192,1536]{1,0:T(8,128)(2,1)} %get-tuple-element.18), channel_id=1, source_target_pairs={{0,1},{1,0},{2,3},{3,2},{4,5},{5,4},{6,7},{7,6},{8,9},{9,8},{10,11... | collective-permute-start | bytes 1769480 | tf_op jit(solution)/shard_map/ppermute | solution.py:334
  16.2 28.4 %all-to-all-start.1 = ((bf16[64,2,768]{2,1,0:T(2,128)(2,1)}), bf16[64,2,768]{2,1,0:T(2,128)(2,1)S(1)}, u32[]{:S(2)}, u32[]{:S(2)}) async-start(bf16[64,2,768]{2,1,0:T(2,128)(2,1)} %get-tuple-element.21), calls=%async_computation.1 | async-start | bytes 393216 | tf_op jit(solution)/shard_map/all_to_all | solution.py:346
  32.6 44.8 %copy-start = (bf16[384,1536]{1,0:T(8,128)(2,1)S(1)}, bf16[384,1536]{1,0:T(8,128)(2,1)}, u32[]{:S(2)}) copy-start(bf16[384,1536]{1,0:T(8,128)(2,1)} %my_rows_ref.1) | copy-start | bytes 3538948
  32.7 44.8 %copy-start.1 = (s32[1,8]{1,0:T(1,128)S(1)}, s32[1,8]{1,0:T(1,128)}, u32[]{:S(2)}) copy-start(s32[1,8]{1,0:T(1,128)} %lens_ref.3) | copy-start | bytes 100

commit v9 on v8

--- a/solution.py
+++ b/solution.py
@@ -78,7 +78,7 @@
 
 
 def attend_kernel(
-    lens_ref, q_ref, k_ref, v_ref, w_ref, queries_ref, sent_ref, rows_ref, total
+    lens_ref, q_ref, k_ref, v_ref, w_ref, queries_ref, sent_ref, sums_ref, rows_ref, total
 ):
     seq_len, width = q_ref.shape
     heads = width // HD
@@ -122,21 +122,22 @@
     features = emb.shape[1]
     queries = queries_ref[...].astype(jnp.float32)
     place = lax.broadcasted_iota(jnp.int32, queries.shape, 0)
-    middle = seq_len // 2
-    pad = jnp.zeros((1, 2 * middle - width), jnp.float32)
+    rest = jnp.zeros((docs - heads, HD), jnp.float32)
     for k in range(sent_ref.shape[0]):
         row = jnp.where(place == k ^ (2 * lax.axis_index(DP[2])), queries, 0.0)
         row = jnp.sum(row, axis=0, keepdims=True)
+        chunks = [row[:, c * HD : (c + 1) * HD] for c in range(heads)]
         sent_ref[k, :, :features] = emb
-        sent_ref[k, :, features:] = jnp.concatenate(
-            [
-                by_head[:heads, :middle],
-                by_head[:heads, middle:],
-                row[:, :middle],
-                jnp.concatenate([row[:, middle:], pad], axis=1),
-            ],
-            axis=0,
-        )
+        sent_ref[k, :, features:] = jnp.concatenate([*chunks, rest], axis=0)
+    sums_ref[...] = by_head[:docs]
+    left = jnp.concatenate([by_head[h : h + 1] for h in range(heads)], axis=1)
+    lines = []
+    for _ in range(3):
+        term = left.astype(jnp.bfloat16).astype(jnp.float32)
+        lines.append(term)
+        left = left - term
+    lines.append(jnp.zeros((13, features), jnp.float32))
+    rows_ref[heads * (HD // 2) :, :] = jnp.concatenate(lines, axis=0).astype(jnp.bfloat16)
     half = HD // 2
     for h in range(heads):
         place = pl.multiple_of(h * HD + (1 - lax.axis_index(HEAD[1])) * half, half)
@@ -147,13 +148,11 @@
     docs, features = whole_ref.shape
     split = got_ref.shape[0]
     width = features // split
-    place = 2 * (HEADS // split)
     parts = []
     for k in range(split):
-        line = got_ref[k, place:, features:]
-        middle = line.shape[1]
-        parts += [line[:1, :], line[1:, : width - middle]]
-    middle = split
+        line = got_ref[k, :, features:]
+        parts += [line[c : c + 1] for c in range(width // HD)]
+    middle = len(parts) // 2
     halves = [jnp.concatenate(parts[:middle], axis=1), jnp.concatenate(parts[middle:], axis=1)]
     both = jnp.concatenate(halves, axis=0).astype(jnp.bfloat16)
     out_ref[...] = jnp.broadcast_to(both[None], out_ref.shape)
@@ -257,7 +256,7 @@
         out_ref[k, :, features:] = losses.astype(jnp.bfloat16)
 
 
-def values_kernel(lens_ref, grads_ref, my_rows_ref, their_rows_ref, got_ref, out_ref, loss_ref):
+def values_kernel(lens_ref, grads_ref, my_rows_ref, their_rows_ref, sums_ref, out_ref, loss_ref):
     docs = lens_ref.shape[1]
     features = my_rows_ref.shape[1]
     seq_len = out_ref.shape[1]
@@ -271,31 +270,36 @@
     loss_ref[...] = jnp.sum(
         jnp.sum(grads[:3, features:], axis=0, keepdims=True), axis=1, keepdims=True
     ) / (grads_ref.shape[0] * lanes)
-    rows = [
-        my_rows_ref[pl.ds(pl.multiple_of(h * HD + low * half, half), half), :]
+    terms = three_terms(grads[:, :features])
+    lens = lens_column(lens_ref, docs)
+    slopes = []
+    for h in range(heads):
+        rows = my_rows_ref[pl.ds(pl.multiple_of(h * HD + low * half, half), half), :]
+        slopes.append(lax.dot_general(terms, rows, NT, preferred_element_type=jnp.float32))
+    for h in range(heads):
+        rows = their_rows_ref[h * half : (h + 1) * half, :]
+        slopes.append(lax.dot_general(terms, rows, NT, preferred_element_type=jnp.float32))
+    slopes = [(of_three(part) / lens * loss_scale).astype(jnp.bfloat16) for part in slopes]
+    seg, _ = document_of(lens_ref, docs, (1, seq_len), 1)
+    member = lax.broadcasted_iota(jnp.int32, (docs, seq_len), 0) == seg
+    mine = [jnp.where(member, sums_ref[h : h + 1], 0.0) for h in range(heads)]
+    lines = their_rows_ref[heads * half :, :].astype(jnp.float32)
+    theirs = [
+        jnp.where(member, lines[t : t + 1, h * seq_len : (h + 1) * seq_len], 0.0)
+        for t in range(3)
         for h in range(heads)
     ]
-    rows = jnp.concatenate([*rows, their_rows_ref[...]], axis=0)
-    terms = three_terms(grads[:, :features])
-    slopes = lax.dot_general(rows, terms, NT, preferred_element_type=jnp.float32)
-    slopes = slopes[:, :docs] + slopes[:, docs : 2 * docs] + slopes[:, 2 * docs :]
-    lane = lax.broadcasted_iota(jnp.int32, (1, docs), 1)
-    lens = jnp.zeros((1, docs), jnp.int32)
-    for j in range(docs):
-        lens = jnp.where(lane == j, lens_ref[0, j], lens)
-    slopes = (slopes / lens.astype(jnp.float32) * loss_scale).astype(jnp.bfloat16)
-    slopes = [slopes[h * half : (h + 1) * half] for h in range(2 * heads)]
-    seg, _ = document_of(lens_ref, docs, (1, seq_len), 1)
-    member = lax.broadcasted_iota(jnp.int32, (docs, seq_len), 0) == seg
-    me = lax.axis_index(HEAD)
-    shares = []
-    for owner in (me, me ^ 1):
-        sums = got_ref[owner, :, features:]
-        sums = jnp.concatenate([sums[:heads], sums[heads : 2 * heads]], axis=1)
-        shares += [jnp.where(member, sums[h : h + 1], 0.0) for h in range(heads)]
-    out = jnp.dot(
-        jnp.concatenate(slopes * 3, axis=1),
-        three_terms(jnp.concatenate(shares, axis=0)),
+    shares = jnp.concatenate(
+        [
+            three_terms(jnp.concatenate(mine, axis=0)),
+            jnp.concatenate(theirs, axis=0).astype(jnp.bfloat16),
+        ],
+        axis=0,
+    )
+    out = lax.dot_general(
+        jnp.concatenate(slopes[:heads] * 3 + slopes[heads:] * 3, axis=0),
+        shares,
+        TN,
         preferred_element_type=jnp.float32,
     )
     out_ref[...] = out.astype(jnp.bfloat16)
@@ -318,14 +322,15 @@
     line = (*DP[:3], *HEAD)
     groups = class_groups()
 
-    partial, wanted = pl.pallas_call(
+    partial, sums, wanted = pl.pallas_call(
         attend_kernel,
         out_shape=(
-            jax.ShapeDtypeStruct((split, docs, features + seq_len // 2), f32),
-            jax.ShapeDtypeStruct((heads * half, features), bf16),
+            jax.ShapeDtypeStruct((split, docs, features + HD), f32),
+            jax.ShapeDtypeStruct((docs, seq_len), f32),
+            jax.ShapeDtypeStruct((heads * half + 16, features), bf16),
         ),
         in_specs=[SMEM] + [VMEM] * 5,
-        out_specs=(VMEM, VMEM),
+        out_specs=(VMEM,) * 3,
         scratch_shapes=[pltpu.VMEM((seq_len, HD), f32)],
         compiler_params=big,
         name="attend",
@@ -398,7 +403,7 @@
         out_specs=(VMEM, VMEM),
         compiler_params=small,
         name="slopes_of_values",
-    )(lengths, grads, out_weight, their_rows, got)
+    )(lengths, grads, out_weight, their_rows, sums)
     return d_values.T, loss.reshape(())
 
 

time: 79.8 us -> 79.4 us (level)
  blocking collectives: 42.6 us -> 41.3 us
  waiting for transfers between devices: 3.28 us -> 4.47 us
    all_to_all x1, waiting for transfers between devices: 1.19 us -> 2.52 us  [per_device(): lax.all_to_all(rows, line, 0, 0, axis_index_groups=groups, tiled=True)]
    all_to_all x1, blocking collectives: 15.1 us -> 14.2 us  [per_device(): grads = lax.all_to_all(grads, (DP[3], *HEAD), 0, 0, tiled=True)]
where the time goes in v9:
time: 79.4 us; the launch traced here: 79 us
  blocking collectives  41.3 us (52%)
  starting transfers between devices  25.1 us (32%)
  Pallas kernels  7.29 us (9%)
  waiting for transfers between devices  4.47 us (6%)
    all_to_all x1, blocking collectives, per_device(): stats = lax.all_to_all(stats, DP[:2], 0, 0, tiled=True)  16.4 us
    all_to_all x1, starting transfers between devices, per_device(): lax.all_to_all(rows, line, 0, 0, axis_index_groups=groups, tiled=True)  16.3 us
    all_to_all x1, blocking collectives, per_device(): grads = lax.all_to_all(grads, (DP[3], *HEAD), 0, 0, tiled=True)  14.2 us
    all_gather x1, blocking collectives, per_device(): units = lax.all_gather(rounded, (DP[2], *HEAD), axis_index_groups=across)  6.02 us
    all_to_all x1, starting transfers between devices, per_device(): got = lax.all_to_all(partial, HEAD, 0, 0, tiled=True)  5.43 us
    all_gather x1, blocking collectives, per_device(): whole = lax.all_gather(whole, DP[3])  4.63 us
    pallas_call x1, Pallas kernels, per_device(): pl.pallas_call(attend_kernel, out_shape=(jax.ShapeDtypeStruct((split, doc...  3.98 us
    ppermute x1, starting transfers between devices, per_device(): their_rows = lax.ppermute(wanted, HEAD, [(i, i ^ 1) for i in range(split)])  3.36 us
  transfers between devices with their start and end apart: 3, of which 2 were waited for; matrix products, arithmetic and copies ran while one was open for 0% of the time, Pallas kernels for 1%

profile of v9, /device:TPU:1, one launch (start us, length us, event | category | flops | bytes accessed | tf_op | source)
XLA Modules:
  0.0 79.0 jit_solution(18417555219384424272)
XLA Ops:
  0.6 0.0 copy-start.3
  0.6 4.0 %attend.1 = (f32[4,8,1664]{2,1,0:T(8,128)}, f32[8,512]{1,0:T(8,128)}, bf16[208,1536]{1,0:T(8,128)(2,1)}) custom-call(s32[1,8]{1,0:T(1,128)} %lens_ref.3, bf16[512,384]{1,0:T(8,128)(2,1)} %q_ref.1, bf16[512,256]{1,0:T(8,128)(2,1)} %k_ref.1, bf16[512,256]{1,0:T(8,128)(2,1)} %v_ref.1, bf16[384,1536]{1,0:T(8,128)(2,1)} %my_rows_ref.1, bf16[4,384]{1,0:T(4,128)(2,1)} %queries_ref.1), custom_call_target="tpu_custom_call" | custom-call | tf_op jit(solution)/shard_map/attend/pallas_call | solution.py:325
  4.6 5.4 %all-to-all-start = ((f32[4,8,1664]{2,1,0:T(8,128)}), f32[4,8,1664]{2,1,0:T(8,128)S(1)}, u32[]{:S(2)}, u32[]{:S(2)}) async-start(f32[4,8,1664]{2,1,0:T(8,128)} %get-tuple-element.17), calls=%async_computation | async-start | bytes 425984 | tf_op jit(solution)/shard_map/all_to_all | solution.py:338
  10.1 3.4 %collective-permute-start = (bf16[208,1536]{1,0:T(8,128)(2,1)}, bf16[208,1536]{1,0:T(8,128)(2,1)S(1)}, u32[]{:S(2)}, u32[]{:S(2)}) collective-permute-start(bf16[208,1536]{1,0:T(8,128)(2,1)} %get-tuple-element.19), channel_id=1, source_target_pairs={{0,1},{1,0},{2,3},{3,2},{4,5},{5,4},{6,7},{7,6},{8,9},{9,8},{10,11... | collective-permute-start | bytes 1916936 | tf_op jit(solution)/shard_map/ppermute | solution.py:339
  13.4 1.9 %all-to-all-done.got_ref = f32[4,8,1664]{2,1,0:T(8,128)S(1)} async-done(((f32[4,8,1664]{2,1,0:T(8,128)}), f32[4,8,1664]{2,1,0:T(8,128)S(1)}, u32[]{:S(2)}, u32[]{:S(2)}) %all-to-all-start) | async-done | bytes 213024 | tf_op jit(solution)/shard_map/all_to_all | solution.py:338
  15.4 0.7 copies.1
  16.1 16.3 %all-to-all-start.1 = ((bf16[64,2,768]{2,1,0:T(2,128)(2,1)}), bf16[64,2,768]{2,1,0:T(2,128)(2,1)S(1)}, u32[]{:S(2)}, u32[]{:S(2)}) async-start(bf16[64,2,768]{2,1,0:T(2,128)(2,1)} %get-tuple-element.22), calls=%async_computation.1 | async-start | bytes 393216 | tf_op jit(solution)/shard_map/all_to_all | solution.py:351
  32.3 0.0 copy-done.3
  32.3 0.0 copy-start
  32.4 0.0 copy-start.1
  32.4 0.0 copy-start.2
  32.4 0.1 reshape.14.pos_ref
  32.5 0.0 collective-permute-done.their_rows_ref
  32.5 4.6 %all-gather = f32[16,1536]{1,0:T(8,128)S(1)} all-gather(f32[8,1536]{1,0:T(8,128)S(1)} %get-tuple-element.20), channel_id=2, replica_groups=mesh['dp_0'=4,'dp_1'=8,'dp_2'=2,'dp_3'=2,'head_0'=2,'head_1'=2] {'dp_3'}, dimensions={0}, use_global_device_ids=true | all-gather | bytes 147456 | tf_op jit(solution)/shard_map/all_gather | solution.py:357
  37.1 0.1 unit.1
  37.2 6.0 %all-gather.1 = bf16[32,1536]{1,0:T(8,128)(2,1)S(1)} all-gather(bf16[16,1536]{1,0:T(8,128)(2,1)S(1)} %get-tuple-element.21), channel_id=3, replica_groups={{0,10},{1,11},{2,8},{3,9},{4,14},{5,15},{6,12},{7,13},{16,26},{17,27},{..., dimensions={0}, use_global_device_ids=true | all-gather | bytes 147456 | tf_op jit(solution)/shard_map/all_gather | solution.py:370
  43.3 2.5 %all-to-all-done.1 = bf16[64,2,768]{2,1,0:T(2,128)(2,1)S(1)} async-done(((bf16[64,2,768]{2,1,0:T(2,128)(2,1)}), bf16[64,2,768]{2,1,0:T(2,128)(2,1)S(1)}, u32[]{:S(2)}, u32[]{:S(2)}) %all-to-all-start.1) | async-done | bytes 196640 | tf_op jit(solution)/shard_map/all_to_all | solution.py:351
  45.8 0.1 reshape.13.q_ref
  45.9 0.3 logits.1
  46.2 16.4 %all_to_all.20.stats_ref = f32[32,2,128]{2,1,0:T(2,128)S(1)} all-to-all(f32[32,2,128]{2,1,0:T(2,128)S(1)} %get-tuple-element.23), channel_id=1, replica_groups=mesh['dp_0'=4,'dp_1'=8,'dp_2'=2,'dp_3'=2,'head_0'=2,'head_1'=2] {'dp_0',..., dimensions={0} | all-to-all | bytes 65536 | tf_op jit(solution)/shard_map/all_to_all | solution.py:384
  62.5 0.3 slopes.1
  62.9 14.2 %all_to_all.21.grads_ref = bf16[8,8,1664]{2,1,0:T(8,128)(2,1)S(1)} all-to-all(bf16[8,8,1664]{2,1,0:T(8,128)(2,1)S(1)} %slopes.1), channel_id=1, replica_groups=mesh['dp_0'=4,'dp_1'=8,'dp_2'=2,'dp_3'=2,'head_0'=2,'head_1'=2] {'dp_3',..., dimensions={0} | all-to-all | bytes 425984 | tf_op jit(solution)/shard_map/all_to_all | solution.py:394
  77.1 0.0 copy-done.1
  77.1 1.8 %slopes_of_values.1 = (bf16[64,512]{1,0:T(8,128)(2,1)}, f32[1,1]{1,0:T(1,128)}) custom-call(s32[1,8]{1,0:T(1,128)S(1)} %copy-done.2, bf16[8,8,1664]{2,1,0:T(8,128)(2,1)S(1)} %all_to_all.21.grads_ref, bf16[384,1536]{1,0:T(8,128)(2,1)S(1)} %copy-done, bf16[208,1536]{1,0:T(8,128)(2,1)S(1)} %collective-permute-done.their_rows_ref, f32[8,512]{1,0:T(8,128)S(1)} %copy-done.1), custom_call_target="tpu_custom_call" | custom-call | tf_op jit(solution)/shard_map/slopes_of_values/pallas_call | solution.py:396
  (2 shorter events, 0.0 us)
Async XLA Ops:
  0.6 31.7 %copy-start.3 = (s32[512]{0:T(512)S(1)}, s32[512]{0:T(512)}, u32[]{:S(2)}) copy-start(s32[512]{0:T(512)} %param.13) | copy-start | bytes 6148
  4.6 10.7 %all-to-all-start = ((f32[4,8,1664]{2,1,0:T(8,128)}), f32[4,8,1664]{2,1,0:T(8,128)S(1)}, u32[]{:S(2)}, u32[]{:S(2)}) async-start(f32[4,8,1664]{2,1,0:T(8,128)} %get-tuple-element.17), calls=%async_computation | async-start | bytes 425984 | tf_op jit(solution)/shard_map/all_to_all | solution.py:338
  10.1 22.4 %collective-permute-start = (bf16[208,1536]{1,0:T(8,128)(2,1)}, bf16[208,1536]{1,0:T(8,128)(2,1)S(1)}, u32[]{:S(2)}, u32[]{:S(2)}) collective-permute-start(bf16[208,1536]{1,0:T(8,128)(2,1)} %get-tuple-element.19), channel_id=1, source_target_pairs={{0,1},{1,0},{2,3},{3,2},{4,5},{5,4},{6,7},{7,6},{8,9},{9,8},{10,11... | collective-permute-start | bytes 1916936 | tf_op jit(solution)/shard_map/ppermute | solution.py:339
  16.1 29.7 %all-to-all-start.1 = ((bf16[64,2,768]{2,1,0:T(2,128)(2,1)}), bf16[64,2,768]{2,1,0:T(2,128)(2,1)S(1)}, u32[]{:S(2)}, u32[]{:S(2)}) async-start(bf16[64,2,768]{2,1,0:T(2,128)(2,1)} %get-tuple-element.22), calls=%async_computation.1 | async-start | bytes 393216 | tf_op jit(solution)/shard_map/all_to_all | solution.py:351
  32.3 44.8 %copy-start = (bf16[384,1536]{1,0:T(8,128)(2,1)S(1)}, bf16[384,1536]{1,0:T(8,128)(2,1)}, u32[]{:S(2)}) copy-start(bf16[384,1536]{1,0:T(8,128)(2,1)} %my_rows_ref.1) | copy-start | bytes 3538948
  32.4 44.8 %copy-start.1 = (f32[8,512]{1,0:T(8,128)S(1)}, f32[8,512]{1,0:T(8,128)}, u32[]{:S(2)}) copy-start(f32[8,512]{1,0:T(8,128)} %get-tuple-element.29.sums_ref) | copy-start | bytes 49156
  32.4 44.8 %copy-start.2 = (s32[1,8]{1,0:T(1,128)S(1)}, s32[1,8]{1,0:T(1,128)}, u32[]{:S(2)}) copy-start(s32[1,8]{1,0:T(1,128)} %lens_ref.3) | copy-start | bytes 100
